TPU v7x, 32 devices: a whole 2x2x4 slice. The times are simulated.
32 devices in a mesh: tm: 2 (over core), gx: 4 (over y, x), gy: 4 (over z).
Axes of the slice: x: 2, y: 2, z: 4, core: 2. Of those that a mesh axis runs over, the one named last changes fastest.
Arguments:
- start_states: float32 [2, 128, 64, 256], P('tm', 'gx', 'gy'), may hold values from 0.5 to 2
- wind_code: int32 [4, 4], P('gx', 'gy'), may hold values from 0 to 7
- wind_profile: float32 [2, 256], replicated, may hold values from 0.05 to 0.4
- vertical_mix: float32 [128, 64, 256], P('gx', 'gy'), may hold values from 0.01 to 0.1
Outputs:
- middle_states: float32 [2, 128, 64, 256], P('tm', 'gx', 'gy')
- final_states: float32 [2, 128, 64, 256], P('tm', 'gx', 'gy')
Inputs may be any that keep to these rules, and one draw needn't show every extreme that they name: `wind_code`: a regime code.
All inputs are finite; a program needn't handle non-finite values.
Results may differ from a plain program's by a relative error of at most 0.00002.
Values sent between devices are 32-bit elements; how exact they have to be, the bound alone decides.
No kernel may reach another device: no remote copies, remote signals or barrier semaphores. Data moves between devices by JAX's collectives and lax.ppermute only.
A program may use at most 64 MiB of HBM per device.

v0:
```python
import jax
import jax.numpy as jnp
from jax import lax
from jax.sharding import PartitionSpec as P

SWEEPS = 3


time_step = 0.5
half_step = 0.25
diffusion_low = 0.04
diffusion_high = 0.1
first_weights = (5.0 / 24.0, 1.0 / 3.0, -1.0 / 24.0)
second_weights = (-1.0 / 24.0, 1.0 / 3.0, 5.0 / 24.0)


def padded_2(x, sides, width):
    for axis, dim in sides:
        devices, length = (lax.axis_size(axis), x.shape[dim])
        up = [(i, (i + 1) % devices) for i in range(devices - 1)]
        down = [(j, i) for i, j in up]
        last = lax.slice_in_dim(x, length - width, length, axis=dim)
        initial = lax.slice_in_dim(x, 0, width, axis=dim)
        before = lax.ppermute(last, axis, up)
        after = lax.ppermute(initial, axis, down)
        x = jnp.concatenate([before, x, after], axis=dim)
    return x


def shifted(x, axis, by):
    devices = lax.axis_size(axis)
    pairs = [(i, i + by) for i in range(devices) if 0 <= i + by < devices]
    return lax.ppermute(x, axis, pairs)


def tendency(padded, sign_x, sign_y, strength, wind_profile, vertical_mix):
    row_count = padded.shape[0] - 4
    columns = padded.shape[1] - 4

    def neighbour(source, step_x, step_y):
        return source[2 + step_x : 2 + step_x + row_count, 2 + step_y : 2 + step_y + columns]

    centre = neighbour(padded, 0, 0)
    squared = padded * padded
    growth = squared / (1.0 + squared)
    growth_centre = neighbour(growth, 0, 0)
    spread = jnp.zeros_like(centre)
    for step_x, step_y in ((1, 0), (-1, 0), (0, 1), (0, -1)):
        weight = 0.5 + 0.5 * (growth_centre + neighbour(growth, step_x, step_y))
        spread = spread + weight * (neighbour(padded, step_x, step_y) - centre)
    upwind_x = jnp.where(sign_x > 0, neighbour(padded, -1, 0), neighbour(padded, 1, 0))
    farther_x = jnp.where(sign_x > 0, neighbour(padded, -2, 0), neighbour(padded, 2, 0))
    upwind_y = jnp.where(sign_y > 0, neighbour(padded, 0, -1), neighbour(padded, 0, 1))
    farther_y = jnp.where(sign_y > 0, neighbour(padded, 0, -2), neighbour(padded, 0, 2))
    carried = wind_profile[0] * (3.0 * centre - 4.0 * upwind_x + farther_x)
    carried = carried + wind_profile[1] * (3.0 * centre - 4.0 * upwind_y + farther_y)
    below_cells = jnp.concatenate([centre[:, :, :1], centre[:, :, :-1]], axis=2)
    above_cells = jnp.concatenate([centre[:, :, 1:], centre[:, :, -1:]], axis=2)
    return (
        strength * spread
        - 0.5 * carried
        + vertical_mix * (below_cells + above_cells - 2.0 * centre)
    )


def sweep_once(first_state, first_rate, slopes, tendency_of):
    middle = (
        first_state
        + half_step * (first_rate - slopes[0])
        + time_step
        * (
            first_weights[0] * slopes[0]
            + first_weights[1] * slopes[1]
            + first_weights[2] * slopes[2]
        )
    )
    middle_rate = tendency_of(middle)
    final_state = (
        middle
        + half_step * (middle_rate - slopes[1])
        + time_step
        * (
            second_weights[0] * slopes[0]
            + second_weights[1] * slopes[1]
            + second_weights[2] * slopes[2]
        )
    )
    final_rate = tendency_of(final_state)
    return ((first_state, middle, final_state), (first_rate, middle_rate, final_rate))


def shards(start_states, wind_code, wind_profile, vertical_mix):
    initial_state = start_states[0]
    regime = wind_code[0, 0]
    sign_x = 1.0 - 2.0 * (regime % 2).astype(jnp.float32)
    sign_y = 1.0 - 2.0 * (regime // 2 % 2).astype(jnp.float32)
    strength = jnp.where(regime // 4 == 1, diffusion_high, diffusion_low)

    def tendency_of(state_field):
        padded = padded_2(state_field, (("gx", 0), ("gy", 1)), 2)
        return tendency(padded, sign_x, sign_y, strength, wind_profile, vertical_mix)

    first_slice = lax.axis_index("tm") == 0
    initial_rate = tendency_of(initial_state)
    states = (initial_state, initial_state, initial_state)
    slopes = (initial_rate, initial_rate, initial_rate)
    for sweep_index in range(SWEEPS):
        arrived, arrived_rate = shifted((states[2], slopes[2]), "tm", 1)
        first_state = jnp.where(first_slice, initial_state, arrived)
        first_rate = jnp.where(first_slice, initial_rate, arrived_rate)
        first_state, first_rate = (first_state, first_rate)
        states, slopes = sweep_once(first_state, first_rate, slopes, tendency_of)
    return (states[1][None], states[2][None])


def solution(mesh):
    in_specs = (P("tm", "gx", "gy", None), P("gx", "gy"), P(), P("gx", "gy", None))
    out_specs = (P("tm", "gx", "gy", None), P("tm", "gx", "gy", None))
    return jax.shard_map(shards, mesh=mesh, in_specs=in_specs, out_specs=out_specs, check_vma=False)
```

profile of v0, /device:TPU:0, one launch (start us, length us, event | category | flops | bytes accessed | tf_op | source)
XLA Modules:
  0.0 137.9 jit_solution(18142025536464073586)
XLA Ops:
  1.4 4.8 %collective-permute-start.1 = (f32[2,16,256]{2,1,0:T(8,128)S(1)}, f32[2,16,256]{2,1,0:T(8,128)S(1)}, u32[]{:S(2)}, u32[]{:S(2)}) collective-permute-start(f32[2,16,256]{2,1,0:T(8,128)S(1)} %get-tuple-element.64), channel_id=1, source_target_pairs={{0,4},{4,8},{8,12},{1,5},{5,9},{9,13},{2,6},{6,10},{10,14},{3,7},{... | collective-permute-start | bytes 98312 | tf_op jit(solution)/shard_map/ppermute | solution.py:24
  7.6 1.6 %collective-permute-start = (f32[32,16,256]{2,1,0:T(8,128)}, f32[32,16,256]{2,1,0:T(8,128)S(1)}, u32[]{:S(2)}, u32[]{:S(2)}) collective-permute-start(f32[32,16,256]{2,1,0:T(8,128)} %bitcast.19), channel_id=1, source_target_pairs={{0,16},{1,17},{2,18},{3,19},{4,20},{5,21},{6,22},{7,23},{8,24},{9,... | collective-permute-start | bytes 1572872 | tf_op jit(solution)/shard_map/ppermute | solution.py:33
  9.2 1.5 %fusion.196 = (f32[32,16,255]{2,1,0:T(8,128)S(1)}, f32[32,16,255]{2,1,0:T(8,128)S(1)}) fusion(f32[32,16,256]{2,1,0:T(8,128)} %bitcast.20), kind=kLoop, calls=%fused_computation.318 | loop fusion | bytes 2088960 | tf_op jit(solution)/shard_map/slice | solution.py:58
  12.1 3.5 %collective-permute-start.3 = (f32[36,2,256]{2,1,0:T(2,128)S(1)}, f32[36,2,256]{2,1,0:T(2,128)S(1)}, u32[]{:S(2)}, u32[]{:S(2)}) collective-permute-start(f32[36,2,256]{2,1,0:T(2,128)S(1)} %get-tuple-element.28), channel_id=1, source_target_pairs={{0,1},{1,2},{2,3},{4,5},{5,6},{6,7},{8,9},{9,10},{10,11},{12,13},{... | collective-permute-start | bytes 221192 | tf_op jit(solution)/shard_map/ppermute | solution.py:24
  17.7 4.2 %collective-permute-done.4 = f32[36,2,256]{2,1,0:T(2,128)S(1)} collective-permute-done((f32[36,2,256]{2,1,0:T(2,128)S(1)}, f32[36,2,256]{2,1,0:T(2,128)S(1)}, u32[]{:S(2)}, u32[]{:S(2)}) %collective-permute-start.4) | collective-permute-done | bytes 73760 | tf_op jit(solution)/shard_map/ppermute | solution.py:25
  24.3 1.3 collective-permute-start.5
  25.6 1.5 %collective-permute-done.5 = f32[32,16,256]{2,1,0:T(8,128)S(1)} collective-permute-done((f32[32,16,256]{2,1,0:T(8,128)S(1)}, f32[32,16,256]{2,1,0:T(8,128)S(1)}, u32[]{:S(2)}, u32[]{:S(2)}) %collective-permute-start.5) | collective-permute-done | bytes 524320 | tf_op jit(solution)/shard_map/ppermute | solution.py:33
  27.3 4.3 %collective-permute-start.6 = (f32[2,16,256]{2,1,0:T(8,128)S(1)}, f32[2,16,256]{2,1,0:T(8,128)S(1)}, u32[]{:S(2)}, u32[]{:S(2)}) collective-permute-start(f32[2,16,256]{2,1,0:T(8,128)S(1)} %get-tuple-element.54), channel_id=1, source_target_pairs={{0,4},{4,8},{8,12},{1,5},{5,9},{9,13},{2,6},{6,10},{10,14},{3,7},{... | collective-permute-start | bytes 98312 | tf_op jit(solution)/shard_map/ppermute | solution.py:24
  33.2 4.2 %collective-permute-done.7 = f32[2,16,256]{2,1,0:T(8,128)S(1)} collective-permute-done((f32[2,16,256]{2,1,0:T(8,128)S(1)}, f32[2,16,256]{2,1,0:T(8,128)S(1)}, u32[]{:S(2)}, u32[]{:S(2)}) %collective-permute-start.7) | collective-permute-done | bytes 32800 | tf_op jit(solution)/shard_map/ppermute | solution.py:25
  37.5 3.5 %collective-permute-start.8 = (f32[36,2,256]{2,1,0:T(2,128)S(1)}, f32[36,2,256]{2,1,0:T(2,128)S(1)}, u32[]{:S(2)}, u32[]{:S(2)}) collective-permute-start(f32[36,2,256]{2,1,0:T(2,128)S(1)} %get-tuple-element.24), channel_id=1, source_target_pairs={{0,1},{1,2},{2,3},{4,5},{5,6},{6,7},{8,9},{9,10},{10,11},{12,13},{... | collective-permute-start | bytes 221192 | tf_op jit(solution)/shard_map/ppermute | solution.py:24
  43.0 4.3 %collective-permute-done.9 = f32[36,2,256]{2,1,0:T(2,128)S(1)} collective-permute-done((f32[36,2,256]{2,1,0:T(2,128)S(1)}, f32[36,2,256]{2,1,0:T(2,128)S(1)}, u32[]{:S(2)}, u32[]{:S(2)}) %collective-permute-start.9) | collective-permute-done | bytes 73760 | tf_op jit(solution)/shard_map/ppermute | solution.py:25
  47.7 1.9 %multiply_add_fusion.3 = (f32[32,16,256]{2,1,0:T(8,128)S(1)}, f32[32,16,256]{2,1,0:T(8,128)S(1)}) fusion(f32[32,16,256]{2,1,0:T(8,128)S(1)} %fusion.147, f32[32,16,256]{2,1,0:T(8,128)S(1)} %collective-permute-done.5, f32[32,16,256]{2,1,0:T(8,128)S(1)} %collective-permute-done, pred[]{:T(512)S(6)} %eq.9, f32[1,32,16,256]{3,2,1,0:T(8,128)S(1)} %copy-done, ...), kind=kLoop, calls=%fused_computation.278 | loop fusion | flops 9175040 | bytes 10029063 | tf_op jit(solution)/shard_map/add | solution.py:79
  51.0 4.7 %collective-permute-start.11 = (f32[2,16,256]{2,1,0:T(8,128)S(1)}, f32[2,16,256]{2,1,0:T(8,128)S(1)}, u32[]{:S(2)}, u32[]{:S(2)}) collective-permute-start(f32[2,16,256]{2,1,0:T(8,128)S(1)} %get-tuple-element.52), channel_id=1, source_target_pairs={{0,4},{4,8},{8,12},{1,5},{5,9},{9,13},{2,6},{6,10},{10,14},{3,7},{... | collective-permute-start | bytes 98312 | tf_op jit(solution)/shard_map/ppermute | solution.py:24
  57.3 4.2 %collective-permute-done.12 = f32[2,16,256]{2,1,0:T(8,128)S(1)} collective-permute-done((f32[2,16,256]{2,1,0:T(8,128)S(1)}, f32[2,16,256]{2,1,0:T(8,128)S(1)}, u32[]{:S(2)}, u32[]{:S(2)}) %collective-permute-start.12) | collective-permute-done | bytes 32800 | tf_op jit(solution)/shard_map/ppermute | solution.py:25
  61.6 3.5 %collective-permute-start.13 = (f32[36,2,256]{2,1,0:T(2,128)S(1)}, f32[36,2,256]{2,1,0:T(2,128)S(1)}, u32[]{:S(2)}, u32[]{:S(2)}) collective-permute-start(f32[36,2,256]{2,1,0:T(2,128)S(1)} %get-tuple-element.20), channel_id=1, source_target_pairs={{0,1},{1,2},{2,3},{4,5},{5,6},{6,7},{8,9},{9,10},{10,11},{12,13},{... | collective-permute-start | bytes 221192 | tf_op jit(solution)/shard_map/ppermute | solution.py:24
  67.0 4.3 %collective-permute-done.14 = f32[36,2,256]{2,1,0:T(2,128)S(1)} collective-permute-done((f32[36,2,256]{2,1,0:T(2,128)S(1)}, f32[36,2,256]{2,1,0:T(2,128)S(1)}, u32[]{:S(2)}, u32[]{:S(2)}) %collective-permute-start.14) | collective-permute-done | bytes 73760 | tf_op jit(solution)/shard_map/ppermute | solution.py:25
  74.1 1.5 %collective-permute-done.15 = f32[32,16,256]{2,1,0:T(8,128)S(1)} collective-permute-done((f32[32,16,256]{2,1,0:T(8,128)S(1)}, f32[32,16,256]{2,1,0:T(8,128)S(1)}, u32[]{:S(2)}, u32[]{:S(2)}) %collective-permute-start.15) | collective-permute-done | bytes 524320 | tf_op jit(solution)/shard_map/ppermute | solution.py:33
  76.0 2.8 %collective-permute-start.16 = (f32[2,16,256]{2,1,0:T(8,128)S(1)}, f32[2,16,256]{2,1,0:T(8,128)S(1)}, u32[]{:S(2)}, u32[]{:S(2)}) collective-permute-start(f32[2,16,256]{2,1,0:T(8,128)S(1)} %get-tuple-element.42), channel_id=1, source_target_pairs={{0,4},{4,8},{8,12},{1,5},{5,9},{9,13},{2,6},{6,10},{10,14},{3,7},{... | collective-permute-start | bytes 98312 | tf_op jit(solution)/shard_map/ppermute | solution.py:24
  80.4 4.2 %collective-permute-done.17 = f32[2,16,256]{2,1,0:T(8,128)S(1)} collective-permute-done((f32[2,16,256]{2,1,0:T(8,128)S(1)}, f32[2,16,256]{2,1,0:T(8,128)S(1)}, u32[]{:S(2)}, u32[]{:S(2)}) %collective-permute-start.17) | collective-permute-done | bytes 32800 | tf_op jit(solution)/shard_map/ppermute | solution.py:25
  84.7 1.9 %collective-permute-start.18 = (f32[36,2,256]{2,1,0:T(2,128)S(1)}, f32[36,2,256]{2,1,0:T(2,128)S(1)}, u32[]{:S(2)}, u32[]{:S(2)}) collective-permute-start(f32[36,2,256]{2,1,0:T(2,128)S(1)} %get-tuple-element.16), channel_id=1, source_target_pairs={{0,1},{1,2},{2,3},{4,5},{5,6},{6,7},{8,9},{9,10},{10,11},{12,13},{... | collective-permute-start | bytes 221192 | tf_op jit(solution)/shard_map/ppermute | solution.py:24
  88.6 4.3 %collective-permute-done.19 = f32[36,2,256]{2,1,0:T(2,128)S(1)} collective-permute-done((f32[36,2,256]{2,1,0:T(2,128)S(1)}, f32[36,2,256]{2,1,0:T(2,128)S(1)}, u32[]{:S(2)}, u32[]{:S(2)}) %collective-permute-start.19) | collective-permute-done | bytes 73760 | tf_op jit(solution)/shard_map/ppermute | solution.py:25
  93.3 1.9 %multiply_add_fusion.1 = (f32[32,16,256]{2,1,0:T(8,128)S(1)}, f32[32,16,256]{2,1,0:T(8,128)S(1)}) fusion(f32[32,16,256]{2,1,0:T(8,128)S(1)} %fusion.97, f32[32,16,256]{2,1,0:T(8,128)S(1)} %multiply_add_fusion.2, f32[32,16,256]{2,1,0:T(8,128)S(1)} %get-tuple-element.5, f32[32,16,256]{2,1,0:T(8,128)S(1)} %fusion.147, ...), kind=kLoop, calls=%fused_computation.276 | loop fusion | flops 8126464 | bytes 10029063 | tf_op jit(solution)/shard_map/add | solution.py:79
  96.5 2.8 %collective-permute-start.21 = (f32[2,16,256]{2,1,0:T(8,128)S(1)}, f32[2,16,256]{2,1,0:T(8,128)S(1)}, u32[]{:S(2)}, u32[]{:S(2)}) collective-permute-start(f32[2,16,256]{2,1,0:T(8,128)S(1)} %get-tuple-element.40), channel_id=1, source_target_pairs={{0,4},{4,8},{8,12},{1,5},{5,9},{9,13},{2,6},{6,10},{10,14},{3,7},{... | collective-permute-start | bytes 98312 | tf_op jit(solution)/shard_map/ppermute | solution.py:24
  100.9 4.2 %collective-permute-done.22 = f32[2,16,256]{2,1,0:T(8,128)S(1)} collective-permute-done((f32[2,16,256]{2,1,0:T(8,128)S(1)}, f32[2,16,256]{2,1,0:T(8,128)S(1)}, u32[]{:S(2)}, u32[]{:S(2)}) %collective-permute-start.22) | collective-permute-done | bytes 32800 | tf_op jit(solution)/shard_map/ppermute | solution.py:25
  105.2 1.9 %collective-permute-start.23 = (f32[36,2,256]{2,1,0:T(2,128)S(1)}, f32[36,2,256]{2,1,0:T(2,128)S(1)}, u32[]{:S(2)}, u32[]{:S(2)}) collective-permute-start(f32[36,2,256]{2,1,0:T(2,128)S(1)} %get-tuple-element.12), channel_id=1, source_target_pairs={{0,1},{1,2},{2,3},{4,5},{5,6},{6,7},{8,9},{9,10},{10,11},{12,13},{... | collective-permute-start | bytes 221192 | tf_op jit(solution)/shard_map/ppermute | solution.py:24
  109.1 4.3 %collective-permute-done.24 = f32[36,2,256]{2,1,0:T(2,128)S(1)} collective-permute-done((f32[36,2,256]{2,1,0:T(2,128)S(1)}, f32[36,2,256]{2,1,0:T(2,128)S(1)}, u32[]{:S(2)}, u32[]{:S(2)}) %collective-permute-start.24) | collective-permute-done | bytes 73760 | tf_op jit(solution)/shard_map/ppermute | solution.py:25
  116.1 1.5 %collective-permute-done.25 = f32[32,16,256]{2,1,0:T(8,128)S(1)} collective-permute-done((f32[32,16,256]{2,1,0:T(8,128)S(1)}, f32[32,16,256]{2,1,0:T(8,128)S(1)}, u32[]{:S(2)}, u32[]{:S(2)}) %collective-permute-start.25) | collective-permute-done | bytes 524320 | tf_op jit(solution)/shard_map/ppermute | solution.py:33
  118.1 2.8 %collective-permute-start.26 = (f32[2,16,256]{2,1,0:T(8,128)S(1)}, f32[2,16,256]{2,1,0:T(8,128)S(1)}, u32[]{:S(2)}, u32[]{:S(2)}) collective-permute-start(f32[2,16,256]{2,1,0:T(8,128)S(1)} %get-tuple-element.34), channel_id=1, source_target_pairs={{0,4},{4,8},{8,12},{1,5},{5,9},{9,13},{2,6},{6,10},{10,14},{3,7},{... | collective-permute-start | bytes 98312 | tf_op jit(solution)/shard_map/ppermute | solution.py:24
  122.5 4.2 %collective-permute-done.27 = f32[2,16,256]{2,1,0:T(8,128)S(1)} collective-permute-done((f32[2,16,256]{2,1,0:T(8,128)S(1)}, f32[2,16,256]{2,1,0:T(8,128)S(1)}, u32[]{:S(2)}, u32[]{:S(2)}) %collective-permute-start.27) | collective-permute-done | bytes 32800 | tf_op jit(solution)/shard_map/ppermute | solution.py:25
  126.8 1.9 %collective-permute-start.28 = (f32[36,2,256]{2,1,0:T(2,128)S(1)}, f32[36,2,256]{2,1,0:T(2,128)S(1)}, u32[]{:S(2)}, u32[]{:S(2)}) collective-permute-start(f32[36,2,256]{2,1,0:T(2,128)S(1)} %get-tuple-element.8), channel_id=1, source_target_pairs={{0,1},{1,2},{2,3},{4,5},{5,6},{6,7},{8,9},{9,10},{10,11},{12,13},{... | collective-permute-start | bytes 221192 | tf_op jit(solution)/shard_map/ppermute | solution.py:24
  130.7 4.3 %collective-permute-done.29 = f32[36,2,256]{2,1,0:T(2,128)S(1)} collective-permute-done((f32[36,2,256]{2,1,0:T(2,128)S(1)}, f32[36,2,256]{2,1,0:T(2,128)S(1)}, u32[]{:S(2)}, u32[]{:S(2)}) %collective-permute-start.29) | collective-permute-done | bytes 73760 | tf_op jit(solution)/shard_map/ppermute | solution.py:25
  135.4 2.6 %fusion.22 = f32[1,32,16,256]{3,2,1,0:T(8,128)} fusion(f32[32,16,256]{2,1,0:T(8,128)S(1)} %multiply_add_fusion, f32[32,16,256]{2,1,0:T(8,128)S(1)} %get-tuple-element.3, f32[36,18,256]{2,1,0:T(8,128)S(1)} %get-tuple-element.7, f32[36,18,256]{2,1,0:T(8,128)S(1)} %get-tuple-element.6, f32[2,16,256]{2,1,0:T(8,128)S(1)} %collective-permute-done.27, ...), kind=kLoop, calls=%fused_computation.71 | loop fusion | flops 8126464 | bytes 9504775 | tf_op jit(solution)/shard_map/broadcast_in_dim | solution.py:113
  (84 shorter events, 35.4 us)
Async XLA Ops:
  1.4 10.1 %collective-permute-start.1 = (f32[2,16,256]{2,1,0:T(8,128)S(1)}, f32[2,16,256]{2,1,0:T(8,128)S(1)}, u32[]{:S(2)}, u32[]{:S(2)}) collective-permute-start(f32[2,16,256]{2,1,0:T(8,128)S(1)} %get-tuple-element.64), channel_id=1, source_target_pairs={{0,4},{4,8},{8,12},{1,5},{5,9},{9,13},{2,6},{6,10},{10,14},{3,7},{... | collective-permute-start | bytes 98312 | tf_op jit(solution)/shard_map/ppermute | solution.py:24
  6.3 5.8 %collective-permute-start.2 = (f32[2,16,256]{2,1,0:T(8,128)S(1)}, f32[2,16,256]{2,1,0:T(8,128)S(1)}, u32[]{:S(2)}, u32[]{:S(2)}) collective-permute-start(f32[2,16,256]{2,1,0:T(8,128)S(1)} %get-tuple-element.65), channel_id=1, source_target_pairs={{4,0},{8,4},{12,8},{5,1},{9,5},{13,9},{6,2},{10,6},{14,10},{7,3},{... | collective-permute-start | bytes 98312 | tf_op jit(solution)/shard_map/ppermute | solution.py:25
  7.6 18.0 %collective-permute-start = (f32[32,16,256]{2,1,0:T(8,128)}, f32[32,16,256]{2,1,0:T(8,128)S(1)}, u32[]{:S(2)}, u32[]{:S(2)}) collective-permute-start(f32[32,16,256]{2,1,0:T(8,128)} %bitcast.19), channel_id=1, source_target_pairs={{0,16},{1,17},{2,18},{3,19},{4,20},{5,21},{6,22},{7,23},{8,24},{9,... | collective-permute-start | bytes 1572872 | tf_op jit(solution)/shard_map/ppermute | solution.py:33
  12.1 4.8 %copy-start.4 = (f32[2,256]{1,0:T(2,128)S(1)}, f32[2,256]{1,0:T(2,128)}, u32[]{:S(2)}) copy-start(f32[2,256]{1,0:T(2,128)} %param.6) | copy-start | bytes 6148
  12.1 5.5 %collective-permute-start.3 = (f32[36,2,256]{2,1,0:T(2,128)S(1)}, f32[36,2,256]{2,1,0:T(2,128)S(1)}, u32[]{:S(2)}, u32[]{:S(2)}) collective-permute-start(f32[36,2,256]{2,1,0:T(2,128)S(1)} %get-tuple-element.28), channel_id=1, source_target_pairs={{0,1},{1,2},{2,3},{4,5},{5,6},{6,7},{8,9},{9,10},{10,11},{12,13},{... | collective-permute-start | bytes 221192 | tf_op jit(solution)/shard_map/ppermute | solution.py:24
  15.6 6.2 %collective-permute-start.4 = (f32[36,2,256]{2,1,0:T(2,128)S(1)}, f32[36,2,256]{2,1,0:T(2,128)S(1)}, u32[]{:S(2)}, u32[]{:S(2)}) collective-permute-start(f32[36,2,256]{2,1,0:T(2,128)S(1)} %get-tuple-element.29), channel_id=1, source_target_pairs={{1,0},{2,1},{3,2},{5,4},{6,5},{7,6},{9,8},{10,9},{11,10},{13,12},{... | collective-permute-start | bytes 221192 | tf_op jit(solution)/shard_map/ppermute | solution.py:25
  24.3 2.8 %collective-permute-start.5 = (f32[32,16,256]{2,1,0:T(8,128)S(1)}, f32[32,16,256]{2,1,0:T(8,128)S(1)}, u32[]{:S(2)}, u32[]{:S(2)}) collective-permute-start(f32[32,16,256]{2,1,0:T(8,128)S(1)} %fusion.147), channel_id=1, source_target_pairs={{0,16},{1,17},{2,18},{3,19},{4,20},{5,21},{6,22},{7,23},{8,24},{9,... | collective-permute-start | bytes 1572872 | tf_op jit(solution)/shard_map/ppermute | solution.py:33
  27.3 5.9 %collective-permute-start.6 = (f32[2,16,256]{2,1,0:T(8,128)S(1)}, f32[2,16,256]{2,1,0:T(8,128)S(1)}, u32[]{:S(2)}, u32[]{:S(2)}) collective-permute-start(f32[2,16,256]{2,1,0:T(8,128)S(1)} %get-tuple-element.54), channel_id=1, source_target_pairs={{0,4},{4,8},{8,12},{1,5},{5,9},{9,13},{2,6},{6,10},{10,14},{3,7},{... | collective-permute-start | bytes 98312 | tf_op jit(solution)/shard_map/ppermute | solution.py:24
  31.7 5.8 %collective-permute-start.7 = (f32[2,16,256]{2,1,0:T(8,128)S(1)}, f32[2,16,256]{2,1,0:T(8,128)S(1)}, u32[]{:S(2)}, u32[]{:S(2)}) collective-permute-start(f32[2,16,256]{2,1,0:T(8,128)S(1)} %get-tuple-element.55), channel_id=1, source_target_pairs={{4,0},{8,4},{12,8},{5,1},{9,5},{13,9},{6,2},{10,6},{14,10},{7,3},{... | collective-permute-start | bytes 98312 | tf_op jit(solution)/shard_map/ppermute | solution.py:25
  37.5 5.5 %collective-permute-start.8 = (f32[36,2,256]{2,1,0:T(2,128)S(1)}, f32[36,2,256]{2,1,0:T(2,128)S(1)}, u32[]{:S(2)}, u32[]{:S(2)}) collective-permute-start(f32[36,2,256]{2,1,0:T(2,128)S(1)} %get-tuple-element.24), channel_id=1, source_target_pairs={{0,1},{1,2},{2,3},{4,5},{5,6},{6,7},{8,9},{9,10},{10,11},{12,13},{... | collective-permute-start | bytes 221192 | tf_op jit(solution)/shard_map/ppermute | solution.py:24
  41.0 6.2 %collective-permute-start.9 = (f32[36,2,256]{2,1,0:T(2,128)S(1)}, f32[36,2,256]{2,1,0:T(2,128)S(1)}, u32[]{:S(2)}, u32[]{:S(2)}) collective-permute-start(f32[36,2,256]{2,1,0:T(2,128)S(1)} %get-tuple-element.25), channel_id=1, source_target_pairs={{1,0},{2,1},{3,2},{5,4},{6,5},{7,6},{9,8},{10,9},{11,10},{13,12},{... | collective-permute-start | bytes 221192 | tf_op jit(solution)/shard_map/ppermute | solution.py:25
  49.6 24.4 %collective-permute-start.10 = (f32[32,16,256]{2,1,0:T(8,128)S(1)}, f32[32,16,256]{2,1,0:T(8,128)S(1)}, u32[]{:S(2)}, u32[]{:S(2)}) collective-permute-start(f32[32,16,256]{2,1,0:T(8,128)S(1)} %get-tuple-element.4), channel_id=1, source_target_pairs={{0,16},{1,17},{2,18},{3,19},{4,20},{5,21},{6,22},{7,23},{8,24},{9,... | collective-permute-start | bytes 1572872 | tf_op jit(solution)/shard_map/ppermute | solution.py:33
  51.0 6.3 %collective-permute-start.11 = (f32[2,16,256]{2,1,0:T(8,128)S(1)}, f32[2,16,256]{2,1,0:T(8,128)S(1)}, u32[]{:S(2)}, u32[]{:S(2)}) collective-permute-start(f32[2,16,256]{2,1,0:T(8,128)S(1)} %get-tuple-element.52), channel_id=1, source_target_pairs={{0,4},{4,8},{8,12},{1,5},{5,9},{9,13},{2,6},{6,10},{10,14},{3,7},{... | collective-permute-start | bytes 98312 | tf_op jit(solution)/shard_map/ppermute | solution.py:24
  55.7 5.8 %collective-permute-start.12 = (f32[2,16,256]{2,1,0:T(8,128)S(1)}, f32[2,16,256]{2,1,0:T(8,128)S(1)}, u32[]{:S(2)}, u32[]{:S(2)}) collective-permute-start(f32[2,16,256]{2,1,0:T(8,128)S(1)} %get-tuple-element.53), channel_id=1, source_target_pairs={{4,0},{8,4},{12,8},{5,1},{9,5},{13,9},{6,2},{10,6},{14,10},{7,3},{... | collective-permute-start | bytes 98312 | tf_op jit(solution)/shard_map/ppermute | solution.py:25
  61.6 5.5 %collective-permute-start.13 = (f32[36,2,256]{2,1,0:T(2,128)S(1)}, f32[36,2,256]{2,1,0:T(2,128)S(1)}, u32[]{:S(2)}, u32[]{:S(2)}) collective-permute-start(f32[36,2,256]{2,1,0:T(2,128)S(1)} %get-tuple-element.20), channel_id=1, source_target_pairs={{0,1},{1,2},{2,3},{4,5},{5,6},{6,7},{8,9},{9,10},{10,11},{12,13},{... | collective-permute-start | bytes 221192 | tf_op jit(solution)/shard_map/ppermute | solution.py:24
  65.1 6.2 %collective-permute-start.14 = (f32[36,2,256]{2,1,0:T(2,128)S(1)}, f32[36,2,256]{2,1,0:T(2,128)S(1)}, u32[]{:S(2)}, u32[]{:S(2)}) collective-permute-start(f32[36,2,256]{2,1,0:T(2,128)S(1)} %get-tuple-element.21), channel_id=1, source_target_pairs={{1,0},{2,1},{3,2},{5,4},{6,5},{7,6},{9,8},{10,9},{11,10},{13,12},{... | collective-permute-start | bytes 221192 | tf_op jit(solution)/shard_map/ppermute | solution.py:25
  72.7 2.8 %collective-permute-start.15 = (f32[32,16,256]{2,1,0:T(8,128)S(1)}, f32[32,16,256]{2,1,0:T(8,128)S(1)}, u32[]{:S(2)}, u32[]{:S(2)}) collective-permute-start(f32[32,16,256]{2,1,0:T(8,128)S(1)} %fusion.97), channel_id=1, source_target_pairs={{0,16},{1,17},{2,18},{3,19},{4,20},{5,21},{6,22},{7,23},{8,24},{9,... | collective-permute-start | bytes 1572872 | tf_op jit(solution)/shard_map/ppermute | solution.py:33
  76.0 4.4 %collective-permute-start.16 = (f32[2,16,256]{2,1,0:T(8,128)S(1)}, f32[2,16,256]{2,1,0:T(8,128)S(1)}, u32[]{:S(2)}, u32[]{:S(2)}) collective-permute-start(f32[2,16,256]{2,1,0:T(8,128)S(1)} %get-tuple-element.42), channel_id=1, source_target_pairs={{0,4},{4,8},{8,12},{1,5},{5,9},{9,13},{2,6},{6,10},{10,14},{3,7},{... | collective-permute-start | bytes 98312 | tf_op jit(solution)/shard_map/ppermute | solution.py:24
  78.8 5.8 %collective-permute-start.17 = (f32[2,16,256]{2,1,0:T(8,128)S(1)}, f32[2,16,256]{2,1,0:T(8,128)S(1)}, u32[]{:S(2)}, u32[]{:S(2)}) collective-permute-start(f32[2,16,256]{2,1,0:T(8,128)S(1)} %get-tuple-element.43), channel_id=1, source_target_pairs={{4,0},{8,4},{12,8},{5,1},{9,5},{13,9},{6,2},{10,6},{14,10},{7,3},{... | collective-permute-start | bytes 98312 | tf_op jit(solution)/shard_map/ppermute | solution.py:25
  84.7 3.9 %collective-permute-start.18 = (f32[36,2,256]{2,1,0:T(2,128)S(1)}, f32[36,2,256]{2,1,0:T(2,128)S(1)}, u32[]{:S(2)}, u32[]{:S(2)}) collective-permute-start(f32[36,2,256]{2,1,0:T(2,128)S(1)} %get-tuple-element.16), channel_id=1, source_target_pairs={{0,1},{1,2},{2,3},{4,5},{5,6},{6,7},{8,9},{9,10},{10,11},{12,13},{... | collective-permute-start | bytes 221192 | tf_op jit(solution)/shard_map/ppermute | solution.py:24
  86.6 6.2 %collective-permute-start.19 = (f32[36,2,256]{2,1,0:T(2,128)S(1)}, f32[36,2,256]{2,1,0:T(2,128)S(1)}, u32[]{:S(2)}, u32[]{:S(2)}) collective-permute-start(f32[36,2,256]{2,1,0:T(2,128)S(1)} %get-tuple-element.17), channel_id=1, source_target_pairs={{1,0},{2,1},{3,2},{5,4},{6,5},{7,6},{9,8},{10,9},{11,10},{13,12},{... | collective-permute-start | bytes 221192 | tf_op jit(solution)/shard_map/ppermute | solution.py:25
  95.2 20.9 %collective-permute-start.20 = (f32[32,16,256]{2,1,0:T(8,128)S(1)}, f32[32,16,256]{2,1,0:T(8,128)S(1)}, u32[]{:S(2)}, u32[]{:S(2)}) collective-permute-start(f32[32,16,256]{2,1,0:T(8,128)S(1)} %get-tuple-element.2), channel_id=1, source_target_pairs={{0,16},{1,17},{2,18},{3,19},{4,20},{5,21},{6,22},{7,23},{8,24},{9,... | collective-permute-start | bytes 1572872 | tf_op jit(solution)/shard_map/ppermute | solution.py:33
  96.5 4.4 %collective-permute-start.21 = (f32[2,16,256]{2,1,0:T(8,128)S(1)}, f32[2,16,256]{2,1,0:T(8,128)S(1)}, u32[]{:S(2)}, u32[]{:S(2)}) collective-permute-start(f32[2,16,256]{2,1,0:T(8,128)S(1)} %get-tuple-element.40), channel_id=1, source_target_pairs={{0,4},{4,8},{8,12},{1,5},{5,9},{9,13},{2,6},{6,10},{10,14},{3,7},{... | collective-permute-start | bytes 98312 | tf_op jit(solution)/shard_map/ppermute | solution.py:24
  99.3 5.8 %collective-permute-start.22 = (f32[2,16,256]{2,1,0:T(8,128)S(1)}, f32[2,16,256]{2,1,0:T(8,128)S(1)}, u32[]{:S(2)}, u32[]{:S(2)}) collective-permute-start(f32[2,16,256]{2,1,0:T(8,128)S(1)} %get-tuple-element.41), channel_id=1, source_target_pairs={{4,0},{8,4},{12,8},{5,1},{9,5},{13,9},{6,2},{10,6},{14,10},{7,3},{... | collective-permute-start | bytes 98312 | tf_op jit(solution)/shard_map/ppermute | solution.py:25
  105.2 3.9 %collective-permute-start.23 = (f32[36,2,256]{2,1,0:T(2,128)S(1)}, f32[36,2,256]{2,1,0:T(2,128)S(1)}, u32[]{:S(2)}, u32[]{:S(2)}) collective-permute-start(f32[36,2,256]{2,1,0:T(2,128)S(1)} %get-tuple-element.12), channel_id=1, source_target_pairs={{0,1},{1,2},{2,3},{4,5},{5,6},{6,7},{8,9},{9,10},{10,11},{12,13},{... | collective-permute-start | bytes 221192 | tf_op jit(solution)/shard_map/ppermute | solution.py:24
  107.1 6.2 %collective-permute-start.24 = (f32[36,2,256]{2,1,0:T(2,128)S(1)}, f32[36,2,256]{2,1,0:T(2,128)S(1)}, u32[]{:S(2)}, u32[]{:S(2)}) collective-permute-start(f32[36,2,256]{2,1,0:T(2,128)S(1)} %get-tuple-element.13), channel_id=1, source_target_pairs={{1,0},{2,1},{3,2},{5,4},{6,5},{7,6},{9,8},{10,9},{11,10},{13,12},{... | collective-permute-start | bytes 221192 | tf_op jit(solution)/shard_map/ppermute | solution.py:25
  114.8 2.8 %collective-permute-start.25 = (f32[32,16,256]{2,1,0:T(8,128)S(1)}, f32[32,16,256]{2,1,0:T(8,128)S(1)}, u32[]{:S(2)}, u32[]{:S(2)}) collective-permute-start(f32[32,16,256]{2,1,0:T(8,128)S(1)} %fusion.47), channel_id=1, source_target_pairs={{0,16},{1,17},{2,18},{3,19},{4,20},{5,21},{6,22},{7,23},{8,24},{9,... | collective-permute-start | bytes 1572872 | tf_op jit(solution)/shard_map/ppermute | solution.py:33
  118.0 17.3 %copy-start.1 = (f32[32,16,256]{2,1,0:T(8,128)}, f32[32,16,256]{2,1,0:T(8,128)S(1)}, u32[]{:S(2)}) copy-start(f32[32,16,256]{2,1,0:T(8,128)S(1)} %multiply_add_fusion) | copy-start | bytes 1572868
  118.1 4.4 %collective-permute-start.26 = (f32[2,16,256]{2,1,0:T(8,128)S(1)}, f32[2,16,256]{2,1,0:T(8,128)S(1)}, u32[]{:S(2)}, u32[]{:S(2)}) collective-permute-start(f32[2,16,256]{2,1,0:T(8,128)S(1)} %get-tuple-element.34), channel_id=1, source_target_pairs={{0,4},{4,8},{8,12},{1,5},{5,9},{9,13},{2,6},{6,10},{10,14},{3,7},{... | collective-permute-start | bytes 98312 | tf_op jit(solution)/shard_map/ppermute | solution.py:24
  120.9 5.8 %collective-permute-start.27 = (f32[2,16,256]{2,1,0:T(8,128)S(1)}, f32[2,16,256]{2,1,0:T(8,128)S(1)}, u32[]{:S(2)}, u32[]{:S(2)}) collective-permute-start(f32[2,16,256]{2,1,0:T(8,128)S(1)} %get-tuple-element.35), channel_id=1, source_target_pairs={{4,0},{8,4},{12,8},{5,1},{9,5},{13,9},{6,2},{10,6},{14,10},{7,3},{... | collective-permute-start | bytes 98312 | tf_op jit(solution)/shard_map/ppermute | solution.py:25
  126.8 3.9 %collective-permute-start.28 = (f32[36,2,256]{2,1,0:T(2,128)S(1)}, f32[36,2,256]{2,1,0:T(2,128)S(1)}, u32[]{:S(2)}, u32[]{:S(2)}) collective-permute-start(f32[36,2,256]{2,1,0:T(2,128)S(1)} %get-tuple-element.8), channel_id=1, source_target_pairs={{0,1},{1,2},{2,3},{4,5},{5,6},{6,7},{8,9},{9,10},{10,11},{12,13},{... | collective-permute-start | bytes 221192 | tf_op jit(solution)/shard_map/ppermute | solution.py:24
  128.7 6.2 %collective-permute-start.29 = (f32[36,2,256]{2,1,0:T(2,128)S(1)}, f32[36,2,256]{2,1,0:T(2,128)S(1)}, u32[]{:S(2)}, u32[]{:S(2)}) collective-permute-start(f32[36,2,256]{2,1,0:T(2,128)S(1)} %get-tuple-element.9), channel_id=1, source_target_pairs={{1,0},{2,1},{3,2},{5,4},{6,5},{7,6},{9,8},{10,9},{11,10},{13,12},{... | collective-permute-start | bytes 221192 | tf_op jit(solution)/shard_map/ppermute | solution.py:25
  (3 other events, 5.3 us)
where the time goes:
time: 139 us; the launch traced here: 138 us
  starting transfers between devices  62.3 us (45%)
  waiting for transfers between devices  54.7 us (39%)
  other arithmetic  13.2 us (9%)
  local copies, waits for them, and re-layouts  5.78 us (4%)
  between operations  1.87 us (1%)
    ppermute x12, waiting for transfers between devices, padded_2(): after = lax.ppermute(initial, axis, down)  47.3 us
    ppermute x12, starting transfers between devices, padded_2(): before = lax.ppermute(last, axis, up)  38.6 us
    ppermute x12, starting transfers between devices, padded_2(): after = lax.ppermute(initial, axis, down)  15.5 us
    ppermute x6, starting transfers between devices, shifted(): return lax.ppermute(x, axis, pairs)  8.24 us
    ppermute x6, waiting for transfers between devices, shifted(): return lax.ppermute(x, axis, pairs)  4.43 us
    add x2, other arithmetic, sweep_once(): middle + half_step * (middle_rate - slopes[1])  3.82 us
    slice x8, local copies, waits for them, and re-layouts, tendency(): above_cells = jnp.concatenate([centre[:, :, 1:], centre[:, :, -1:]], axis=2)  3.31 us
    add x3, other arithmetic, tendency(): strength * spread - 0.5 * carried  3.06 us
  transfers between devices with their start and end apart: 30, of which 25 were waited for; matrix products, arithmetic and copies ran while one was open for 6% of the time, Pallas kernels for 0%

commit v1 on v0

v1 whole, which is shorter than its diff:
```python
import functools
import jax
import jax.numpy as jnp
from jax import lax
from jax.experimental import pallas as pl
from jax.experimental.pallas import tpu as pltpu
from jax.sharding import PartitionSpec as P

SWEEPS = 3
HALO = 4 * SWEEPS
LANES = 128
TILE = 8
time_step = 0.5
half_step = 0.25
diffusion_low = 0.04
diffusion_high = 0.1
first_weights = (5.0 / 24.0, 1.0 / 3.0, -1.0 / 24.0)
second_weights = (-1.0 / 24.0, 1.0 / 3.0, 5.0 / 24.0)


def row_classes(reach, own):
    steps = reach // 2
    groups = {}
    for a in range(steps, -1, -1):
        beside = 2 * (steps - a) if a else reach
        tiles = -(-(own + 2 * beside) // TILE)
        groups.setdefault(tiles, []).append(a)
    out = []
    for tiles, members in sorted(groups.items()):
        beside = max(2 * (steps - a) if a else reach for a in members)
        out.append((tiles, HALO - beside, min(members), max(members)))
    return out


def growth(u):
    return 0.75 - 0.5 / (1.0 + u * u)


def sweeps(n, slices, own_rows, own_columns, codes, wind, mix, first, g0, g1, mid, act, middle_out, final_out):
    halves = mix.shape[0]
    lane = lax.broadcasted_iota(jnp.int32, (TILE, LANES), 1)
    line = lax.broadcasted_iota(jnp.int32, (TILE, LANES), 0)
    bottom, top = lane == 0, lane == LANES - 1
    cx = [jnp.broadcast_to(-0.5 * wind[0:1, z * LANES:(z + 1) * LANES], (TILE, LANES)) for z in range(halves)]
    cy = [jnp.broadcast_to(-0.5 * wind[1:2, z * LANES:(z + 1) * LANES], (TILE, LANES)) for z in range(halves)]
    c3 = [3.0 * (a + b) for a, b in zip(cx, cy)]
    parity = lax.rem(n, 2)
    before = jnp.maximum(n - 1, 0)
    other = lax.rem(before, 2)
    fslot = jnp.where(n == 0, 0, 1 + parity)

    def prior(sweep):
        if sweep == 1:
            return before, jnp.where(before == 0, 0, 1 + other)
        return (jnp.where(n == 0, 0, slices + 2 * other + sweep - 2),
                jnp.where(n == 0, 0, 3 + 2 * other + sweep - 2))

    def evaluate(reach, source, active, finish):
        def block(x, column, tiles):
            for k in range(tiles):
                y = column + TILE * k
                edges = [e for e in (HALO, HALO + own_columns) if y < e < y + TILE]
                sides = [sum(p >= e for e in (HALO, HALO + own_columns)) for p in [y] + edges]
                words = [codes[x * 3 + j] for j in sides]
                kh = [jnp.where(w >= 8, 0.0, jnp.where(w >= 4, diffusion_high, diffusion_low)) for w in words]
                step_x = [1 - 2 * lax.rem(w, 2) for w in words]
                step_y = [1 - 2 * lax.rem(w // 2, 2) for w in words]

                def merge(parts):
                    got = parts[-1]
                    for e, part in zip(reversed(edges), reversed(parts[:-1])):
                        got = jnp.where(line < e - y, part, got)
                    return got
                strength = merge([jnp.full((TILE, LANES), s, jnp.float32) for s in kh])
                u = [{} for _ in range(halves)]
                for z in range(halves):
                    src, a_ref = source(z), active(z)
                    col = {i: src[x + i, pl.ds(y, TILE), :] for i in (-1, 0, 1, 2)}
                    act_c = {i: a_ref[x + i, pl.ds(y, TILE), :] for i in (-1, 0, 1, 2)}
                    flux = [(act_c[i] + act_c[i + 1]) * (col[i + 1] - col[i]) for i in (-1, 0, 1)]
                    for r in range(2):
                        uc, ac = col[r], act_c[r]
                        spread = flux[r + 1] - flux[r]
                        for s in (1, -1):
                            un = src[x + r, pl.ds(y + s, TILE), :]
                            an = a_ref[x + r, pl.ds(y + s, TILE), :]
                            spread = spread + (ac + an) * (un - uc)
                        near_x = merge([src[x + r - s, pl.ds(y, TILE), :] for s in step_x])
                        far_x = merge([src[x + r - 2 * s, pl.ds(y, TILE), :] for s in step_x])
                        near_y = merge([src[x + r, pl.ds(y - s, TILE), :] for s in step_y])
                        far_y = merge([src[x + r, pl.ds(y - 2 * s, TILE), :] for s in step_y])
                        total = (strength * spread + c3[z] * uc + cx[z] * (far_x - 4.0 * near_x)
                                 + cy[z] * (far_y - 4.0 * near_y))
                        u[z][r] = (uc, total)
                for r in range(2):
                    ups = [pltpu.roll(u[z][r][0], LANES - 1, 1) for z in range(halves)]
                    downs = [pltpu.roll(u[z][r][0], 1, 1) for z in range(halves)]
                    rates = []
                    for z in range(halves):
                        uc, total = u[z][r]
                        above = jnp.where(top, ups[z + 1] if z + 1 < halves else uc, ups[z])
                        below = jnp.where(bottom, downs[z - 1] if z else uc, downs[z])
                        rates.append(total + mix[z, x + r, pl.ds(y, TILE), :] * ((above - uc) + (below - uc)))
                    finish(x + r, y, rates, [u[z][r][0] for z in range(halves)])

        for tiles, column, near, far in row_classes(reach, own_columns):
            if near == 0:
                count, begin = own_rows // 2 + 2 * far, HALO - 2 * far

                @pl.loop(0, count)
                def _(i, begin=begin, column=column, tiles=tiles):
                    block(begin + 2 * i, column, tiles)
            else:
                width = far - near + 1

                @pl.loop(0, 2 * width)
                def _(i, column=column, tiles=tiles, near=near, far=far, width=width):
                    low = HALO - 2 * far + 2 * i
                    high = HALO + own_rows + 2 * (near - 1) + 2 * (i - width)
                    block(jnp.where(i < width, low, high), column, tiles)

    def at(ref, *lead):
        return lambda z: ref.at[(*lead, z)]

    def put(ref, lead, z, x, y, value):
        ref[(*lead, z, x, pl.ds(y, TILE), slice(None))] = value

    def get(ref, lead, z, x, y):
        return ref[(*lead, z, x, pl.ds(y, TILE), slice(None))]

    w1 = [time_step * w for w in first_weights]
    w2 = [time_step * w for w in second_weights]
    q1, q2 = sum(w1), sum(w2)
    first_1, g0_1 = prior(1)
    first_2, g0_2 = prior(2)
    first_3, g0_3 = prior(3)
    last_1, last_2 = slices + 2 * parity, slices + 2 * parity + 1
    rate_1, rate_2 = 3 + 2 * parity, 4 + 2 * parity
    start = n == 0

    def end_1(x, y, rates, us):
        for z, f in enumerate(rates):
            put(g0, (fslot,), z, x, y, f)
            g = jnp.where(start, f, get(g0, (g0_1,), z, x, y))
            m = get(first, (first_1,), z, x, y) + half_step * (g - f) + q1 * f
            put(mid, (), z, x, y, m)
            put(act, (1,), z, x, y, growth(m))

    def end_2(x, y, rates, us):
        for z, g in enumerate(rates):
            put(g1, (0,), z, x, y, g)
            f = get(g0, (fslot,), z, x, y)
            last = us[z] + half_step * (g - f) + q2 * f
            put(first, (last_1,), z, x, y, last)
            put(act, (0,), z, x, y, growth(last))

    def end_3(x, y, rates, us):
        for z, g in enumerate(rates):
            put(g0, (rate_1,), z, x, y, g)
            m = (get(first, (first_2,), z, x, y) + half_step * get(g0, (g0_2,), z, x, y)
                 + (w1[0] - half_step) * get(g0, (g0_1,), z, x, y) + w1[1] * get(g1, (0,), z, x, y) + w1[2] * g)
            put(mid, (), z, x, y, m)
            put(act, (1,), z, x, y, growth(m))

    def end_4(x, y, rates, us):
        for z, g in enumerate(rates):
            put(g1, (1,), z, x, y, g)
            last = (us[z] + half_step * g + w2[0] * get(g0, (g0_1,), z, x, y)
                    + (w2[1] - half_step) * get(g1, (0,), z, x, y) + w2[2] * get(g0, (rate_1,), z, x, y))
            put(first, (last_2,), z, x, y, last)
            put(act, (0,), z, x, y, growth(last))

    def end_5(x, y, rates, us):
        for z, g in enumerate(rates):
            put(g0, (rate_2,), z, x, y, g)
            m = (get(first, (first_3,), z, x, y) + half_step * get(g0, (g0_3,), z, x, y)
                 + (w1[0] - half_step) * get(g0, (g0_2,), z, x, y) + w1[1] * get(g1, (1,), z, x, y) + w1[2] * g)
            put(mid, (), z, x, y, m)
            put(act, (1,), z, x, y, growth(m))

    def end_6(x, y, rates, us):
        for z, g in enumerate(rates):
            last = (us[z] + half_step * g + w2[0] * get(g0, (g0_2,), z, x, y)
                    + (w2[1] - half_step) * get(g1, (1,), z, x, y) + w2[2] * get(g0, (rate_2,), z, x, y))
            where = (n, x - HALO, pl.ds(y - HALO, TILE), pl.ds(z * LANES, LANES))
            middle_out[where] = us[z]
            final_out[where] = last

    evaluate(10, at(first, n), at(act, 0), end_1)
    evaluate(8, at(mid), at(act, 1), end_2)
    evaluate(6, at(first, last_1), at(act, 0), end_3)
    evaluate(4, at(mid), at(act, 1), end_4)
    evaluate(2, at(first, last_2), at(act, 0), end_5)
    evaluate(0, at(mid), at(act, 1), end_6)


def outside(word, low_x, low_y):
    return jnp.where(word == 0, 8 + (0 if low_x else 1) + (0 if low_y else 2), word - 1)


def fill(first, act, mix, a, z, x, y, value, slices):
    where = (z, x, pl.ds(y, value.shape[0]), slice(None))
    if a < slices:
        first[(a, *where)] = value
    else:
        mix[where] = value


def corner_rows():
    offset = 0
    for d in range(HALO):
        wide = HALO - 2 * (d // 2 + 1)
        if wide:
            yield d, offset, wide
            offset += wide


CORNER = sum(w for _, _, w in corner_rows())


def pack_kernel(where_ref, code, own, other, mixing, beside_x, beside_y, diagonal_1, diagonal_2):
    t = where_ref[0]
    rows, columns, levels = own.shape
    halves = levels // LANES
    deep = rows - HALO
    word = jnp.full((TILE, LANES), (code[0, 0] + 1).astype(jnp.float32))
    beside_x[beside_x.shape[0] - 1] = jnp.full(beside_x.shape[1:], (code[0, 0] + 1).astype(jnp.float32))
    for ref in (beside_y, diagonal_1, diagonal_2):
        ref[0, 0, pl.ds(ref.shape[2] - TILE, TILE), :] = word

    def side(low):
        for a, pair in enumerate(((own, other) if low else (other, own), (other, own) if low else (own, other), None)):
            ref = mixing if pair is None else pair[0]
            if a < 2:
                ref = (own, other)[a] if low else (other, own)[a]
            at_x = 0 if low else deep
            beside_x[pl.ds(a * HALO, HALO)] = ref[pl.ds(at_x, HALO)]
            at_y = 0 if low else columns - HALO
            for z in range(halves):
                lanes = pl.ds(z * LANES, LANES)

                @pl.loop(0, rows)
                def _(x):
                    line = ref[x, :, lanes]
                    beside_y[a, z, pl.ds(x * HALO, HALO), :] = line[at_y:at_y + HALO]
                for d, offset, wide in corner_rows():
                    x = d if low else rows - 1 - d
                    line = ref[x, :, lanes]
                    near, far = line[:wide], line[columns - wide:]
                    diagonal_1[a, z, pl.ds(offset, wide), :] = near if low else far
                    diagonal_2[a, z, pl.ds(offset, wide), :] = far if low else near

    pl.when(t == 0)(lambda: side(True))
    pl.when(t != 0)(lambda: side(False))


def pair_kernel(where_ref, code, wind, own, other, mixing, halo_x, halo_y, passed_y, corner_1, corner_2,
                middle_out, final_out, first, g0, g1, mid, act, mix, codes):
    t = where_ref[0]
    block_rows, columns, levels = own.shape
    halves = levels // LANES
    half = block_rows // 2
    inner = half + HALO
    tail = halo_y.shape[2] - TILE

    def word_of(tile):
        return jnp.max(tile).astype(jnp.int32)

    word_x = word_of(halo_x[halo_x.shape[0] - 1, pl.ds(0, TILE), pl.ds(0, LANES)])
    word_y, word_p = word_of(halo_y[0, 0, pl.ds(tail, TILE), :]), word_of(passed_y[0, 0, pl.ds(tail, TILE), :])
    word_1 = word_of(corner_1[0, 0, pl.ds(corner_1.shape[2] - TILE, TILE), :])
    word_2 = word_of(corner_2[0, 0, pl.ds(corner_2.shape[2] - TILE, TILE), :])

    def side(low):
        at_own, from_own, at_x = (HALO, 0, 0) if low else (0, block_rows - inner, inner)
        low_y, high_y = (halo_y, passed_y) if low else (passed_y, halo_y)
        low_corner, high_corner = (corner_1, corner_2) if low else (corner_2, corner_1)
        word_low, word_high = (word_y, word_p) if low else (word_p, word_y)
        corner_low, corner_high = (word_1, word_2) if low else (word_2, word_1)

        @pl.loop(0, inner)
        def _(i):
            codes[(at_own + i) * 3] = outside(word_low, True, True)
            codes[(at_own + i) * 3 + 1] = code[0, 0]
            codes[(at_own + i) * 3 + 2] = outside(word_high, True, False)

        @pl.loop(0, HALO)
        def _(i):
            codes[(at_x + i) * 3] = outside(corner_low, low, True)
            codes[(at_x + i) * 3 + 1] = outside(word_x, low, True)
            codes[(at_x + i) * 3 + 2] = outside(corner_high, low, False)

        for a in range(3):
            ref = mixing if a == 2 else ((own, other)[a] if low else (other, own)[a])
            for z in range(halves):
                lanes = pl.ds(z * LANES, LANES)

                @pl.loop(0, inner)
                def _(i):
                    x = from_own + i
                    for y in range(0, columns, TILE):
                        fill(first, act, mix, a, z, at_own + i, HALO + y, ref[x, pl.ds(y, TILE), lanes], 2)
                    fill(first, act, mix, a, z, at_own + i, 0, low_y[a, z, pl.ds(x * HALO, HALO), :], 2)
                    fill(first, act, mix, a, z, at_own + i, HALO + columns, high_y[a, z, pl.ds(x * HALO, HALO), :], 2)

                @pl.loop(0, HALO)
                def _(i):
                    for y in range(0, columns, TILE):
                        fill(first, act, mix, a, z, at_x + i, HALO + y, halo_x[a * HALO + i, pl.ds(y, TILE), lanes], 2)
                for d, offset, wide in corner_rows():
                    x = HALO - 1 - d if low else inner + d
                    fill(first, act, mix, a, z, x, HALO - wide, low_corner[a, z, pl.ds(offset, wide), :], 2)
                    fill(first, act, mix, a, z, x, HALO + columns, high_corner[a, z, pl.ds(offset, wide), :], 2)

    pl.when(t == 0)(lambda: side(True))
    pl.when(t != 0)(lambda: side(False))

    @pl.loop(0, 2)
    def _(n):
        activate(n, first, act)
        sweeps(n, 2, half, columns, codes, wind, mix, first, g0, g1, mid, act, middle_out, final_out)


def activate(n, first, act):
    rows, columns = first.shape[2:4]

    @pl.loop(0, rows)
    def _(x):
        for z in range(first.shape[1]):
            for y in range(0, columns, TILE):
                act[0, z, x, pl.ds(y, TILE), :] = growth(first[n, z, x, pl.ds(y, TILE), :])


def planes(slices, rows, columns, levels):
    plane = (levels // LANES, rows, columns + TILE, LANES)
    return [pltpu.VMEM((k, *plane), jnp.float32) for k in (slices + 4, 7, 2)] + [
        pltpu.VMEM(plane, jnp.float32), pltpu.VMEM((2, *plane), jnp.float32), pltpu.VMEM(plane, jnp.float32)]


VMEM = pl.BlockSpec(memory_space=pltpu.VMEM)
SMEM = pl.BlockSpec(memory_space=pltpu.SMEM)
LIMIT = 56 * 2**20


def of(*shape):
    return jax.ShapeDtypeStruct(shape, jnp.float32)


def pair_solution(state, code, wind, mixing, sizes):
    axes = ("tm", "gx", "gy")
    rows, columns, levels = state.shape
    halves = levels // LANES
    t = lax.axis_index("tm")
    where = t.astype(jnp.int32).reshape(1)

    def partners(step_x, step_y):
        pairs = []
        for x in range(sizes[1]):
            for y in range(sizes[2]):
                u, v = x - step_x, y - step_y
                if 0 <= u < sizes[1] and 0 <= v < sizes[2]:
                    here, there = x * sizes[2] + y, (sizes[1] + u) * sizes[2] + v
                    pairs += [(here, there), (there, here)]
        return pairs

    swap = [(0, 1), (1, 0)]
    other = lax.ppermute(state, "tm", swap)
    packed = pl.pallas_call(
        pack_kernel,
        out_shape=(of(3 * HALO + 1, columns, levels), of(3, halves, rows * HALO + TILE, LANES),
                   of(3, halves, CORNER + 12, LANES), of(3, halves, CORNER + 12, LANES)),
        in_specs=[SMEM, SMEM, VMEM, VMEM, VMEM], out_specs=[VMEM] * 4,
        compiler_params=pltpu.CompilerParams(vmem_limit_bytes=LIMIT),
    )(where, code, state, other, mixing)
    halo_x = lax.ppermute(packed[0], axes, partners(1, 0))
    halo_y = lax.ppermute(packed[1], axes, partners(0, 1))
    corner_1 = lax.ppermute(packed[2], axes, partners(1, 1))
    corner_2 = lax.ppermute(packed[3], axes, partners(1, -1))
    passed_y = lax.ppermute(halo_y, "tm", swap)
    half = rows // 2
    out = of(2, half, columns, levels)
    middle, final = pl.pallas_call(
        pair_kernel, out_shape=(out, out),
        in_specs=[SMEM, SMEM] + [VMEM] * 9, out_specs=[VMEM] * 2,
        scratch_shapes=planes(2, half + 2 * HALO, columns + 2 * HALO, levels) + [
            pltpu.SMEM((3 * (half + 2 * HALO),), jnp.int32)],
        compiler_params=pltpu.CompilerParams(vmem_limit_bytes=LIMIT),
    )(where, code, wind, state, other, mixing, halo_x, halo_y, passed_y, corner_1, corner_2)
    both = jnp.stack([middle, final])
    mine = lax.dynamic_index_in_dim(both, t, 1, keepdims=False)
    got = lax.ppermute(lax.dynamic_index_in_dim(both, 1 - t, 1, keepdims=False), "tm", swap)
    whole = jnp.where(t == 0, jnp.concatenate([mine, got], 1), jnp.concatenate([got, mine], 1))
    return whole[0][None], whole[1][None]


def whole_kernel(own_rows, own_columns, codes, wind, state, mixing, middle_out, final_out, first, g0, g1, mid, act, mix):
    slices, rows, columns, levels = state.shape

    @pl.loop(0, rows)
    def _(x):
        for z in range(levels // LANES):
            lanes = pl.ds(z * LANES, LANES)
            for y in range(0, columns, TILE):
                mix[z, x, pl.ds(y, TILE), :] = mixing[x, pl.ds(y, TILE), lanes]
                for n in range(slices):
                    first[n, z, x, pl.ds(y, TILE), :] = state[n, x, pl.ds(y, TILE), lanes]

    @pl.loop(0, slices)
    def _(n):
        activate(n, first, act)
        sweeps(n, slices, own_rows, own_columns, codes, wind, mix, first, g0, g1, mid, act, middle_out, final_out)


def padded(x, sides, width):
    for axis, dim in sides:
        devices, length = lax.axis_size(axis), x.shape[dim]
        up = [(i, i + 1) for i in range(devices - 1)]
        down = [(j, i) for i, j in up]
        before = lax.ppermute(lax.slice_in_dim(x, length - width, length, axis=dim), axis, up)
        after = lax.ppermute(lax.slice_in_dim(x, 0, width, axis=dim), axis, down)
        x = jnp.concatenate([before, x, after], axis=dim)
    return x


def any_solution(state, code, wind, mixing, sizes):
    slices = sizes[0]
    rows, columns, levels = state.shape
    t, share = lax.axis_index("tm"), rows // slices
    wide = padded(jnp.stack([state, mixing]), (("gx", 1), ("gy", 2)), HALO)
    words = padded((code + 1).astype(jnp.float32), (("gx", 0), ("gy", 1)), 1).astype(jnp.int32)
    table = jnp.stack([jnp.stack([outside(words[i, j], i == 0, j == 0) for j in range(3)]) for i in range(3)])
    cut = functools.partial(lax.dynamic_slice_in_dim, start_index=t * share, slice_size=share + 2 * HALO)
    state = cut(lax.all_gather(wide[0], "tm"), axis=1)
    mixing = cut(wide[1], axis=0)
    line = t * share + jnp.arange(share + 2 * HALO)
    codes = table[(line >= HALO).astype(jnp.int32) + (line >= HALO + rows).astype(jnp.int32)].reshape(-1)
    out = of(slices, share, columns, levels)
    both = pl.pallas_call(
        functools.partial(whole_kernel, share, columns), out_shape=(out, out),
        in_specs=[SMEM] + [VMEM] * 3, out_specs=[VMEM] * 2,
        scratch_shapes=planes(slices, share + 2 * HALO, columns + 2 * HALO, levels),
        compiler_params=pltpu.CompilerParams(vmem_limit_bytes=LIMIT),
    )(codes, wind, state, mixing)
    return tuple(lax.all_to_all(x, "tm", 0, 1, tiled=True) for x in both)


def solution(mesh):
    sizes = tuple(mesh.shape[a] for a in ("tm", "gx", "gy"))
    run = pair_solution if sizes[0] == 2 else any_solution

    def shards(start_states, wind_code, wind_profile, vertical_mix):
        return run(start_states[0], wind_code, wind_profile, vertical_mix, sizes)

    in_specs = (P("tm", "gx", "gy", None), P("gx", "gy"), P(), P("gx", "gy", None))
    out_specs = (P("tm", "gx", "gy", None), P("tm", "gx", "gy", None))
    return jax.shard_map(shards, mesh=mesh, in_specs=in_specs, out_specs=out_specs, check_vma=False)
```

time: 139 us -> 90.1 us (0.65)
  the two profiles are of different devices: /device:TPU:0 before, /device:TPU:19 now
where the time goes in v1:
time: 90.1 us; the launch traced here: 89.8 us
  waiting for transfers between devices  36 us (40%)
  Pallas kernels  33.3 us (37%)
  starting transfers between devices  14 us (16%)
  local copies, waits for them, and re-layouts  3.65 us (4%)
  between operations  1.37 us (2%)
  other arithmetic  1.35 us (1%)
    pallas_call x1, Pallas kernels, pair_solution(): pl.pallas_call(pair_kernel, out_shape=(out, out), in_specs=[SMEM, SMEM] +...  29.3 us
    ppermute x1, waiting for transfers between devices, pair_solution(): halo_y = lax.ppermute(packed[1], axes, partners(0, 1))  14.5 us
    ppermute x1, waiting for transfers between devices, pair_solution(): halo_x = lax.ppermute(packed[0], axes, partners(1, 0))  9.55 us
    ppermute x1, waiting for transfers between devices, pair_solution(): corner_1 = lax.ppermute(packed[2], axes, partners(1, 1))  5.31 us
    ppermute x1, starting transfers between devices, pair_solution(): corner_1 = lax.ppermute(packed[2], axes, partners(1, 1))  4.34 us
    pallas_call x1, Pallas kernels, pair_solution(): pl.pallas_call(pack_kernel, out_shape=(of(3 * HALO + 1, columns, levels),...  3.98 us
    ppermute x1, waiting for transfers between devices, pair_solution(): corner_2 = lax.ppermute(packed[3], axes, partners(1, -1))  3.68 us
    ppermute x1, starting transfers between devices, pair_solution(): halo_y = lax.ppermute(packed[1], axes, partners(0, 1))  3.46 us
  transfers between devices with their start and end apart: 7, of which 6 were waited for; matrix products, arithmetic and copies ran while one was open for 0% of the time, Pallas kernels for 0%

profile of v1, /device:TPU:19, one launch (start us, length us, event | category | flops | bytes accessed | tf_op | source)
XLA Modules:
  0.0 89.8 jit_solution(13331384926170681985)
XLA Ops:
  0.6 0.7 collective-permute-start
  2.0 1.1 %collective-permute-done.other = f32[32,16,256]{2,1,0:T(8,128)S(1)} collective-permute-done((f32[32,16,256]{2,1,0:T(8,128)}, f32[32,16,256]{2,1,0:T(8,128)S(1)}, u32[]{:S(2)}, u32[]{:S(2)}) %collective-permute-start) | collective-permute-done | bytes 524320 | tf_op jit(solution)/shard_map/ppermute | solution.py:367
  3.1 0.0 copy-start
  3.1 0.8 copy-done
  3.9 4.0 %shard_map.59 = (f32[37,16,256]{2,1,0:T(8,128)}, f32[3,2,392,128]{3,2,1,0:T(8,128)}, f32[3,2,72,128]{3,2,1,0:T(8,128)}, f32[3,2,72,128]{3,2,1,0:T(8,128)}) custom-call(s32[1]{0:T(128)} %bitcast.where_ref, s32[1,1]{1,0:T(1,128)S(6)} %copy.6.code, f32[32,16,256]{2,1,0:T(8,128)} %bitcast.9, f32[32,16,256]{2,1,0:T(8,128)} %copy-done, f32[32,16,256]{2,1,0:T(8,128)} %mixing.3), custom_call_target="tpu_custom_call" | custom-call | tf_op jit(solution)/shard_map/pallas_call | solution.py:368
  7.9 3.5 %collective-permute-start.2 = (f32[3,2,392,128]{3,2,1,0:T(8,128)}, f32[3,2,392,128]{3,2,1,0:T(8,128)S(1)}, u32[]{:S(2)}, u32[]{:S(2)}) collective-permute-start(f32[3,2,392,128]{3,2,1,0:T(8,128)} %get-tuple-element.9), channel_id=1, source_target_pairs={{1,16},{16,1},{2,17},{17,2},{3,18},{18,3},{5,20},{20,5},{6,21},{21... | collective-permute-start | bytes 3612680 | tf_op jit(solution)/shard_map/ppermute | solution.py:376
  11.4 14.5 %collective-permute-done.2.halo_y = f32[3,2,392,128]{3,2,1,0:T(8,128)S(1)} collective-permute-done((f32[3,2,392,128]{3,2,1,0:T(8,128)}, f32[3,2,392,128]{3,2,1,0:T(8,128)S(1)}, u32[]{:S(2)}, u32[]{:S(2)}) %collective-permute-start.2) | collective-permute-done | bytes 1204256 | tf_op jit(solution)/shard_map/ppermute | solution.py:376
  25.9 0.0 copy-start.1
  25.9 0.4 collective-permute-start.3
  26.3 3.1 %collective-permute-start.1 = (f32[37,16,256]{2,1,0:T(8,128)}, f32[37,16,256]{2,1,0:T(8,128)S(1)}, u32[]{:S(2)}, u32[]{:S(2)}) collective-permute-start(f32[37,16,256]{2,1,0:T(8,128)} %get-tuple-element.8), channel_id=1, source_target_pairs={{4,16},{16,4},{5,17},{17,5},{6,18},{18,6},{7,19},{19,7},{8,20},{20... | collective-permute-start | bytes 1818632 | tf_op jit(solution)/shard_map/ppermute | solution.py:375
  29.4 4.3 %collective-permute-start.4 = (f32[3,2,72,128]{3,2,1,0:T(8,128)}, f32[3,2,72,128]{3,2,1,0:T(8,128)S(1)}, u32[]{:S(2)}, u32[]{:S(2)}) collective-permute-start(f32[3,2,72,128]{3,2,1,0:T(8,128)} %get-tuple-element.10), channel_id=1, source_target_pairs={{5,16},{16,5},{6,17},{17,6},{7,18},{18,7},{9,20},{20,9},{10,21},{2... | collective-permute-start | bytes 663560 | tf_op jit(solution)/shard_map/ppermute | solution.py:377
  33.7 1.9 %collective-permute-start.5 = (f32[3,2,72,128]{3,2,1,0:T(8,128)}, f32[3,2,72,128]{3,2,1,0:T(8,128)S(1)}, u32[]{:S(2)}, u32[]{:S(2)}) collective-permute-start(f32[3,2,72,128]{3,2,1,0:T(8,128)} %get-tuple-element.11), channel_id=1, source_target_pairs={{4,17},{17,4},{5,18},{18,5},{6,19},{19,6},{8,21},{21,8},{9,22},{22... | collective-permute-start | bytes 663560 | tf_op jit(solution)/shard_map/ppermute | solution.py:378
  35.7 5.3 %collective-permute-done.4.corner_1 = f32[3,2,72,128]{3,2,1,0:T(8,128)S(1)} collective-permute-done((f32[3,2,72,128]{3,2,1,0:T(8,128)}, f32[3,2,72,128]{3,2,1,0:T(8,128)S(1)}, u32[]{:S(2)}, u32[]{:S(2)}) %collective-permute-start.4) | collective-permute-done | bytes 221216 | tf_op jit(solution)/shard_map/ppermute | solution.py:377
  41.0 0.0 copy-start.4
  41.0 3.7 %collective-permute-done.5.corner_2 = f32[3,2,72,128]{3,2,1,0:T(8,128)S(1)} collective-permute-done((f32[3,2,72,128]{3,2,1,0:T(8,128)}, f32[3,2,72,128]{3,2,1,0:T(8,128)S(1)}, u32[]{:S(2)}, u32[]{:S(2)}) %collective-permute-start.5) | collective-permute-done | bytes 221216 | tf_op jit(solution)/shard_map/ppermute | solution.py:378
  44.7 0.0 copy-start.5
  44.7 9.6 %collective-permute-done.1.halo_x = f32[37,16,256]{2,1,0:T(8,128)S(1)} collective-permute-done((f32[37,16,256]{2,1,0:T(8,128)}, f32[37,16,256]{2,1,0:T(8,128)S(1)}, u32[]{:S(2)}, u32[]{:S(2)}) %collective-permute-start.1) | collective-permute-done | bytes 606240 | tf_op jit(solution)/shard_map/ppermute | solution.py:375
  54.2 0.0 copy-start.3
  54.2 0.0 collective-permute-done.3.passed_y
  54.2 0.0 copy-done.1
  54.2 0.0 copy-done.4
  54.2 0.0 copy-done.5
  54.2 0.8 copy-done.3
  55.0 0.0 copy-start.2
  55.0 1.0 %copy-done.2 = f32[3,2,392,128]{3,2,1,0:T(8,128)} copy-done((f32[3,2,392,128]{3,2,1,0:T(8,128)}, f32[3,2,392,128]{3,2,1,0:T(8,128)S(1)}, u32[]{:S(2)}) %copy-start.2) | copy-done | bytes 1204248
  56.1 29.3 %shard_map.60 = (f32[2,16,16,256]{3,2,1,0:T(8,128)}, f32[2,16,16,256]{3,2,1,0:T(8,128)}) custom-call(s32[1]{0:T(128)} %bitcast.where_ref, s32[1,1]{1,0:T(1,128)S(6)} %copy.6.code, f32[2,256]{1,0:T(2,128)} %wind.1, f32[32,16,256]{2,1,0:T(8,128)} %bitcast.10, f32[32,16,256]{2,1,0:T(8,128)} %copy-done, f32[32,16,256]{2,1,0:T(8,128)} %mixing.3, ...), custom_call_target="tpu_custom_call" | custom-call | tf_op jit(solution)/shard_map/pallas_call | solution.py:382
  85.4 1.3 %fusion.3 = (f32[2,16,16,256]{3,2,1,0:T(8,128)S(1)}, f32[2,16,16,256]{3,2,1,0:T(8,128)S(1)}) fusion(s32[]{:T(128)S(6)} %select_n.16, f32[1,2,16,16,256]{4,3,2,1,0:T(8,128)} %bitcast.11, f32[1,2,16,16,256]{4,3,2,1,0:T(8,128)} %bitcast.12, s32[]{:T(128)S(6)} %select_n.17), kind=kLoop, calls=%fused_computation.8 | loop fusion | flops 262144 | bytes 2097160 | tf_op jit(solution)/shard_map/jit(dynamic_index_in_dim)/squeeze | solution.py:390
  86.7 0.1 collective-permute-start.6
  86.7 1.9 %collective-permute-done.6 = f32[2,16,16,256]{3,2,1,0:T(8,128)S(1)} collective-permute-done((f32[2,16,16,256]{3,2,1,0:T(8,128)S(1)}, f32[2,16,16,256]{3,2,1,0:T(8,128)S(1)}, u32[]{:S(2)}, u32[]{:S(2)}) %collective-permute-start.6) | collective-permute-done | bytes 524320 | tf_op jit(solution)/shard_map/ppermute | solution.py:391
  88.6 0.1 maximum_select_fusion
  88.7 1.0 %fusion.4 = (f32[1,32,16,256]{3,2,1,0:T(8,128)}, f32[1,32,16,256]{3,2,1,0:T(8,128)}) fusion(f32[2,32,16,256]{3,2,1,0:T(8,128)S(1)} %maximum_select_fusion), kind=kLoop, calls=%fused_computation.9 | loop fusion | bytes 2097152 | tf_op jit(solution)/shard_map/slice | solution.py:393
Async XLA Ops:
  0.6 2.5 %collective-permute-start = (f32[32,16,256]{2,1,0:T(8,128)}, f32[32,16,256]{2,1,0:T(8,128)S(1)}, u32[]{:S(2)}, u32[]{:S(2)}) collective-permute-start(f32[32,16,256]{2,1,0:T(8,128)} %bitcast.8), channel_id=1, source_target_pairs={{0,16},{16,0},{1,17},{17,1},{2,18},{18,2},{3,19},{19,3},{4,20},{20... | collective-permute-start | bytes 1572872 | tf_op jit(solution)/shard_map/ppermute | solution.py:367
  3.1 0.8 copy-start
  7.9 18.0 %collective-permute-start.2 = (f32[3,2,392,128]{3,2,1,0:T(8,128)}, f32[3,2,392,128]{3,2,1,0:T(8,128)S(1)}, u32[]{:S(2)}, u32[]{:S(2)}) collective-permute-start(f32[3,2,392,128]{3,2,1,0:T(8,128)} %get-tuple-element.9), channel_id=1, source_target_pairs={{1,16},{16,1},{2,17},{17,2},{3,18},{18,3},{5,20},{20,5},{6,21},{21... | collective-permute-start | bytes 3612680 | tf_op jit(solution)/shard_map/ppermute | solution.py:376
  25.9 28.3 %copy-start.1 = (f32[3,2,392,128]{3,2,1,0:T(8,128)}, f32[3,2,392,128]{3,2,1,0:T(8,128)S(1)}, u32[]{:S(2)}) copy-start(f32[3,2,392,128]{3,2,1,0:T(8,128)S(1)} %collective-permute-done.2.halo_y) | copy-start | bytes 3612676
  25.9 28.3 %collective-permute-start.3 = (f32[3,2,392,128]{3,2,1,0:T(8,128)S(1)}, f32[3,2,392,128]{3,2,1,0:T(8,128)S(1)}, u32[]{:S(2)}, u32[]{:S(2)}) collective-permute-start(f32[3,2,392,128]{3,2,1,0:T(8,128)S(1)} %collective-permute-done.2.halo_y), channel_id=1, source_target_pairs={{0,16},{16,0},{1,17},{17,1},{2,18},{18,2},{3,19},{19,3},{4,20},{20... | collective-permute-start | bytes 3612680 | tf_op jit(solution)/shard_map/ppermute | solution.py:379
  26.3 27.9 %collective-permute-start.1 = (f32[37,16,256]{2,1,0:T(8,128)}, f32[37,16,256]{2,1,0:T(8,128)S(1)}, u32[]{:S(2)}, u32[]{:S(2)}) collective-permute-start(f32[37,16,256]{2,1,0:T(8,128)} %get-tuple-element.8), channel_id=1, source_target_pairs={{4,16},{16,4},{5,17},{17,5},{6,18},{18,6},{7,19},{19,7},{8,20},{20... | collective-permute-start | bytes 1818632 | tf_op jit(solution)/shard_map/ppermute | solution.py:375
  29.4 11.6 %collective-permute-start.4 = (f32[3,2,72,128]{3,2,1,0:T(8,128)}, f32[3,2,72,128]{3,2,1,0:T(8,128)S(1)}, u32[]{:S(2)}, u32[]{:S(2)}) collective-permute-start(f32[3,2,72,128]{3,2,1,0:T(8,128)} %get-tuple-element.10), channel_id=1, source_target_pairs={{5,16},{16,5},{6,17},{17,6},{7,18},{18,7},{9,20},{20,9},{10,21},{2... | collective-permute-start | bytes 663560 | tf_op jit(solution)/shard_map/ppermute | solution.py:377
  33.7 10.9 %collective-permute-start.5 = (f32[3,2,72,128]{3,2,1,0:T(8,128)}, f32[3,2,72,128]{3,2,1,0:T(8,128)S(1)}, u32[]{:S(2)}, u32[]{:S(2)}) collective-permute-start(f32[3,2,72,128]{3,2,1,0:T(8,128)} %get-tuple-element.11), channel_id=1, source_target_pairs={{4,17},{17,4},{5,18},{18,5},{6,19},{19,6},{8,21},{21,8},{9,22},{22... | collective-permute-start | bytes 663560 | tf_op jit(solution)/shard_map/ppermute | solution.py:378
  41.0 13.3 %copy-start.4 = (f32[3,2,72,128]{3,2,1,0:T(8,128)}, f32[3,2,72,128]{3,2,1,0:T(8,128)S(1)}, u32[]{:S(2)}) copy-start(f32[3,2,72,128]{3,2,1,0:T(8,128)S(1)} %collective-permute-done.4.corner_1) | copy-start | bytes 663556
  44.7 9.6 %copy-start.5 = (f32[3,2,72,128]{3,2,1,0:T(8,128)}, f32[3,2,72,128]{3,2,1,0:T(8,128)S(1)}, u32[]{:S(2)}) copy-start(f32[3,2,72,128]{3,2,1,0:T(8,128)S(1)} %collective-permute-done.5.corner_2) | copy-start | bytes 663556
  54.2 0.8 copy-start.3
  55.0 1.0 %copy-start.2 = (f32[3,2,392,128]{3,2,1,0:T(8,128)}, f32[3,2,392,128]{3,2,1,0:T(8,128)S(1)}, u32[]{:S(2)}) copy-start(f32[3,2,392,128]{3,2,1,0:T(8,128)S(1)} %collective-permute-done.3.passed_y) | copy-start | bytes 3612676
  86.7 2.0 %collective-permute-start.6 = (f32[2,16,16,256]{3,2,1,0:T(8,128)S(1)}, f32[2,16,16,256]{3,2,1,0:T(8,128)S(1)}, u32[]{:S(2)}, u32[]{:S(2)}) collective-permute-start(f32[2,16,16,256]{3,2,1,0:T(8,128)S(1)} %get-tuple-element.17), channel_id=1, source_target_pairs={{0,16},{16,0},{1,17},{17,1},{2,18},{18,2},{3,19},{19,3},{4,20},{20... | collective-permute-start | bytes 1572872 | tf_op jit(solution)/shard_map/ppermute | solution.py:391

commit v2 on v0

v2 whole, which is shorter than its diff:
```python
import functools
import jax
import jax.numpy as jnp
from jax import lax
from jax.experimental import pallas as pl
from jax.experimental.pallas import tpu as pltpu
from jax.sharding import PartitionSpec as P

SWEEPS = 3
HALO = 4 * SWEEPS
LANES = 128
TILE = 8
time_step = 0.5
half_step = 0.25
diffusion_low = 0.04
diffusion_high = 0.1
first_weights = (5.0 / 24.0, 1.0 / 3.0, -1.0 / 24.0)
second_weights = (-1.0 / 24.0, 1.0 / 3.0, 5.0 / 24.0)


def row_classes(reach, own):
    steps = reach // 2
    groups = {}
    for a in range(steps + 1):
        beside = 2 * (steps - a) if a else reach
        groups.setdefault((-(-(own + 2 * beside) // TILE), a == 0), []).append((a, beside))
    out = []
    for (tiles, _), members in sorted(groups.items()):
        beside = max(b for _, b in members)
        begins = range(max(2, HALO + own + beside - TILE * tiles), HALO - beside + 1)
        cuts = lambda begin: sum(begin < e < begin + TILE * tiles and (e - begin) % TILE > 0 for e in (HALO, HALO + own))
        out.append((tiles, min(begins, key=cuts), members[0][0], members[-1][0]))
    return out


def growth(u):
    return 1.5 - 1.0 / (1.0 + u * u)


def sweeps(own_rows, own_columns, codes, wind, mix, start, mid, last_1, last_2, f, g1, g1b, g2, g2b, act_a, act_b,
           write):
    halves = mix.shape[0]
    slices, parts = range(start.shape[0]), range(halves)
    scale = 0.5 * half_step
    lane = lax.broadcasted_iota(jnp.int32, (TILE, LANES), 1)
    line = lax.broadcasted_iota(jnp.int32, (TILE, LANES), 0)
    bottom, top = lane == 0, lane == LANES - 1
    cx = [jnp.broadcast_to(-0.5 * half_step * wind[0:1, z * LANES:(z + 1) * LANES], (TILE, LANES)) for z in parts]
    cy = [jnp.broadcast_to(-0.5 * half_step * wind[1:2, z * LANES:(z + 1) * LANES], (TILE, LANES)) for z in parts]
    c3 = [3.0 * (a + b) for a, b in zip(cx, cy)]

    def merge(edges, values):
        got = values[-1]
        for e, value in zip(reversed(edges), reversed(values[:-1])):
            got = jnp.where(line < e, value, got)
        return got

    def evaluate(reach, source, active, finish):
        def block(x, count, column, tiles):
            rows = range(count)
            puts, below_flux = [], {}
            for k in range(tiles):
                y = column + TILE * k
                edges = [e - y for e in (HALO, HALO + own_columns) if y < e < y + TILE]
                sides = [sum(p >= e for e in (HALO, HALO + own_columns)) for p in [y] + [y + e for e in edges]]
                words = [codes[x * 3 + j] for j in sides]
                kh = [jnp.where(w >= 8, 0.0, jnp.where(w >= 4, scale * diffusion_high, scale * diffusion_low)) for w in words]
                step_x = [1 - 2 * (w & 1) for w in words]
                step_y = [1 - (w & 2) for w in words]
                strength = merge(edges, [jnp.full((TILE, LANES), s, jnp.float32) for s in kh])
                rates = {}
                for n in slices:
                    def u_at(z, i, j):
                        return source[n, z, x + i, pl.ds(y + j, TILE), :]

                    def a_at(z, i, j):
                        return active[n, z, x + i, pl.ds(y + j, TILE), :]

                    centre = {(z, r): u_at(z, r, 0) for z in parts for r in rows}
                    ups = {c: pltpu.roll(u, LANES - 1, 1) for c, u in centre.items()}
                    downs = {c: pltpu.roll(u, 1, 1) for c, u in centre.items()}
                    total = {}
                    for z in parts:
                        col = [u_at(z, -1, 0)] + [centre[z, r] for r in rows] + [u_at(z, count, 0)]
                        act = [a_at(z, i, 0) for i in range(-1, count + 1)]
                        flux = [(act[i] + act[i + 1]) * (col[i + 1] - col[i]) for i in range(count + 1)]
                        for r in rows:
                            uc, ac = col[r + 1], act[r + 1]
                            up = (ac + a_at(z, r, 1)) * (u_at(z, r, 1) - uc)
                            moved = pltpu.roll(up, 1, 0)
                            if k:
                                down = jnp.where(line == 0, below_flux[n, z, r], moved)
                            else:
                                down = (ac + a_at(z, r, -1)) * (uc - u_at(z, r, -1))
                            below_flux[n, z, r] = moved
                            spread = (flux[r + 1] - flux[r]) + (up - down)
                            near_x = merge(edges, [u_at(z, r - s, 0) for s in step_x])
                            far_x = merge(edges, [u_at(z, r - 2 * s, 0) for s in step_x])
                            near_y = merge(edges, [u_at(z, r, -s) for s in step_y])
                            far_y = merge(edges, [u_at(z, r, -2 * s) for s in step_y])
                            total[z, r] = ((strength * spread + c3[z] * uc) + cx[z] * (far_x - 4.0 * near_x)
                                           + cy[z] * (far_y - 4.0 * near_y))
                    for r in rows:
                        for z in parts:
                            u = centre[z, r]
                            above = jnp.where(top, ups[z + 1, r] if z + 1 < halves else u, ups[z, r])
                            below = jnp.where(bottom, downs[z - 1, r] if z else u, downs[z, r])
                            bend = (above - u) + (below - u)
                            rate = total[z, r] + mix[z, x + r, pl.ds(y, TILE), :] * bend
                            rates[n, z, r] = rate

                            def get(ref, m=n):
                                return ref[m, z, x + r, pl.ds(y, TILE), :]

                            def put(ref, value):
                                puts.append((ref, (n, z, x + r, y), value))
                            finish(get, put, n, rates.get((n - 1, z, r), rate), u, rate)
            for ref, at, value in puts:
                write(ref, at, value)

        for tiles, column, near, far in row_classes(reach, own_columns):
            if near == 0:
                group = 4 if own_rows % 4 == 0 else 2

                @pl.loop(0, own_rows // group)
                def _(i, column=column, tiles=tiles, group=group):
                    block(HALO + group * i, group, column, tiles)
            else:
                span = 2 * (far - near + 1)
                group = 4 if span % 4 == 0 else 2
                width = span // group

                @pl.loop(0, 2 * width, unroll=2 if group == 2 else 1)
                def _(i, column=column, tiles=tiles, near=near, far=far, width=width, group=group):
                    low = HALO - 2 * far + group * i
                    high = HALO + own_rows + 2 * (near - 1) + group * (i - width)
                    block(jnp.where(i < width, low, high), group, column, tiles)

    w1 = [time_step / half_step * w for w in first_weights]
    w2 = [time_step / half_step * w for w in second_weights]
    assert abs(sum(w1) - 1) < 1e-12 and abs(sum(w2) - 1) < 1e-12

    def end_1(get, put, n, earlier, u, rate):
        m = get(start, max(n - 1, 0)) + ((earlier - rate) + rate)
        put(f, rate)
        put(mid, m)
        put(act_b, growth(m))

    def end_2(get, put, n, earlier, u, rate):
        first = get(f)
        last = u + ((rate - first) + first)
        put(g1, rate)
        put(last_1, last)
        put(act_a, growth(last))

    def end_3(get, put, n, earlier, u, rate):
        begin = get(last_1, n - 1) if n else get(start, 0)
        g0 = earlier if n else get(f, 0)
        m = begin + g0 + (w1[0] - 1.0) * get(f, max(n - 1, 0)) + w1[1] * get(g1) + w1[2] * rate
        put(g2, rate)
        put(mid, m)
        put(act_b, growth(m))

    def end_4(get, put, n, earlier, u, rate):
        last = u + rate + w2[0] * get(f, max(n - 1, 0)) + (w2[1] - 1.0) * get(g1) + w2[2] * get(g2)
        put(g1b, rate)
        put(last_2, last)
        put(act_a, growth(last))

    def end_5(get, put, n, earlier, u, rate):
        begin = get(last_2, n - 1) if n else get(start, 0)
        g0 = earlier if n else get(f, 0)
        before = get(g2, n - 1) if n else get(f, 0)
        m = begin + g0 + (w1[0] - 1.0) * before + w1[1] * get(g1b) + w1[2] * rate
        put(g2b, rate)
        put(mid, m)
        put(act_b, growth(m))

    def end_6(get, put, n, earlier, u, rate):
        before = get(g2, n - 1) if n else get(f, 0)
        put("middle", u)
        put("final", u + rate + w2[0] * before + (w2[1] - 1.0) * get(g1b) + w2[2] * get(g2b))

    evaluate(10, start, act_a, end_1)
    evaluate(8, mid, act_b, end_2)
    evaluate(6, last_1, act_a, end_3)
    evaluate(4, mid, act_b, end_4)
    evaluate(2, last_2, act_a, end_5)
    evaluate(0, mid, act_b, end_6)


def outside(word, low_x, low_y):
    return jnp.where(word == 0, 8 + (0 if low_x else 1) + (0 if low_y else 2), word - 1)


DEPTHS = (HALO, HALO, HALO - 2)


def corner_rows():
    out, offset = [], 0
    for a, depth in enumerate(DEPTHS):
        for d in range(depth - 2):
            wide = depth - 2 * (d // 2 + 1)
            out.append((a, d, offset, wide))
            offset += wide
    return out, offset


CORNER_ROWS, CORNER_SIZE = corner_rows()
BEFORE = tuple(sum(DEPTHS[:a]) for a in range(len(DEPTHS) + 1))


def pack_kernel(where_ref, code, own, other, mixing, beside_x, beside_y, diagonal_1, diagonal_2):
    t = where_ref[0]
    rows, columns, levels = own.shape
    word = jnp.full((TILE, LANES), (code[0, 0] + 1).astype(jnp.float32))
    for ref in (beside_x, beside_y, diagonal_1, diagonal_2):
        ref[0, pl.ds(ref.shape[1] - TILE, TILE), :] = word

    def side(low):
        arrays = (own, other, mixing) if low else (other, own, mixing)
        for z in range(levels // LANES):
            lanes = pl.ds(z * LANES, LANES)
            for a, depth in enumerate(DEPTHS):
                for i in range(depth):
                    x = i if low else rows - depth + i
                    beside_x[z, pl.ds((BEFORE[a] + i) * columns, columns), :] = arrays[a][x, :, lanes]
            for a, d, offset, wide in CORNER_ROWS:
                x = d if low else rows - 1 - d
                near, far = arrays[a][x, pl.ds(0, wide), lanes], arrays[a][x, pl.ds(columns - wide, wide), lanes]
                diagonal_1[z, pl.ds(offset, wide), :] = near if low else far
                diagonal_2[z, pl.ds(offset, wide), :] = far if low else near

        @pl.loop(0, rows // 2)
        def _(i):
            for x in (2 * i, 2 * i + 1):
                for z in range(levels // LANES):
                    for a, depth in enumerate(DEPTHS):
                        line = arrays[a][x, pl.ds(0 if low else columns - depth, depth), pl.ds(z * LANES, LANES)]
                        beside_y[z, pl.ds(BEFORE[a] * rows + x * depth, depth), :] = line

    pl.when(t == 0)(lambda: side(True))
    pl.when(t != 0)(lambda: side(False))


def pair_kernel(where_ref, code, wind, own, other, mixing, halo_x, halo_y, passed_y, corner_1, corner_2,
                mine_middle, mine_final, theirs, start, mid, last_1, last_2, f, g1, g1b, g2, g2b, act_a, act_b,
                mix, both, codes):
    t = where_ref[0]
    block_rows, columns, levels = own.shape
    halves = levels // LANES
    half = block_rows // 2
    inner = half + HALO

    def word_of(ref):
        return jnp.max(ref[0, pl.ds(ref.shape[1] - TILE, TILE), :]).astype(jnp.int32)

    word_x, word_y, word_p, word_1, word_2 = [word_of(r) for r in (halo_x, halo_y, passed_y, corner_1, corner_2)]

    def fill(a, z, x, y, value):
        at = (z, x, pl.ds(y, value.shape[0]), slice(None))
        if a < 2:
            start[(a, *at)] = value
            act_a[(a, *at)] = growth(value)
        else:
            mix[at] = half_step * value

    def side(low):
        at_own, from_own, at_x = (HALO, 0, 0) if low else (0, block_rows - inner, inner)
        low_y, high_y = (halo_y, passed_y) if low else (passed_y, halo_y)
        low_corner, high_corner = (corner_1, corner_2) if low else (corner_2, corner_1)
        word_low, word_high = (word_y, word_p) if low else (word_p, word_y)
        corner_low, corner_high = (word_1, word_2) if low else (word_2, word_1)
        arrays = (own, other, mixing) if low else (other, own, mixing)

        @pl.loop(0, inner)
        def _(i):
            codes[(at_own + i) * 3] = outside(word_low, True, True)
            codes[(at_own + i) * 3 + 1] = code[0, 0]
            codes[(at_own + i) * 3 + 2] = outside(word_high, True, False)

        @pl.loop(0, HALO)
        def _(i):
            codes[(at_x + i) * 3] = outside(corner_low, low, True)
            codes[(at_x + i) * 3 + 1] = outside(word_x, low, True)
            codes[(at_x + i) * 3 + 2] = outside(corner_high, low, False)

        @pl.loop(0, inner // 2)
        def _(pair):
            for i in (2 * pair, 2 * pair + 1):
                x = from_own + i
                for z in range(halves):
                    for a, depth in enumerate(DEPTHS):
                        for y in range(0, columns, TILE):
                            fill(a, z, at_own + i, HALO + y, arrays[a][x, pl.ds(y, TILE), pl.ds(z * LANES, LANES)])
                        at = pl.ds(BEFORE[a] * block_rows + x * depth, depth)
                        fill(a, z, at_own + i, HALO - depth, low_y[z, at, :])
                        fill(a, z, at_own + i, HALO + columns, high_y[z, at, :])

        for z in range(halves):
            for a, depth in enumerate(DEPTHS):
                for i in range(depth):
                    x = HALO - depth + i if low else inner + i
                    for y in range(0, columns, TILE):
                        fill(a, z, x, HALO + y, halo_x[z, pl.ds((BEFORE[a] + i) * columns + y, TILE), :])
            for a, d, offset, wide in CORNER_ROWS:
                x = HALO - 1 - d if low else inner + d
                fill(a, z, x, HALO - wide, low_corner[z, pl.ds(offset, wide), :])
                fill(a, z, x, HALO + columns, high_corner[z, pl.ds(offset, wide), :])

    pl.when(t == 0)(lambda: side(True))
    pl.when(t != 0)(lambda: side(False))

    def write(ref, at, value):
        n, z, x, y = at
        if isinstance(ref, str):
            place = jnp.where(t == n, 0, 1)
            both[place, 0 if ref == "middle" else 1, x - HALO, pl.ds(y - HALO, TILE), pl.ds(z * LANES, LANES)] = value
        else:
            ref[n, z, x, pl.ds(y, TILE), :] = value

    sweeps(half, columns, codes, wind, mix, start, mid, last_1, last_2, f, g1, g1b, g2, g2b, act_a, act_b, write)
    here = pl.ds(t * half, half)
    mine_middle[here] = both[0, 0]
    mine_final[here] = both[0, 1]
    theirs[...] = both[1]


VMEM = pl.BlockSpec(memory_space=pltpu.VMEM)
SMEM = pl.BlockSpec(memory_space=pltpu.SMEM)
LIMIT = 56 * 2**20


def of(*shape):
    return jax.ShapeDtypeStruct(shape, jnp.float32)


def pair_shards(state, code, wind, mixing, sizes):
    axes = ("tm", "gx", "gy")
    rows, columns, levels = state.shape
    halves = levels // LANES
    t = lax.axis_index("tm")
    where = t.astype(jnp.int32).reshape(1)

    def partners(step_x, step_y):
        pairs = []
        for x in range(sizes[1]):
            for y in range(sizes[2]):
                u, v = x - step_x, y - step_y
                if 0 <= u < sizes[1] and 0 <= v < sizes[2]:
                    here, there = x * sizes[2] + y, (sizes[1] + u) * sizes[2] + v
                    pairs += [(here, there), (there, here)]
        return pairs

    swap = [(0, 1), (1, 0)]
    other = lax.ppermute(state, "tm", swap)
    corner = of(halves, CORNER_SIZE + TILE, LANES)
    to_x, to_y, to_1, to_2 = pl.pallas_call(
        pack_kernel,
        out_shape=(of(halves, BEFORE[-1] * columns + TILE, LANES), of(halves, BEFORE[-1] * rows + TILE, LANES), corner, corner),
        in_specs=[SMEM, SMEM, VMEM, VMEM, VMEM], out_specs=[VMEM] * 4,
        compiler_params=pltpu.CompilerParams(vmem_limit_bytes=LIMIT),
    )(where, code, state, other, mixing)
    halo_x = lax.ppermute(to_x, axes, partners(1, 0))
    halo_y = lax.ppermute(to_y, axes, partners(0, 1))
    corner_1 = lax.ppermute(to_1, axes, partners(1, 1))
    corner_2 = lax.ppermute(to_2, axes, partners(1, -1))
    halo_x, halo_y, corner_1, corner_2 = lax.optimization_barrier((halo_x, halo_y, corner_1, corner_2))
    passed_y = lax.ppermute(halo_y, "tm", swap)
    half = rows // 2
    plane = (halves, half + 2 * HALO, columns + 2 * HALO + TILE, LANES)
    middle, final, theirs = pl.pallas_call(
        pair_kernel, out_shape=(of(*state.shape), of(*state.shape), of(2, half, columns, levels)),
        in_specs=[SMEM, SMEM] + [VMEM] * 9, out_specs=[VMEM] * 3,
        scratch_shapes=[pltpu.VMEM((2, *plane), jnp.float32)] * 11 + [
            pltpu.VMEM(plane, jnp.float32), pltpu.VMEM((2, 2, half, columns, levels), jnp.float32),
            pltpu.SMEM((3 * (half + 2 * HALO),), jnp.int32)],
        compiler_params=pltpu.CompilerParams(vmem_limit_bytes=LIMIT),
    )(where, code, wind, state, other, mixing, halo_x, halo_y, passed_y, corner_1, corner_2)
    got = lax.ppermute(theirs, "tm", swap)
    there = ((1 - t) * half, 0, 0)
    return lax.dynamic_update_slice(middle, got[0], there)[None], lax.dynamic_update_slice(final, got[1], there)[None]


def padded(x, sides, width):
    for axis, dim in sides:
        devices, length = lax.axis_size(axis), x.shape[dim]
        up = [(i, i + 1) for i in range(devices - 1)]
        down = [(j, i) for i, j in up]
        before = lax.ppermute(lax.slice_in_dim(x, length - width, length, axis=dim), axis, up)
        after = lax.ppermute(lax.slice_in_dim(x, 0, width, axis=dim), axis, down)
        x = jnp.concatenate([before, x, after], axis=dim)
    return x


def tendency(u, sign_x, sign_y, strength, wind, mixing):
    rows, columns = mixing.shape[:2]

    def beside(source, step_x, step_y):
        return source[2 + step_x:2 + step_x + rows, 2 + step_y:2 + step_y + columns]

    centre = beside(u, 0, 0)
    act = 0.5 * growth(u)
    spread = sum((beside(act, 0, 0) + beside(act, *s)) * (beside(u, *s) - centre) for s in ((1, 0), (-1, 0), (0, 1), (0, -1)))
    near_x, far_x = (jnp.where(sign_x > 0, beside(u, -k, 0), beside(u, k, 0)) for k in (1, 2))
    near_y, far_y = (jnp.where(sign_y > 0, beside(u, 0, -k), beside(u, 0, k)) for k in (1, 2))
    carried = wind[0] * (3.0 * centre - 4.0 * near_x + far_x) + wind[1] * (3.0 * centre - 4.0 * near_y + far_y)
    below = jnp.concatenate([centre[:, :, :1], centre[:, :, :-1]], axis=2)
    above = jnp.concatenate([centre[:, :, 1:], centre[:, :, -1:]], axis=2)
    return strength * spread - 0.5 * carried + mixing * (below + above - 2.0 * centre)


def slice_shards(state, code, wind, mixing, sizes):
    word = code[0, 0]
    strength = jnp.where(word // 4 == 1, diffusion_high, diffusion_low)

    def rate_of(u):
        return tendency(padded(u, (("gx", 0), ("gy", 1)), 2), 1 - 2 * (word % 2), 1 - 2 * (word // 2 % 2), strength, wind, mixing)

    start_rate = rate_of(state)
    last, rates = state, (start_rate,) * 3
    for _ in range(SWEEPS):
        arrived = lax.ppermute((last, rates[2]), "tm", [(i, i + 1) for i in range(sizes[0] - 1)])
        first, g0 = (jnp.where(lax.axis_index("tm") == 0, a, b) for a, b in zip((state, start_rate), arrived))
        middle = first + half_step * (g0 - rates[0]) + time_step * sum(w * r for w, r in zip(first_weights, rates))
        g1 = rate_of(middle)
        last = middle + half_step * (g1 - rates[1]) + time_step * sum(w * r for w, r in zip(second_weights, rates))
        rates = g0, g1, rate_of(last)
    return middle[None], last[None]


def solution(mesh):
    sizes = tuple(mesh.shape[a] for a in ("tm", "gx", "gy"))
    run = pair_shards if sizes[0] == 2 else slice_shards

    def shards(start_states, wind_code, wind_profile, vertical_mix):
        return run(start_states[0], wind_code, wind_profile, vertical_mix, sizes)

    in_specs = (P("tm", "gx", "gy", None), P("gx", "gy"), P(), P("gx", "gy", None))
    out_specs = (P("tm", "gx", "gy", None), P("tm", "gx", "gy", None))
    return jax.shard_map(shards, mesh=mesh, in_specs=in_specs, out_specs=out_specs, check_vma=False)
```

time: 139 us -> 58.9 us (0.42)
  the two profiles are of different devices: /device:TPU:0 before, /device:TPU:19 now
where the time goes in v2:
time: 58.9 us; the launch traced here: 58.7 us
  waiting for transfers between devices  21.4 us (36%)
  Pallas kernels  20.6 us (35%)
  starting transfers between devices  12.6 us (21%)
  local copies, waits for them, and re-layouts  2.64 us (4%)
  between operations  1.35 us (2%)
    pallas_call x1, Pallas kernels, pair_shards(): pl.pallas_call(pair_kernel, out_shape=(of(*state.shape), of(*state.shape)...  17.7 us
    ppermute x1, waiting for transfers between devices, pair_shards(): corner_1 = lax.ppermute(to_1, axes, partners(1, 1))  11.6 us
    ppermute x1, waiting for transfers between devices, pair_shards(): halo_x = lax.ppermute(to_x, axes, partners(1, 0))  3.96 us
    ppermute x1, starting transfers between devices, pair_shards(): halo_y = lax.ppermute(to_y, axes, partners(0, 1))  3.45 us
    ppermute x1, starting transfers between devices, pair_shards(): corner_2 = lax.ppermute(to_2, axes, partners(1, -1))  3.32 us
    ppermute x1, starting transfers between devices, pair_shards(): corner_1 = lax.ppermute(to_1, axes, partners(1, 1))  2.93 us
    pallas_call x1, Pallas kernels, pair_shards(): pl.pallas_call(pack_kernel, out_shape=(of(halves, BEFORE[-1] * columns +...  2.89 us
    ppermute x1, waiting for transfers between devices, pair_shards(): passed_y = lax.ppermute(halo_y, 'tm', swap)  2.75 us
  transfers between devices with their start and end apart: 7, of which 5 were waited for; matrix products, arithmetic and copies ran while one was open for 0% of the time, Pallas kernels for 0%

profile of v2, /device:TPU:19, one launch (start us, length us, event | category | flops | bytes accessed | tf_op | source)
XLA Modules:
  0.0 58.7 jit_solution(7255809216594084268)
XLA Ops:
  0.6 0.7 %collective-permute-start = (f32[32,16,256]{2,1,0:T(8,128)}, f32[32,16,256]{2,1,0:T(8,128)S(1)}, u32[]{:S(2)}, u32[]{:S(2)}) collective-permute-start(f32[32,16,256]{2,1,0:T(8,128)} %bitcast.4), channel_id=1, source_target_pairs={{0,16},{16,0},{1,17},{17,1},{2,18},{18,2},{3,19},{19,3},{4,20},{20... | collective-permute-start | bytes 1572872 | tf_op jit(solution)/shard_map/ppermute | solution.py:356
  2.0 1.1 %collective-permute-done.other = f32[32,16,256]{2,1,0:T(8,128)S(1)} collective-permute-done((f32[32,16,256]{2,1,0:T(8,128)}, f32[32,16,256]{2,1,0:T(8,128)S(1)}, u32[]{:S(2)}, u32[]{:S(2)}) %collective-permute-start) | collective-permute-done | bytes 524320 | tf_op jit(solution)/shard_map/ppermute | solution.py:356
  3.1 0.0 copy-start
  3.1 0.8 %copy-done = f32[32,16,256]{2,1,0:T(8,128)} copy-done((f32[32,16,256]{2,1,0:T(8,128)}, f32[32,16,256]{2,1,0:T(8,128)S(1)}, u32[]{:S(2)}) %copy-start) | copy-done | bytes 524312
  3.9 2.9 %shard_map.59 = (f32[2,552,128]{2,1,0:T(8,128)}, f32[2,1096,128]{2,1,0:T(8,128)}, f32[2,168,128]{2,1,0:T(8,128)}, f32[2,168,128]{2,1,0:T(8,128)}) custom-call(s32[1]{0:T(128)} %bitcast.where_ref, s32[1,1]{1,0:T(1,128)S(6)} %copy.8.code, f32[32,16,256]{2,1,0:T(8,128)} %bitcast.5, f32[32,16,256]{2,1,0:T(8,128)} %copy-done, f32[32,16,256]{2,1,0:T(8,128)} %mixing.3), custom_call_target="tpu_custom_call" | custom-call | tf_op jit(solution)/shard_map/pallas_call | solution.py:358
  6.8 3.4 %collective-permute-start.2 = (f32[2,1096,128]{2,1,0:T(8,128)}, f32[2,1096,128]{2,1,0:T(8,128)S(1)}, u32[]{:S(2)}, u32[]{:S(2)}) collective-permute-start(f32[2,1096,128]{2,1,0:T(8,128)} %get-tuple-element.14), channel_id=1, source_target_pairs={{1,16},{16,1},{2,17},{17,2},{3,18},{18,3},{5,20},{20,5},{6,21},{21... | collective-permute-start | bytes 3366920 | tf_op jit(solution)/shard_map/ppermute | solution.py:365
  10.3 2.0 %collective-permute-start.1 = (f32[2,552,128]{2,1,0:T(8,128)}, f32[2,552,128]{2,1,0:T(8,128)S(1)}, u32[]{:S(2)}, u32[]{:S(2)}) collective-permute-start(f32[2,552,128]{2,1,0:T(8,128)} %get-tuple-element.13), channel_id=1, source_target_pairs={{4,16},{16,4},{5,17},{17,5},{6,18},{18,6},{7,19},{19,7},{8,20},{20... | collective-permute-start | bytes 1695752 | tf_op jit(solution)/shard_map/ppermute | solution.py:364
  12.3 2.9 %collective-permute-start.3 = (f32[2,168,128]{2,1,0:T(8,128)}, f32[2,168,128]{2,1,0:T(8,128)S(1)}, u32[]{:S(2)}, u32[]{:S(2)}) collective-permute-start(f32[2,168,128]{2,1,0:T(8,128)} %get-tuple-element.15), channel_id=1, source_target_pairs={{5,16},{16,5},{6,17},{17,6},{7,18},{18,7},{9,20},{20,9},{10,21},{2... | collective-permute-start | bytes 516104 | tf_op jit(solution)/shard_map/ppermute | solution.py:366
  15.2 3.3 %collective-permute-start.4 = (f32[2,168,128]{2,1,0:T(8,128)}, f32[2,168,128]{2,1,0:T(8,128)S(1)}, u32[]{:S(2)}, u32[]{:S(2)}) collective-permute-start(f32[2,168,128]{2,1,0:T(8,128)} %get-tuple-element.16), channel_id=1, source_target_pairs={{4,17},{17,4},{5,18},{18,5},{6,19},{19,6},{8,21},{21,8},{9,22},{22... | collective-permute-start | bytes 516104 | tf_op jit(solution)/shard_map/ppermute | solution.py:367
  18.6 11.6 %collective-permute-done.3.corner_1 = f32[2,168,128]{2,1,0:T(8,128)S(1)} collective-permute-done((f32[2,168,128]{2,1,0:T(8,128)}, f32[2,168,128]{2,1,0:T(8,128)S(1)}, u32[]{:S(2)}, u32[]{:S(2)}) %collective-permute-start.3) | collective-permute-done | bytes 172064 | tf_op jit(solution)/shard_map/ppermute | solution.py:366
  30.2 0.0 copy-start.4
  30.2 0.0 collective-permute-done.4.corner_2
  30.2 0.0 copy-start.5
  30.2 4.0 %collective-permute-done.1.halo_x = f32[2,552,128]{2,1,0:T(8,128)S(1)} collective-permute-done((f32[2,552,128]{2,1,0:T(8,128)}, f32[2,552,128]{2,1,0:T(8,128)S(1)}, u32[]{:S(2)}, u32[]{:S(2)}) %collective-permute-start.1) | collective-permute-done | bytes 565280 | tf_op jit(solution)/shard_map/ppermute | solution.py:364
  34.1 0.0 copy-start.3
  34.1 0.0 collective-permute-done.2.halo_y
  34.1 0.0 copy-start.1
  34.1 0.1 collective-permute-start.5
  34.2 2.8 %collective-permute-done.5.passed_y = f32[2,1096,128]{2,1,0:T(8,128)S(1)} collective-permute-done((f32[2,1096,128]{2,1,0:T(8,128)S(1)}, f32[2,1096,128]{2,1,0:T(8,128)S(1)}, u32[]{:S(2)}, u32[]{:S(2)}) %collective-permute-start.5) | collective-permute-done | bytes 1122336 | tf_op jit(solution)/shard_map/ppermute | solution.py:369
  37.0 0.0 copy-done.4
  37.0 0.0 copy-done.5
  37.0 0.0 copy-done.3
  37.0 0.0 copy-done.1
  37.0 0.0 copy-start.2
  37.0 1.0 %copy-done.2 = f32[2,1096,128]{2,1,0:T(8,128)} copy-done((f32[2,1096,128]{2,1,0:T(8,128)}, f32[2,1096,128]{2,1,0:T(8,128)S(1)}, u32[]{:S(2)}) %copy-start.2) | copy-done | bytes 1122328
  38.0 17.7 %shard_map.60 = (f32[32,16,256]{2,1,0:T(8,128)}, f32[32,16,256]{2,1,0:T(8,128)}, f32[2,16,16,256]{3,2,1,0:T(8,128)}) custom-call(s32[1]{0:T(128)} %bitcast.where_ref, s32[1,1]{1,0:T(1,128)S(6)} %copy.8.code, f32[2,256]{1,0:T(2,128)} %wind.1, f32[32,16,256]{2,1,0:T(8,128)} %bitcast.6, f32[32,16,256]{2,1,0:T(8,128)} %copy-done, f32[32,16,256]{2,1,0:T(8,128)} %mixing.3, ...), custom_call_target="tpu_custom_call" | custom-call | tf_op jit(solution)/shard_map/pallas_call | solution.py:372
  55.7 0.1 collective-permute-start.6
  55.8 2.0 %collective-permute-done.6 = f32[2,16,16,256]{3,2,1,0:T(8,128)S(1)} collective-permute-done((f32[2,16,16,256]{3,2,1,0:T(8,128)}, f32[2,16,16,256]{3,2,1,0:T(8,128)S(1)}, u32[]{:S(2)}, u32[]{:S(2)}) %collective-permute-start.6) | collective-permute-done | bytes 524320 | tf_op jit(solution)/shard_map/ppermute | solution.py:380
  57.8 0.8 %slice_dynamic-update-slice_fusion = (f32[1,32,16,256]{3,2,1,0:T(8,128)}, f32[1,32,16,256]{3,2,1,0:T(8,128)}) fusion(f32[1,32,16,256]{3,2,1,0:T(8,128)} %bitcast.8, s32[]{:T(128)S(6)} %select_n.4, f32[2,16,16,256]{3,2,1,0:T(8,128)S(1)} %collective-permute-done.6, f32[1,32,16,256]{3,2,1,0:T(8,128)} %bitcast.7), kind=kLoop, calls=%fused_computation | loop fusion | bytes 1048580 | tf_op jit(solution)/shard_map/dynamic_update_slice | solution.py:382
Async XLA Ops:
  0.6 2.5 %collective-permute-start = (f32[32,16,256]{2,1,0:T(8,128)}, f32[32,16,256]{2,1,0:T(8,128)S(1)}, u32[]{:S(2)}, u32[]{:S(2)}) collective-permute-start(f32[32,16,256]{2,1,0:T(8,128)} %bitcast.4), channel_id=1, source_target_pairs={{0,16},{16,0},{1,17},{17,1},{2,18},{18,2},{3,19},{19,3},{4,20},{20... | collective-permute-start | bytes 1572872 | tf_op jit(solution)/shard_map/ppermute | solution.py:356
  3.1 0.8 %copy-start = (f32[32,16,256]{2,1,0:T(8,128)}, f32[32,16,256]{2,1,0:T(8,128)S(1)}, u32[]{:S(2)}) copy-start(f32[32,16,256]{2,1,0:T(8,128)S(1)} %collective-permute-done.other) | copy-start | bytes 1572868
  6.8 27.3 %collective-permute-start.2 = (f32[2,1096,128]{2,1,0:T(8,128)}, f32[2,1096,128]{2,1,0:T(8,128)S(1)}, u32[]{:S(2)}, u32[]{:S(2)}) collective-permute-start(f32[2,1096,128]{2,1,0:T(8,128)} %get-tuple-element.14), channel_id=1, source_target_pairs={{1,16},{16,1},{2,17},{17,2},{3,18},{18,3},{5,20},{20,5},{6,21},{21... | collective-permute-start | bytes 3366920 | tf_op jit(solution)/shard_map/ppermute | solution.py:365
  10.3 23.9 %collective-permute-start.1 = (f32[2,552,128]{2,1,0:T(8,128)}, f32[2,552,128]{2,1,0:T(8,128)S(1)}, u32[]{:S(2)}, u32[]{:S(2)}) collective-permute-start(f32[2,552,128]{2,1,0:T(8,128)} %get-tuple-element.13), channel_id=1, source_target_pairs={{4,16},{16,4},{5,17},{17,5},{6,18},{18,6},{7,19},{19,7},{8,20},{20... | collective-permute-start | bytes 1695752 | tf_op jit(solution)/shard_map/ppermute | solution.py:364
  12.3 17.9 %collective-permute-start.3 = (f32[2,168,128]{2,1,0:T(8,128)}, f32[2,168,128]{2,1,0:T(8,128)S(1)}, u32[]{:S(2)}, u32[]{:S(2)}) collective-permute-start(f32[2,168,128]{2,1,0:T(8,128)} %get-tuple-element.15), channel_id=1, source_target_pairs={{5,16},{16,5},{6,17},{17,6},{7,18},{18,7},{9,20},{20,9},{10,21},{2... | collective-permute-start | bytes 516104 | tf_op jit(solution)/shard_map/ppermute | solution.py:366
  15.2 14.9 %collective-permute-start.4 = (f32[2,168,128]{2,1,0:T(8,128)}, f32[2,168,128]{2,1,0:T(8,128)S(1)}, u32[]{:S(2)}, u32[]{:S(2)}) collective-permute-start(f32[2,168,128]{2,1,0:T(8,128)} %get-tuple-element.16), channel_id=1, source_target_pairs={{4,17},{17,4},{5,18},{18,5},{6,19},{19,6},{8,21},{21,8},{9,22},{22... | collective-permute-start | bytes 516104 | tf_op jit(solution)/shard_map/ppermute | solution.py:367
  30.2 6.8 %copy-start.4 = (f32[2,168,128]{2,1,0:T(8,128)}, f32[2,168,128]{2,1,0:T(8,128)S(1)}, u32[]{:S(2)}) copy-start(f32[2,168,128]{2,1,0:T(8,128)S(1)} %collective-permute-done.3.corner_1) | copy-start | bytes 516100
  30.2 6.8 %copy-start.5 = (f32[2,168,128]{2,1,0:T(8,128)}, f32[2,168,128]{2,1,0:T(8,128)S(1)}, u32[]{:S(2)}) copy-start(f32[2,168,128]{2,1,0:T(8,128)S(1)} %collective-permute-done.4.corner_2) | copy-start | bytes 516100
  34.1 2.8 %copy-start.3 = (f32[2,552,128]{2,1,0:T(8,128)}, f32[2,552,128]{2,1,0:T(8,128)S(1)}, u32[]{:S(2)}) copy-start(f32[2,552,128]{2,1,0:T(8,128)S(1)} %collective-permute-done.1.halo_x) | copy-start | bytes 1695748
  34.1 2.8 %copy-start.1 = (f32[2,1096,128]{2,1,0:T(8,128)}, f32[2,1096,128]{2,1,0:T(8,128)S(1)}, u32[]{:S(2)}) copy-start(f32[2,1096,128]{2,1,0:T(8,128)S(1)} %collective-permute-done.2.halo_y) | copy-start | bytes 3366916
  34.1 2.8 %collective-permute-start.5 = (f32[2,1096,128]{2,1,0:T(8,128)S(1)}, f32[2,1096,128]{2,1,0:T(8,128)S(1)}, u32[]{:S(2)}, u32[]{:S(2)}) collective-permute-start(f32[2,1096,128]{2,1,0:T(8,128)S(1)} %collective-permute-done.2.halo_y), channel_id=1, source_target_pairs={{0,16},{16,0},{1,17},{17,1},{2,18},{18,2},{3,19},{19,3},{4,20},{20... | collective-permute-start | bytes 3366920 | tf_op jit(solution)/shard_map/ppermute | solution.py:369
  37.0 1.0 %copy-start.2 = (f32[2,1096,128]{2,1,0:T(8,128)}, f32[2,1096,128]{2,1,0:T(8,128)S(1)}, u32[]{:S(2)}) copy-start(f32[2,1096,128]{2,1,0:T(8,128)S(1)} %collective-permute-done.5.passed_y) | copy-start | bytes 3366916
  55.7 2.1 %collective-permute-start.6 = (f32[2,16,16,256]{3,2,1,0:T(8,128)}, f32[2,16,16,256]{3,2,1,0:T(8,128)S(1)}, u32[]{:S(2)}, u32[]{:S(2)}) collective-permute-start(f32[2,16,16,256]{3,2,1,0:T(8,128)} %get-tuple-element.22), channel_id=1, source_target_pairs={{0,16},{16,0},{1,17},{17,1},{2,18},{18,2},{3,19},{19,3},{4,20},{20... | collective-permute-start | bytes 1572872 | tf_op jit(solution)/shard_map/ppermute | solution.py:380

commit v3 on v2

--- a/solution.py
+++ b/solution.py
@@ -335,6 +335,10 @@
     return jax.ShapeDtypeStruct(shape, jnp.float32)
 
 
+def near(x):
+    return pltpu.with_memory_space_constraint(x, pltpu.VMEM)
+
+
 def pair_shards(state, code, wind, mixing, sizes):
     axes = ("tm", "gx", "gy")
     rows, columns, levels = state.shape
@@ -353,11 +357,12 @@
         return pairs
 
     swap = [(0, 1), (1, 0)]
-    other = lax.ppermute(state, "tm", swap)
-    corner = of(halves, CORNER_SIZE + TILE, LANES)
+    other = near(lax.ppermute(state, "tm", swap))
+    corner = (halves, CORNER_SIZE + TILE, LANES)
     to_x, to_y, to_1, to_2 = pl.pallas_call(
         pack_kernel,
-        out_shape=(of(halves, BEFORE[-1] * columns + TILE, LANES), of(halves, BEFORE[-1] * rows + TILE, LANES), corner, corner),
+        out_shape=[pltpu.VMEM(s, jnp.float32) for s in (
+            (halves, BEFORE[-1] * columns + TILE, LANES), (halves, BEFORE[-1] * rows + TILE, LANES), corner, corner)],
         in_specs=[SMEM, SMEM, VMEM, VMEM, VMEM], out_specs=[VMEM] * 4,
         compiler_params=pltpu.CompilerParams(vmem_limit_bytes=LIMIT),
     )(where, code, state, other, mixing)
@@ -367,10 +372,11 @@
     corner_2 = lax.ppermute(to_2, axes, partners(1, -1))
     halo_x, halo_y, corner_1, corner_2 = lax.optimization_barrier((halo_x, halo_y, corner_1, corner_2))
     passed_y = lax.ppermute(halo_y, "tm", swap)
+    halo_x, halo_y, passed_y, corner_1, corner_2 = map(near, (halo_x, halo_y, passed_y, corner_1, corner_2))
     half = rows // 2
     plane = (halves, half + 2 * HALO, columns + 2 * HALO + TILE, LANES)
     middle, final, theirs = pl.pallas_call(
-        pair_kernel, out_shape=(of(*state.shape), of(*state.shape), of(2, half, columns, levels)),
+        pair_kernel, out_shape=(of(*state.shape), of(*state.shape), pltpu.VMEM((2, half, columns, levels), jnp.float32)),
         in_specs=[SMEM, SMEM] + [VMEM] * 9, out_specs=[VMEM] * 3,
         scratch_shapes=[pltpu.VMEM((2, *plane), jnp.float32)] * 11 + [
             pltpu.VMEM(plane, jnp.float32), pltpu.VMEM((2, 2, half, columns, levels), jnp.float32),

time: 58.9 us -> 53.9 us (0.915)
  Pallas kernels: 20.6 us -> 17.9 us
  local copies, waits for them, and re-layouts: 2.64 us -> 0.82 us
    unnamed x12 -> x0, local copies, waits for them, and re-layouts: 1.82 us -> none
    pallas_call x1, Pallas kernels: 2.89 us -> 1.44 us  [pair_shards(): pl.pallas_call(pack_kernel, out_shape=[pltpu.VMEM(s, jnp.float32) for s i...]
    pallas_call x1, Pallas kernels: 17.7 us -> 16.4 us  [pair_shards(): pl.pallas_call(pair_kernel, out_shape=(of(*state.shape), of(*state.shape)...]
where the time goes in v3:
time: 53.9 us; the launch traced here: 53.6 us
  waiting for transfers between devices  21 us (39%)
  Pallas kernels  17.9 us (33%)
  starting transfers between devices  12.6 us (23%)
  between operations  1.33 us (2%)
  local copies, waits for them, and re-layouts  0.82 us (2%)
    pallas_call x1, Pallas kernels, pair_shards(): pl.pallas_call(pair_kernel, out_shape=(of(*state.shape), of(*state.shape)...  16.4 us
    ppermute x1, waiting for transfers between devices, pair_shards(): corner_1 = lax.ppermute(to_1, axes, partners(1, 1))  11.4 us
    ppermute x1, waiting for transfers between devices, pair_shards(): halo_x = lax.ppermute(to_x, axes, partners(1, 0))  3.95 us
    ppermute x1, starting transfers between devices, pair_shards(): halo_y = lax.ppermute(to_y, axes, partners(0, 1))  3.47 us
    ppermute x1, starting transfers between devices, pair_shards(): corner_2 = lax.ppermute(to_2, axes, partners(1, -1))  3.33 us
    ppermute x1, starting transfers between devices, pair_shards(): corner_1 = lax.ppermute(to_1, axes, partners(1, 1))  2.93 us
    ppermute x1, waiting for transfers between devices, pair_shards(): passed_y = lax.ppermute(halo_y, 'tm', swap)  2.76 us
    ppermute x1, starting transfers between devices, pair_shards(): halo_x = lax.ppermute(to_x, axes, partners(1, 0))  2 us
  transfers between devices with their start and end apart: 7, of which 5 were waited for; matrix products, arithmetic and copies ran while one was open for 0% of the time, Pallas kernels for 0%

profile of v3, /device:TPU:19, one launch (start us, length us, event | category | flops | bytes accessed | tf_op | source)
XLA Modules:
  0.0 53.6 jit_solution(286170530228292357)
XLA Ops:
  0.6 0.7 %collective-permute-start = (f32[32,16,256]{2,1,0:T(8,128)}, f32[32,16,256]{2,1,0:T(8,128)S(1)}, u32[]{:S(2)}, u32[]{:S(2)}) collective-permute-start(f32[32,16,256]{2,1,0:T(8,128)} %bitcast.4), channel_id=1, source_target_pairs={{0,16},{16,0},{1,17},{17,1},{2,18},{18,2},{3,19},{19,3},{4,20},{20... | collective-permute-start | bytes 1572872 | tf_op jit(solution)/shard_map/ppermute | solution.py:360
  2.0 1.1 %collective-permute-done.other = f32[32,16,256]{2,1,0:T(8,128)S(1)} collective-permute-done((f32[32,16,256]{2,1,0:T(8,128)}, f32[32,16,256]{2,1,0:T(8,128)S(1)}, u32[]{:S(2)}, u32[]{:S(2)}) %collective-permute-start) | collective-permute-done | bytes 524320 | tf_op jit(solution)/shard_map/ppermute | solution.py:360
  3.1 1.4 %shard_map.59 = (f32[2,552,128]{2,1,0:T(8,128)S(1)}, f32[2,1096,128]{2,1,0:T(8,128)S(1)}, f32[2,168,128]{2,1,0:T(8,128)S(1)}, f32[2,168,128]{2,1,0:T(8,128)S(1)}) custom-call(s32[1]{0:T(128)} %bitcast.where_ref, s32[1,1]{1,0:T(1,128)S(6)} %copy.8.code, f32[32,16,256]{2,1,0:T(8,128)} %bitcast.5, f32[32,16,256]{2,1,0:T(8,128)S(1)} %collective-permute-done.other, ...), custom_call_target="tpu_custom_call" | custom-call | tf_op jit(solution)/shard_map/pallas_call | solution.py:362
  4.6 3.5 %collective-permute-start.2 = (f32[2,1096,128]{2,1,0:T(8,128)S(1)}, f32[2,1096,128]{2,1,0:T(8,128)S(1)}, u32[]{:S(2)}, u32[]{:S(2)}) collective-permute-start(f32[2,1096,128]{2,1,0:T(8,128)S(1)} %get-tuple-element.14), channel_id=1, source_target_pairs={{1,16},{16,1},{2,17},{17,2},{3,18},{18,3},{5,20},{20,5},{6,21},{21... | collective-permute-start | bytes 3366920 | tf_op jit(solution)/shard_map/ppermute | solution.py:370
  8.1 2.0 %collective-permute-start.1 = (f32[2,552,128]{2,1,0:T(8,128)S(1)}, f32[2,552,128]{2,1,0:T(8,128)S(1)}, u32[]{:S(2)}, u32[]{:S(2)}) collective-permute-start(f32[2,552,128]{2,1,0:T(8,128)S(1)} %get-tuple-element.13), channel_id=1, source_target_pairs={{4,16},{16,4},{5,17},{17,5},{6,18},{18,6},{7,19},{19,7},{8,20},{20... | collective-permute-start | bytes 1695752 | tf_op jit(solution)/shard_map/ppermute | solution.py:369
  10.1 2.9 %collective-permute-start.3 = (f32[2,168,128]{2,1,0:T(8,128)S(1)}, f32[2,168,128]{2,1,0:T(8,128)S(1)}, u32[]{:S(2)}, u32[]{:S(2)}) collective-permute-start(f32[2,168,128]{2,1,0:T(8,128)S(1)} %get-tuple-element.15), channel_id=1, source_target_pairs={{5,16},{16,5},{6,17},{17,6},{7,18},{18,7},{9,20},{20,9},{10,21},{2... | collective-permute-start | bytes 516104 | tf_op jit(solution)/shard_map/ppermute | solution.py:371
  13.0 3.3 %collective-permute-start.4 = (f32[2,168,128]{2,1,0:T(8,128)S(1)}, f32[2,168,128]{2,1,0:T(8,128)S(1)}, u32[]{:S(2)}, u32[]{:S(2)}) collective-permute-start(f32[2,168,128]{2,1,0:T(8,128)S(1)} %get-tuple-element.16), channel_id=1, source_target_pairs={{4,17},{17,4},{5,18},{18,5},{6,19},{19,6},{8,21},{21,8},{9,22},{22... | collective-permute-start | bytes 516104 | tf_op jit(solution)/shard_map/ppermute | solution.py:372
  16.3 11.4 %collective-permute-done.3.corner_1 = f32[2,168,128]{2,1,0:T(8,128)S(1)} collective-permute-done((f32[2,168,128]{2,1,0:T(8,128)S(1)}, f32[2,168,128]{2,1,0:T(8,128)S(1)}, u32[]{:S(2)}, u32[]{:S(2)}) %collective-permute-start.3) | collective-permute-done | bytes 172064 | tf_op jit(solution)/shard_map/ppermute | solution.py:371
  27.7 0.0 collective-permute-done.4.corner_2
  27.7 4.0 %collective-permute-done.1.halo_x = f32[2,552,128]{2,1,0:T(8,128)S(1)} collective-permute-done((f32[2,552,128]{2,1,0:T(8,128)S(1)}, f32[2,552,128]{2,1,0:T(8,128)S(1)}, u32[]{:S(2)}, u32[]{:S(2)}) %collective-permute-start.1) | collective-permute-done | bytes 565280 | tf_op jit(solution)/shard_map/ppermute | solution.py:369
  31.7 0.0 collective-permute-done.2.halo_y
  31.7 0.0 collective-permute-start.5
  31.7 2.8 %collective-permute-done.5.passed_y = f32[2,1096,128]{2,1,0:T(8,128)S(1)} collective-permute-done((f32[2,1096,128]{2,1,0:T(8,128)S(1)}, f32[2,1096,128]{2,1,0:T(8,128)S(1)}, u32[]{:S(2)}, u32[]{:S(2)}) %collective-permute-start.5) | collective-permute-done | bytes 1122336 | tf_op jit(solution)/shard_map/ppermute | solution.py:374
  34.5 16.4 %shard_map.60 = (f32[32,16,256]{2,1,0:T(8,128)}, f32[32,16,256]{2,1,0:T(8,128)}, f32[2,16,16,256]{3,2,1,0:T(8,128)S(1)}) custom-call(s32[1]{0:T(128)} %bitcast.where_ref, s32[1,1]{1,0:T(1,128)S(6)} %copy.8.code, f32[2,256]{1,0:T(2,128)} %wind.1, f32[32,16,256]{2,1,0:T(8,128)} %bitcast.6, f32[32,16,256]{2,1,0:T(8,128)S(1)} %collective-permute-done.other, ...), custom_call_target="tpu_custom_call" | custom-call | tf_op jit(solution)/shard_map/pallas_call | solution.py:378
  50.9 0.1 collective-permute-start.6
  51.0 1.8 %collective-permute-done.6 = f32[2,16,16,256]{3,2,1,0:T(8,128)S(1)} collective-permute-done((f32[2,16,16,256]{3,2,1,0:T(8,128)S(1)}, f32[2,16,16,256]{3,2,1,0:T(8,128)S(1)}, u32[]{:S(2)}, u32[]{:S(2)}) %collective-permute-start.6) | collective-permute-done | bytes 524320 | tf_op jit(solution)/shard_map/ppermute | solution.py:386
  52.8 0.8 %slice_dynamic-update-slice_fusion = (f32[1,32,16,256]{3,2,1,0:T(8,128)}, f32[1,32,16,256]{3,2,1,0:T(8,128)}) fusion(f32[1,32,16,256]{3,2,1,0:T(8,128)} %bitcast.8, s32[]{:T(128)S(6)} %select_n.4, f32[2,16,16,256]{3,2,1,0:T(8,128)S(1)} %collective-permute-done.6, f32[1,32,16,256]{3,2,1,0:T(8,128)} %bitcast.7), kind=kLoop, calls=%fused_computation | loop fusion | bytes 1048580 | tf_op jit(solution)/shard_map/dynamic_update_slice | solution.py:388
Async XLA Ops:
  0.6 2.5 %collective-permute-start = (f32[32,16,256]{2,1,0:T(8,128)}, f32[32,16,256]{2,1,0:T(8,128)S(1)}, u32[]{:S(2)}, u32[]{:S(2)}) collective-permute-start(f32[32,16,256]{2,1,0:T(8,128)} %bitcast.4), channel_id=1, source_target_pairs={{0,16},{16,0},{1,17},{17,1},{2,18},{18,2},{3,19},{19,3},{4,20},{20... | collective-permute-start | bytes 1572872 | tf_op jit(solution)/shard_map/ppermute | solution.py:360
  4.6 27.1 %collective-permute-start.2 = (f32[2,1096,128]{2,1,0:T(8,128)S(1)}, f32[2,1096,128]{2,1,0:T(8,128)S(1)}, u32[]{:S(2)}, u32[]{:S(2)}) collective-permute-start(f32[2,1096,128]{2,1,0:T(8,128)S(1)} %get-tuple-element.14), channel_id=1, source_target_pairs={{1,16},{16,1},{2,17},{17,2},{3,18},{18,3},{5,20},{20,5},{6,21},{21... | collective-permute-start | bytes 3366920 | tf_op jit(solution)/shard_map/ppermute | solution.py:370
  8.1 23.6 %collective-permute-start.1 = (f32[2,552,128]{2,1,0:T(8,128)S(1)}, f32[2,552,128]{2,1,0:T(8,128)S(1)}, u32[]{:S(2)}, u32[]{:S(2)}) collective-permute-start(f32[2,552,128]{2,1,0:T(8,128)S(1)} %get-tuple-element.13), channel_id=1, source_target_pairs={{4,16},{16,4},{5,17},{17,5},{6,18},{18,6},{7,19},{19,7},{8,20},{20... | collective-permute-start | bytes 1695752 | tf_op jit(solution)/shard_map/ppermute | solution.py:369
  10.1 17.7 %collective-permute-start.3 = (f32[2,168,128]{2,1,0:T(8,128)S(1)}, f32[2,168,128]{2,1,0:T(8,128)S(1)}, u32[]{:S(2)}, u32[]{:S(2)}) collective-permute-start(f32[2,168,128]{2,1,0:T(8,128)S(1)} %get-tuple-element.15), channel_id=1, source_target_pairs={{5,16},{16,5},{6,17},{17,6},{7,18},{18,7},{9,20},{20,9},{10,21},{2... | collective-permute-start | bytes 516104 | tf_op jit(solution)/shard_map/ppermute | solution.py:371
  13.0 14.7 %collective-permute-start.4 = (f32[2,168,128]{2,1,0:T(8,128)S(1)}, f32[2,168,128]{2,1,0:T(8,128)S(1)}, u32[]{:S(2)}, u32[]{:S(2)}) collective-permute-start(f32[2,168,128]{2,1,0:T(8,128)S(1)} %get-tuple-element.16), channel_id=1, source_target_pairs={{4,17},{17,4},{5,18},{18,5},{6,19},{19,6},{8,21},{21,8},{9,22},{22... | collective-permute-start | bytes 516104 | tf_op jit(solution)/shard_map/ppermute | solution.py:372
  31.7 2.8 %collective-permute-start.5 = (f32[2,1096,128]{2,1,0:T(8,128)S(1)}, f32[2,1096,128]{2,1,0:T(8,128)S(1)}, u32[]{:S(2)}, u32[]{:S(2)}) collective-permute-start(f32[2,1096,128]{2,1,0:T(8,128)S(1)} %collective-permute-done.2.halo_y), channel_id=1, source_target_pairs={{0,16},{16,0},{1,17},{17,1},{2,18},{18,2},{3,19},{19,3},{4,20},{20... | collective-permute-start | bytes 3366920 | tf_op jit(solution)/shard_map/ppermute | solution.py:374
  50.9 1.9 %collective-permute-start.6 = (f32[2,16,16,256]{3,2,1,0:T(8,128)S(1)}, f32[2,16,16,256]{3,2,1,0:T(8,128)S(1)}, u32[]{:S(2)}, u32[]{:S(2)}) collective-permute-start(f32[2,16,16,256]{3,2,1,0:T(8,128)S(1)} %get-tuple-element.22), channel_id=1, source_target_pairs={{0,16},{16,0},{1,17},{17,1},{2,18},{18,2},{3,19},{19,3},{4,20},{20... | collective-permute-start | bytes 1572872 | tf_op jit(solution)/shard_map/ppermute | solution.py:386

commit v4 on v3

--- a/solution.py
+++ b/solution.py
@@ -210,6 +210,15 @@
 BEFORE = tuple(sum(DEPTHS[:a]) for a in range(len(DEPTHS) + 1))
 
 
+def load_kernel(state, mixing, state_near, mixing_near, semaphores):
+    made = [pltpu.make_async_copy(a, b, semaphores.at[k])
+            for k, (a, b) in enumerate(((state, state_near), (mixing, mixing_near)))]
+    for one in made:
+        one.start()
+    for one in made:
+        one.wait()
+
+
 def pack_kernel(where_ref, code, own, other, mixing, beside_x, beside_y, diagonal_1, diagonal_2):
     t = where_ref[0]
     rows, columns, levels = own.shape
@@ -244,7 +253,7 @@
 
 
 def pair_kernel(where_ref, code, wind, own, other, mixing, halo_x, halo_y, passed_y, corner_1, corner_2,
-                mine_middle, mine_final, theirs, start, mid, last_1, last_2, f, g1, g1b, g2, g2b, act_a, act_b,
+                mine, theirs, start, mid, last_1, last_2, f, g1, g1b, g2, g2b, act_a, act_b,
                 mix, both, codes):
     t = where_ref[0]
     block_rows, columns, levels = own.shape
@@ -320,14 +329,30 @@
             ref[n, z, x, pl.ds(y, TILE), :] = value
 
     sweeps(half, columns, codes, wind, mix, start, mid, last_1, last_2, f, g1, g1b, g2, g2b, act_a, act_b, write)
-    here = pl.ds(t * half, half)
-    mine_middle[here] = both[0, 0]
-    mine_final[here] = both[0, 1]
+    mine[...] = both[0]
     theirs[...] = both[1]
+
+
+def merge_kernel(where_ref, mine, got, middle, final, semaphores):
+    t = where_ref[0]
+    half = mine.shape[1]
+
+    def merge(low):
+        halves = (mine, got) if low else (got, mine)
+        made = [pltpu.make_async_copy(part.at[k], out.at[pl.ds(h * half, half)], semaphores.at[2 * h + k])
+                for h, part in enumerate(halves) for k, out in enumerate((middle, final))]
+        for one in made:
+            one.start()
+        for one in made:
+            one.wait()
+
+    pl.when(t == 0)(lambda: merge(True))
+    pl.when(t != 0)(lambda: merge(False))
 
 
 VMEM = pl.BlockSpec(memory_space=pltpu.VMEM)
 SMEM = pl.BlockSpec(memory_space=pltpu.SMEM)
+ANY = pl.BlockSpec(memory_space=pl.ANY)
 LIMIT = 56 * 2**20
 
 
@@ -358,6 +383,12 @@
 
     swap = [(0, 1), (1, 0)]
     other = near(lax.ppermute(state, "tm", swap))
+    state, mixing = pl.pallas_call(
+        load_kernel, out_shape=[pltpu.VMEM(x.shape, jnp.float32) for x in (state, mixing)],
+        in_specs=[ANY] * 2, out_specs=[VMEM] * 2, scratch_shapes=[pltpu.SemaphoreType.DMA((2,))],
+        cost_estimate=pl.CostEstimate(flops=0, bytes_accessed=16 * state.size, transcendentals=0),
+    )(state, mixing)
+    state, mixing = near(state), near(mixing)
     corner = (halves, CORNER_SIZE + TILE, LANES)
     to_x, to_y, to_1, to_2 = pl.pallas_call(
         pack_kernel,
@@ -375,17 +406,20 @@
     halo_x, halo_y, passed_y, corner_1, corner_2 = map(near, (halo_x, halo_y, passed_y, corner_1, corner_2))
     half = rows // 2
     plane = (halves, half + 2 * HALO, columns + 2 * HALO + TILE, LANES)
-    middle, final, theirs = pl.pallas_call(
-        pair_kernel, out_shape=(of(*state.shape), of(*state.shape), pltpu.VMEM((2, half, columns, levels), jnp.float32)),
-        in_specs=[SMEM, SMEM] + [VMEM] * 9, out_specs=[VMEM] * 3,
+    mine, theirs = pl.pallas_call(
+        pair_kernel, out_shape=[pltpu.VMEM((2, half, columns, levels), jnp.float32)] * 2,
+        in_specs=[SMEM, SMEM] + [VMEM] * 9, out_specs=[VMEM] * 2,
         scratch_shapes=[pltpu.VMEM((2, *plane), jnp.float32)] * 11 + [
             pltpu.VMEM(plane, jnp.float32), pltpu.VMEM((2, 2, half, columns, levels), jnp.float32),
             pltpu.SMEM((3 * (half + 2 * HALO),), jnp.int32)],
         compiler_params=pltpu.CompilerParams(vmem_limit_bytes=LIMIT),
     )(where, code, wind, state, other, mixing, halo_x, halo_y, passed_y, corner_1, corner_2)
     got = lax.ppermute(theirs, "tm", swap)
-    there = ((1 - t) * half, 0, 0)
-    return lax.dynamic_update_slice(middle, got[0], there)[None], lax.dynamic_update_slice(final, got[1], there)[None]
+    middle, final = pl.pallas_call(
+        merge_kernel, out_shape=[of(*state.shape)] * 2, in_specs=[SMEM, VMEM, VMEM], out_specs=[ANY] * 2,
+        scratch_shapes=[pltpu.SemaphoreType.DMA((4,))],
+    )(where, near(mine), near(got))
+    return middle[None], final[None]
 
 
 def padded(x, sides, width):

time: 53.9 us -> 51.6 us (0.957)
  waiting for transfers between devices: 21 us -> 20.1 us
  local copies, waits for them, and re-layouts: 0.82 us -> 0 us
    pallas_call x1, Pallas kernels: 1.44 us -> 0.26 us  [pair_shards(): pl.pallas_call(pack_kernel, out_shape=[pltpu.VMEM(s, jnp.float32) for s i...]
    ppermute x1, waiting for transfers between devices: 1.1 us -> 0.01 us  [pair_shards(): other = near(lax.ppermute(state, 'tm', swap))]
    dynamic_update_slice x1 -> x0, local copies, waits for them, and re-layouts: 0.82 us -> none  [pair_shards(): lax.dynamic_update_slice(final, got[1], there)[None]]
    pallas_call x1 -> x3, Pallas kernels: 16.4 us -> 17.2 us  [the longest x1 15 us: pair_shards(): pl.pallas_call(pair_kernel, out_shape=[pltpu.VMEM((2, half, columns, leve...]
  transfers between devices with their start and end apart: 7 -> 7, of which waited for: 5 -> 4; matrix products, arithmetic and copies ran while one was open for 0% -> 0% of each run, Pallas kernels for 0% -> 2%
where the time goes in v4:
time: 51.6 us; the launch traced here: 51.4 us
  waiting for transfers between devices  20.1 us (39%)
  Pallas kernels  17.5 us (34%)
  starting transfers between devices  12.5 us (24%)
  between operations  1.35 us (3%)
    pallas_call x1, Pallas kernels, pair_shards(): pl.pallas_call(pair_kernel, out_shape=[pltpu.VMEM((2, half, columns, leve...  15 us
    ppermute x1, waiting for transfers between devices, pair_shards(): corner_1 = lax.ppermute(to_1, axes, partners(1, 1))  11.3 us
    ppermute x1, waiting for transfers between devices, pair_shards(): halo_x = lax.ppermute(to_x, axes, partners(1, 0))  4.23 us
    ppermute x1, starting transfers between devices, pair_shards(): halo_y = lax.ppermute(to_y, axes, partners(0, 1))  3.3 us
    ppermute x1, starting transfers between devices, pair_shards(): corner_2 = lax.ppermute(to_2, axes, partners(1, -1))  3.15 us
    ppermute x1, starting transfers between devices, pair_shards(): corner_1 = lax.ppermute(to_1, axes, partners(1, 1))  2.93 us
    ppermute x1, waiting for transfers between devices, pair_shards(): passed_y = lax.ppermute(halo_y, 'tm', swap)  2.76 us
    ppermute x1, starting transfers between devices, pair_shards(): halo_x = lax.ppermute(to_x, axes, partners(1, 0))  2.18 us
  transfers between devices with their start and end apart: 7, of which 4 were waited for; matrix products, arithmetic and copies ran while one was open for 0% of the time, Pallas kernels for 2%

profile of v4, /device:TPU:19, one launch (start us, length us, event | category | flops | bytes accessed | tf_op | source)
XLA Modules:
  0.0 51.4 jit_solution(16083191428420985135)
XLA Ops:
  0.6 0.7 %collective-permute-start = (f32[32,16,256]{2,1,0:T(8,128)}, f32[32,16,256]{2,1,0:T(8,128)S(1)}, u32[]{:S(2)}, u32[]{:S(2)}) collective-permute-start(f32[32,16,256]{2,1,0:T(8,128)} %bitcast.4), channel_id=1, source_target_pairs={{0,16},{16,0},{1,17},{17,1},{2,18},{18,2},{3,19},{19,3},{4,20},{20... | collective-permute-start | bytes 1572872 | tf_op jit(solution)/shard_map/ppermute | solution.py:385
  2.0 1.2 %shard_map.59 = (f32[32,16,256]{2,1,0:T(8,128)S(1)}, f32[32,16,256]{2,1,0:T(8,128)S(1)}) custom-call(f32[32,16,256]{2,1,0:T(8,128)} %bitcast.5, f32[32,16,256]{2,1,0:T(8,128)} %mixing.1), custom_call_target="tpu_custom_call" | custom-call | bytes 2097152 | tf_op jit(solution)/shard_map/pallas_call | solution.py:386
  3.2 0.0 collective-permute-done.other
  3.3 0.3 shard_map.60
  3.5 3.3 %collective-permute-start.2 = (f32[2,1096,128]{2,1,0:T(8,128)S(1)}, f32[2,1096,128]{2,1,0:T(8,128)S(1)}, u32[]{:S(2)}, u32[]{:S(2)}) collective-permute-start(f32[2,1096,128]{2,1,0:T(8,128)S(1)} %get-tuple-element.19), channel_id=1, source_target_pairs={{1,16},{16,1},{2,17},{17,2},{3,18},{18,3},{5,20},{20,5},{6,21},{21... | collective-permute-start | bytes 3366920 | tf_op jit(solution)/shard_map/ppermute | solution.py:401
  6.8 2.2 %collective-permute-start.1 = (f32[2,552,128]{2,1,0:T(8,128)S(1)}, f32[2,552,128]{2,1,0:T(8,128)S(1)}, u32[]{:S(2)}, u32[]{:S(2)}) collective-permute-start(f32[2,552,128]{2,1,0:T(8,128)S(1)} %get-tuple-element.18), channel_id=1, source_target_pairs={{4,16},{16,4},{5,17},{17,5},{6,18},{18,6},{7,19},{19,7},{8,20},{20... | collective-permute-start | bytes 1695752 | tf_op jit(solution)/shard_map/ppermute | solution.py:400
  9.0 2.9 %collective-permute-start.3 = (f32[2,168,128]{2,1,0:T(8,128)S(1)}, f32[2,168,128]{2,1,0:T(8,128)S(1)}, u32[]{:S(2)}, u32[]{:S(2)}) collective-permute-start(f32[2,168,128]{2,1,0:T(8,128)S(1)} %get-tuple-element.20), channel_id=1, source_target_pairs={{5,16},{16,5},{6,17},{17,6},{7,18},{18,7},{9,20},{20,9},{10,21},{2... | collective-permute-start | bytes 516104 | tf_op jit(solution)/shard_map/ppermute | solution.py:402
  12.0 3.2 %collective-permute-start.4 = (f32[2,168,128]{2,1,0:T(8,128)S(1)}, f32[2,168,128]{2,1,0:T(8,128)S(1)}, u32[]{:S(2)}, u32[]{:S(2)}) collective-permute-start(f32[2,168,128]{2,1,0:T(8,128)S(1)} %get-tuple-element.21), channel_id=1, source_target_pairs={{4,17},{17,4},{5,18},{18,5},{6,19},{19,6},{8,21},{21,8},{9,22},{22... | collective-permute-start | bytes 516104 | tf_op jit(solution)/shard_map/ppermute | solution.py:403
  15.1 11.3 %collective-permute-done.3.corner_1 = f32[2,168,128]{2,1,0:T(8,128)S(1)} collective-permute-done((f32[2,168,128]{2,1,0:T(8,128)S(1)}, f32[2,168,128]{2,1,0:T(8,128)S(1)}, u32[]{:S(2)}, u32[]{:S(2)}) %collective-permute-start.3) | collective-permute-done | bytes 172064 | tf_op jit(solution)/shard_map/ppermute | solution.py:402
  26.4 0.0 collective-permute-done.4.corner_2
  26.4 4.2 %collective-permute-done.1.halo_x = f32[2,552,128]{2,1,0:T(8,128)S(1)} collective-permute-done((f32[2,552,128]{2,1,0:T(8,128)S(1)}, f32[2,552,128]{2,1,0:T(8,128)S(1)}, u32[]{:S(2)}, u32[]{:S(2)}) %collective-permute-start.1) | collective-permute-done | bytes 565280 | tf_op jit(solution)/shard_map/ppermute | solution.py:400
  30.6 0.0 collective-permute-done.2.halo_y
  30.6 0.0 collective-permute-start.5
  30.6 2.8 %collective-permute-done.5.passed_y = f32[2,1096,128]{2,1,0:T(8,128)S(1)} collective-permute-done((f32[2,1096,128]{2,1,0:T(8,128)S(1)}, f32[2,1096,128]{2,1,0:T(8,128)S(1)}, u32[]{:S(2)}, u32[]{:S(2)}) %collective-permute-start.5) | collective-permute-done | bytes 1122336 | tf_op jit(solution)/shard_map/ppermute | solution.py:405
  33.4 15.0 %shard_map.61 = (f32[2,16,16,256]{3,2,1,0:T(8,128)S(1)}, f32[2,16,16,256]{3,2,1,0:T(8,128)S(1)}) custom-call(s32[1]{0:T(128)} %bitcast.where_ref, s32[1,1]{1,0:T(1,128)S(6)} %copy.6.code, f32[2,256]{1,0:T(2,128)} %wind.1, f32[32,16,256]{2,1,0:T(8,128)S(1)} %get-tuple-element.16.own, f32[32,16,256]{2,1,0:T(8,128)S(1)} %collective-permute-done.other, ...), custom_call_target="tpu_custom_call" | custom-call | tf_op jit(solution)/shard_map/pallas_call | solution.py:409
  48.4 0.2 collective-permute-start.6
  48.6 1.8 %collective-permute-done.6.got = f32[2,16,16,256]{3,2,1,0:T(8,128)S(1)} collective-permute-done((f32[2,16,16,256]{3,2,1,0:T(8,128)S(1)}, f32[2,16,16,256]{3,2,1,0:T(8,128)S(1)}, u32[]{:S(2)}, u32[]{:S(2)}) %collective-permute-start.6) | collective-permute-done | bytes 524320 | tf_op jit(solution)/shard_map/ppermute | solution.py:417
  50.4 1.0 %shard_map.62 = (f32[32,16,256]{2,1,0:T(8,128)}, f32[32,16,256]{2,1,0:T(8,128)}) custom-call(s32[1]{0:T(128)} %bitcast.where_ref, f32[2,16,16,256]{3,2,1,0:T(8,128)S(1)} %get-tuple-element.26.mine, f32[2,16,16,256]{3,2,1,0:T(8,128)S(1)} %collective-permute-done.6.got), custom_call_target="tpu_custom_call" | custom-call | tf_op jit(solution)/shard_map/pallas_call | solution.py:418
Async XLA Ops:
  0.6 2.6 %collective-permute-start = (f32[32,16,256]{2,1,0:T(8,128)}, f32[32,16,256]{2,1,0:T(8,128)S(1)}, u32[]{:S(2)}, u32[]{:S(2)}) collective-permute-start(f32[32,16,256]{2,1,0:T(8,128)} %bitcast.4), channel_id=1, source_target_pairs={{0,16},{16,0},{1,17},{17,1},{2,18},{18,2},{3,19},{19,3},{4,20},{20... | collective-permute-start | bytes 1572872 | tf_op jit(solution)/shard_map/ppermute | solution.py:385
  3.5 27.1 %collective-permute-start.2 = (f32[2,1096,128]{2,1,0:T(8,128)S(1)}, f32[2,1096,128]{2,1,0:T(8,128)S(1)}, u32[]{:S(2)}, u32[]{:S(2)}) collective-permute-start(f32[2,1096,128]{2,1,0:T(8,128)S(1)} %get-tuple-element.19), channel_id=1, source_target_pairs={{1,16},{16,1},{2,17},{17,2},{3,18},{18,3},{5,20},{20,5},{6,21},{21... | collective-permute-start | bytes 3366920 | tf_op jit(solution)/shard_map/ppermute | solution.py:401
  6.8 23.8 %collective-permute-start.1 = (f32[2,552,128]{2,1,0:T(8,128)S(1)}, f32[2,552,128]{2,1,0:T(8,128)S(1)}, u32[]{:S(2)}, u32[]{:S(2)}) collective-permute-start(f32[2,552,128]{2,1,0:T(8,128)S(1)} %get-tuple-element.18), channel_id=1, source_target_pairs={{4,16},{16,4},{5,17},{17,5},{6,18},{18,6},{7,19},{19,7},{8,20},{20... | collective-permute-start | bytes 1695752 | tf_op jit(solution)/shard_map/ppermute | solution.py:400
  9.0 17.4 %collective-permute-start.3 = (f32[2,168,128]{2,1,0:T(8,128)S(1)}, f32[2,168,128]{2,1,0:T(8,128)S(1)}, u32[]{:S(2)}, u32[]{:S(2)}) collective-permute-start(f32[2,168,128]{2,1,0:T(8,128)S(1)} %get-tuple-element.20), channel_id=1, source_target_pairs={{5,16},{16,5},{6,17},{17,6},{7,18},{18,7},{9,20},{20,9},{10,21},{2... | collective-permute-start | bytes 516104 | tf_op jit(solution)/shard_map/ppermute | solution.py:402
  12.0 14.5 %collective-permute-start.4 = (f32[2,168,128]{2,1,0:T(8,128)S(1)}, f32[2,168,128]{2,1,0:T(8,128)S(1)}, u32[]{:S(2)}, u32[]{:S(2)}) collective-permute-start(f32[2,168,128]{2,1,0:T(8,128)S(1)} %get-tuple-element.21), channel_id=1, source_target_pairs={{4,17},{17,4},{5,18},{18,5},{6,19},{19,6},{8,21},{21,8},{9,22},{22... | collective-permute-start | bytes 516104 | tf_op jit(solution)/shard_map/ppermute | solution.py:403
  30.6 2.8 %collective-permute-start.5 = (f32[2,1096,128]{2,1,0:T(8,128)S(1)}, f32[2,1096,128]{2,1,0:T(8,128)S(1)}, u32[]{:S(2)}, u32[]{:S(2)}) collective-permute-start(f32[2,1096,128]{2,1,0:T(8,128)S(1)} %collective-permute-done.2.halo_y), channel_id=1, source_target_pairs={{0,16},{16,0},{1,17},{17,1},{2,18},{18,2},{3,19},{19,3},{4,20},{20... | collective-permute-start | bytes 3366920 | tf_op jit(solution)/shard_map/ppermute | solution.py:405
  48.4 2.0 %collective-permute-start.6 = (f32[2,16,16,256]{3,2,1,0:T(8,128)S(1)}, f32[2,16,16,256]{3,2,1,0:T(8,128)S(1)}, u32[]{:S(2)}, u32[]{:S(2)}) collective-permute-start(f32[2,16,16,256]{3,2,1,0:T(8,128)S(1)} %get-tuple-element.27), channel_id=1, source_target_pairs={{0,16},{16,0},{1,17},{17,1},{2,18},{18,2},{3,19},{19,3},{4,20},{20... | collective-permute-start | bytes 1572872 | tf_op jit(solution)/shard_map/ppermute | solution.py:417

commit v5 on v4

--- a/solution.py
+++ b/solution.py
@@ -37,8 +37,8 @@
     return 1.5 - 1.0 / (1.0 + u * u)
 
 
-def sweeps(own_rows, own_columns, codes, wind, mix, start, mid, last_1, last_2, f, g1, g1b, g2, g2b, act_a, act_b,
-           write):
+def sweeps(stages, part, own_rows, own_columns, codes, wind, mix, start, mid, last_1, last_2, f, g1, g1b, g2, g2b,
+           act_a, act_b, write):
     halves = mix.shape[0]
     slices, parts = range(start.shape[0]), range(halves)
     scale = 0.5 * half_step
@@ -119,6 +119,7 @@
                 write(ref, at, value)
 
         for tiles, column, near, far in row_classes(reach, own_columns):
+            column, tiles = part(column, tiles)
             if near == 0:
                 group = 4 if own_rows % 4 == 0 else 2
 
@@ -181,12 +182,25 @@
         put("middle", u)
         put("final", u + rate + w2[0] * before + (w2[1] - 1.0) * get(g1b) + w2[2] * get(g2b))
 
-    evaluate(10, start, act_a, end_1)
-    evaluate(8, mid, act_b, end_2)
-    evaluate(6, last_1, act_a, end_3)
-    evaluate(4, mid, act_b, end_4)
-    evaluate(2, last_2, act_a, end_5)
-    evaluate(0, mid, act_b, end_6)
+    every = ((10, start, act_a, end_1), (8, mid, act_b, end_2), (6, last_1, act_a, end_3),
+             (4, mid, act_b, end_4), (2, last_2, act_a, end_5), (0, mid, act_b, end_6))
+    for stage in stages:
+        evaluate(*every[stage])
+
+
+def whole(column, tiles):
+    return column, tiles
+
+
+def apart(low, own_columns, passed):
+    def part(column, tiles):
+        end = HALO + own_columns
+        if low:
+            free = sum(column + TILE * k + TILE + 2 <= end for k in range(tiles))
+            return (column + TILE * free, tiles - free) if passed else (column, free)
+        bound = sum(column + TILE * k - 2 < HALO for k in range(tiles))
+        return (column, bound) if passed else (column + TILE * bound, tiles - bound)
+    return part
 
 
 def outside(word, low_x, low_y):
@@ -210,9 +224,8 @@
 BEFORE = tuple(sum(DEPTHS[:a]) for a in range(len(DEPTHS) + 1))
 
 
-def load_kernel(state, mixing, state_near, mixing_near, semaphores):
-    made = [pltpu.make_async_copy(a, b, semaphores.at[k])
-            for k, (a, b) in enumerate(((state, state_near), (mixing, mixing_near)))]
+def load_kernel(*refs):
+    made = [pltpu.make_async_copy(a, b, refs[6].at[k]) for k, (a, b) in enumerate(zip(refs[:3], refs[3:6]))]
     for one in made:
         one.start()
     for one in made:
@@ -252,60 +265,85 @@
     pl.when(t != 0)(lambda: side(False))
 
 
-def pair_kernel(where_ref, code, wind, own, other, mixing, halo_x, halo_y, passed_y, corner_1, corner_2,
-                mine, theirs, start, mid, last_1, last_2, f, g1, g1b, g2, g2b, act_a, act_b,
-                mix, both, codes):
-    t = where_ref[0]
-    block_rows, columns, levels = own.shape
-    halves = levels // LANES
-    half = block_rows // 2
-    inner = half + HALO
-
-    def word_of(ref):
-        return jnp.max(ref[0, pl.ds(ref.shape[1] - TILE, TILE), :]).astype(jnp.int32)
-
-    word_x, word_y, word_p, word_1, word_2 = [word_of(r) for r in (halo_x, halo_y, passed_y, corner_1, corner_2)]
-
+def filler(start, act, mix):
     def fill(a, z, x, y, value):
         at = (z, x, pl.ds(y, value.shape[0]), slice(None))
         if a < 2:
             start[(a, *at)] = value
-            act_a[(a, *at)] = growth(value)
+            act[(a, *at)] = growth(value)
         else:
             mix[at] = half_step * value
+    return fill
+
+
+def fill_y(fill, arrived, low, beyond, own_shape):
+    block_rows, columns, levels = own_shape
+    inner = block_rows // 2 + HALO
+    at_own, from_own = (HALO, 0) if low else (0, block_rows - inner)
+
+    @pl.loop(0, inner // 4)
+    def _(group):
+        for r in range(4):
+            i = 4 * group + r
+            for z in range(levels // LANES):
+                for a, depth in enumerate(DEPTHS):
+                    value = arrived[z, pl.ds(BEFORE[a] * block_rows + (from_own + i) * depth, depth), :]
+                    fill(a, z, at_own + i, HALO + columns if beyond else HALO - depth, value)
+
+
+def fill_codes(low, code, words, codes, inner):
+    word_x, word_y, word_p, word_1, word_2 = words
+    at_own, at_x = (HALO, 0) if low else (0, inner)
+    word_low, word_high = (word_y, word_p) if low else (word_p, word_y)
+    corner_low, corner_high = (word_1, word_2) if low else (word_2, word_1)
+
+    @pl.loop(0, inner)
+    def _(i):
+        codes[(at_own + i) * 3] = outside(word_low, True, True)
+        codes[(at_own + i) * 3 + 1] = code[0, 0]
+        codes[(at_own + i) * 3 + 2] = outside(word_high, True, False)
+
+    @pl.loop(0, HALO)
+    def _(i):
+        codes[(at_x + i) * 3] = outside(corner_low, low, True)
+        codes[(at_x + i) * 3 + 1] = outside(word_x, low, True)
+        codes[(at_x + i) * 3 + 2] = outside(corner_high, low, False)
+
+
+def word_of(ref):
+    return jnp.max(ref[0, pl.ds(ref.shape[1] - TILE, TILE), :]).astype(jnp.int32)
+
+
+def store(ref, at, value):
+    n, z, x, y = at
+    ref[n, z, x, pl.ds(y, TILE), :] = value
+
+
+def fill_kernel(where_ref, code, wind, own, other, mixing, halo_x, halo_y, corner_1, corner_2,
+                start, act_a, mix, f, mid, act_b, codes):
+    t = where_ref[0]
+    block_rows, columns, levels = own.shape
+    halves = levels // LANES
+    inner = block_rows // 2 + HALO
+    fill = filler(start, act_a, mix)
+    words = [word_of(halo_x), word_of(halo_y), 0, word_of(corner_1), word_of(corner_2)]
 
     def side(low):
-        at_own, from_own, at_x = (HALO, 0, 0) if low else (0, block_rows - inner, inner)
-        low_y, high_y = (halo_y, passed_y) if low else (passed_y, halo_y)
+        at_own, from_own = (HALO, 0) if low else (0, block_rows - inner)
         low_corner, high_corner = (corner_1, corner_2) if low else (corner_2, corner_1)
-        word_low, word_high = (word_y, word_p) if low else (word_p, word_y)
-        corner_low, corner_high = (word_1, word_2) if low else (word_2, word_1)
         arrays = (own, other, mixing) if low else (other, own, mixing)
-
-        @pl.loop(0, inner)
-        def _(i):
-            codes[(at_own + i) * 3] = outside(word_low, True, True)
-            codes[(at_own + i) * 3 + 1] = code[0, 0]
-            codes[(at_own + i) * 3 + 2] = outside(word_high, True, False)
-
-        @pl.loop(0, HALO)
-        def _(i):
-            codes[(at_x + i) * 3] = outside(corner_low, low, True)
-            codes[(at_x + i) * 3 + 1] = outside(word_x, low, True)
-            codes[(at_x + i) * 3 + 2] = outside(corner_high, low, False)
-
-        @pl.loop(0, inner // 2)
-        def _(pair):
-            for i in (2 * pair, 2 * pair + 1):
-                x = from_own + i
+        fill_codes(low, code, words, codes, inner)
+
+        @pl.loop(0, inner // 4)
+        def _(group):
+            for r in range(4):
+                i = 4 * group + r
                 for z in range(halves):
-                    for a, depth in enumerate(DEPTHS):
+                    for a in range(len(DEPTHS)):
                         for y in range(0, columns, TILE):
-                            fill(a, z, at_own + i, HALO + y, arrays[a][x, pl.ds(y, TILE), pl.ds(z * LANES, LANES)])
-                        at = pl.ds(BEFORE[a] * block_rows + x * depth, depth)
-                        fill(a, z, at_own + i, HALO - depth, low_y[z, at, :])
-                        fill(a, z, at_own + i, HALO + columns, high_y[z, at, :])
-
+                            fill(a, z, at_own + i, HALO + y, arrays[a][from_own + i, pl.ds(y, TILE), pl.ds(z * LANES, LANES)])
+
+        fill_y(fill, halo_y, low, not low, own.shape)
         for z in range(halves):
             for a, depth in enumerate(DEPTHS):
                 for i in range(depth):
@@ -316,6 +354,26 @@
                 x = HALO - 1 - d if low else inner + d
                 fill(a, z, x, HALO - wide, low_corner[z, pl.ds(offset, wide), :])
                 fill(a, z, x, HALO + columns, high_corner[z, pl.ds(offset, wide), :])
+        sweeps((0,), apart(low, columns, False), block_rows // 2, columns, codes, wind, mix, start, mid, None, None, f,
+               None, None, None, None, act_a, act_b, store)
+
+    pl.when(t == 0)(lambda: side(True))
+    pl.when(t != 0)(lambda: side(False))
+
+
+def pair_kernel(where_ref, code, wind, halo_x, halo_y, passed_y, corner_1, corner_2, *rest):
+    mine, theirs, start, act_a, mix, f, mid, act_b, last_1, last_2, g1, g1b, g2, g2b, both, codes = rest[6:]
+    t = where_ref[0]
+    half, columns = both.shape[2:4]
+    words = [word_of(r) for r in (halo_x, halo_y, passed_y, corner_1, corner_2)]
+
+    def run(stages, part, write):
+        sweeps(stages, part, half, columns, codes, wind, mix, start, mid, last_1, last_2, f, g1, g1b, g2, g2b, act_a, act_b, write)
+
+    def side(low):
+        fill_codes(low, code, words, codes, half + HALO)
+        fill_y(filler(start, act_a, mix), passed_y, low, low, (2 * half, columns, both.shape[4]))
+        run((0,), apart(low, columns, True), store)
 
     pl.when(t == 0)(lambda: side(True))
     pl.when(t != 0)(lambda: side(False))
@@ -326,9 +384,9 @@
             place = jnp.where(t == n, 0, 1)
             both[place, 0 if ref == "middle" else 1, x - HALO, pl.ds(y - HALO, TILE), pl.ds(z * LANES, LANES)] = value
         else:
-            ref[n, z, x, pl.ds(y, TILE), :] = value
-
-    sweeps(half, columns, codes, wind, mix, start, mid, last_1, last_2, f, g1, g1b, g2, g2b, act_a, act_b, write)
+            store(ref, at, value)
+
+    run(range(1, 6), whole, write)
     mine[...] = both[0]
     theirs[...] = both[1]
 
@@ -353,7 +411,7 @@
 VMEM = pl.BlockSpec(memory_space=pltpu.VMEM)
 SMEM = pl.BlockSpec(memory_space=pltpu.SMEM)
 ANY = pl.BlockSpec(memory_space=pl.ANY)
-LIMIT = 56 * 2**20
+LIMIT = 30 * 2**20
 
 
 def of(*shape):
@@ -382,42 +440,51 @@
         return pairs
 
     swap = [(0, 1), (1, 0)]
+    small = pltpu.CompilerParams(vmem_limit_bytes=4 * 2**20)
     other = near(lax.ppermute(state, "tm", swap))
-    state, mixing = pl.pallas_call(
-        load_kernel, out_shape=[pltpu.VMEM(x.shape, jnp.float32) for x in (state, mixing)],
-        in_specs=[ANY] * 2, out_specs=[VMEM] * 2, scratch_shapes=[pltpu.SemaphoreType.DMA((2,))],
+    local = state, mixing, wind
+    local = pl.pallas_call(
+        load_kernel, out_shape=[pltpu.VMEM(x.shape, jnp.float32) for x in local],
+        in_specs=[ANY] * 3, out_specs=[VMEM] * 3, scratch_shapes=[pltpu.SemaphoreType.DMA((3,))],
+        compiler_params=pltpu.CompilerParams(vmem_limit_bytes=60 * 2**20),
         cost_estimate=pl.CostEstimate(flops=0, bytes_accessed=16 * state.size, transcendentals=0),
-    )(state, mixing)
-    state, mixing = near(state), near(mixing)
+    )(*local)
+    state, mixing, wind = map(near, local)
     corner = (halves, CORNER_SIZE + TILE, LANES)
     to_x, to_y, to_1, to_2 = pl.pallas_call(
         pack_kernel,
         out_shape=[pltpu.VMEM(s, jnp.float32) for s in (
             (halves, BEFORE[-1] * columns + TILE, LANES), (halves, BEFORE[-1] * rows + TILE, LANES), corner, corner)],
         in_specs=[SMEM, SMEM, VMEM, VMEM, VMEM], out_specs=[VMEM] * 4,
-        compiler_params=pltpu.CompilerParams(vmem_limit_bytes=LIMIT),
+        compiler_params=small,
     )(where, code, state, other, mixing)
     halo_x = lax.ppermute(to_x, axes, partners(1, 0))
     halo_y = lax.ppermute(to_y, axes, partners(0, 1))
     corner_1 = lax.ppermute(to_1, axes, partners(1, 1))
     corner_2 = lax.ppermute(to_2, axes, partners(1, -1))
     halo_x, halo_y, corner_1, corner_2 = lax.optimization_barrier((halo_x, halo_y, corner_1, corner_2))
-    passed_y = lax.ppermute(halo_y, "tm", swap)
-    halo_x, halo_y, passed_y, corner_1, corner_2 = map(near, (halo_x, halo_y, passed_y, corner_1, corner_2))
+    passed_y = near(lax.ppermute(halo_y, "tm", swap))
+    halo_x, halo_y, corner_1, corner_2 = map(near, (halo_x, halo_y, corner_1, corner_2))
     half = rows // 2
     plane = (halves, half + 2 * HALO, columns + 2 * HALO + TILE, LANES)
-    mine, theirs = pl.pallas_call(
-        pair_kernel, out_shape=[pltpu.VMEM((2, half, columns, levels), jnp.float32)] * 2,
-        in_specs=[SMEM, SMEM] + [VMEM] * 9, out_specs=[VMEM] * 2,
-        scratch_shapes=[pltpu.VMEM((2, *plane), jnp.float32)] * 11 + [
-            pltpu.VMEM(plane, jnp.float32), pltpu.VMEM((2, 2, half, columns, levels), jnp.float32),
-            pltpu.SMEM((3 * (half + 2 * HALO),), jnp.int32)],
-        compiler_params=pltpu.CompilerParams(vmem_limit_bytes=LIMIT),
-    )(where, code, wind, state, other, mixing, halo_x, halo_y, passed_y, corner_1, corner_2)
+    planes = [pltpu.VMEM(s, jnp.float32) for s in ((2, *plane), (2, *plane), plane, (2, *plane), (2, *plane), (2, *plane))]
+    params = pltpu.CompilerParams(vmem_limit_bytes=LIMIT)
+    filled = pl.pallas_call(
+        fill_kernel, out_shape=planes, in_specs=[SMEM, SMEM] + [VMEM] * 8, out_specs=[VMEM] * 6,
+        scratch_shapes=[pltpu.SMEM((3 * (half + 2 * HALO),), jnp.int32)], compiler_params=small,
+        cost_estimate=pl.CostEstimate(flops=0, bytes_accessed=1 << 23, transcendentals=0),
+    )(where, code, wind, state, other, mixing, halo_x, halo_y, corner_1, corner_2)
+    mine, theirs, *_ = pl.pallas_call(
+        pair_kernel, out_shape=[pltpu.VMEM((2, half, columns, levels), jnp.float32)] * 2 + planes,
+        in_specs=[SMEM, SMEM] + [VMEM] * 12, out_specs=[VMEM] * 8, input_output_aliases={8 + k: 2 + k for k in range(6)},
+        scratch_shapes=[pltpu.VMEM((2, *plane), jnp.float32)] * 6 + [
+            pltpu.VMEM((2, 2, half, columns, levels), jnp.float32), pltpu.SMEM((3 * (half + 2 * HALO),), jnp.int32)],
+        compiler_params=params,
+    )(where, code, wind, halo_x, halo_y, passed_y, corner_1, corner_2, *map(near, filled))
     got = lax.ppermute(theirs, "tm", swap)
     middle, final = pl.pallas_call(
         merge_kernel, out_shape=[of(*state.shape)] * 2, in_specs=[SMEM, VMEM, VMEM], out_specs=[ANY] * 2,
-        scratch_shapes=[pltpu.SemaphoreType.DMA((4,))],
+        scratch_shapes=[pltpu.SemaphoreType.DMA((4,))], compiler_params=small,
     )(where, near(mine), near(got))
     return middle[None], final[None]
 

time: 51.6 us -> 49.7 us (0.963)
  waiting for transfers between devices: 20.1 us -> 17.1 us
    pallas_call x0 -> x1, Pallas kernels: none -> 3.2 us  [pair_shards(): pl.pallas_call(fill_kernel, out_shape=planes, in_specs=[SMEM, SMEM] + [VM...]
    ppermute x1, waiting for transfers between devices: 2.76 us -> 0.01 us  [pair_shards(): passed_y = near(lax.ppermute(halo_y, 'tm', swap))]
    pallas_call x1, Pallas kernels: 15 us -> 12.3 us  [pair_shards(): pl.pallas_call(pair_kernel, out_shape=[pltpu.VMEM((2, half, columns, leve...]
  transfers between devices with their start and end apart: 7 -> 7, of which waited for: 4 -> 3; matrix products, arithmetic and copies ran while one was open for 0% -> 0% of each run, Pallas kernels for 2% -> 9%
where the time goes in v5:
time: 49.7 us; the launch traced here: 49.5 us
  Pallas kernels  18 us (36%)
  waiting for transfers between devices  17.1 us (34%)
  starting transfers between devices  13 us (26%)
  between operations  1.36 us (3%)
    pallas_call x1, Pallas kernels, pair_shards(): pl.pallas_call(pair_kernel, out_shape=[pltpu.VMEM((2, half, columns, leve...  12.3 us
    ppermute x1, waiting for transfers between devices, pair_shards(): corner_1 = lax.ppermute(to_1, axes, partners(1, 1))  11.3 us
    ppermute x1, waiting for transfers between devices, pair_shards(): halo_x = lax.ppermute(to_x, axes, partners(1, 0))  4.24 us
    ppermute x1, starting transfers between devices, pair_shards(): halo_y = lax.ppermute(to_y, axes, partners(0, 1))  3.29 us
    pallas_call x1, Pallas kernels, pair_shards(): pl.pallas_call(fill_kernel, out_shape=planes, in_specs=[SMEM, SMEM] + [VM...  3.2 us
    ppermute x1, starting transfers between devices, pair_shards(): corner_2 = lax.ppermute(to_2, axes, partners(1, -1))  3.14 us
    ppermute x1, starting transfers between devices, pair_shards(): corner_1 = lax.ppermute(to_1, axes, partners(1, 1))  2.93 us
    ppermute x1, starting transfers between devices, pair_shards(): halo_x = lax.ppermute(to_x, axes, partners(1, 0))  2.19 us
  transfers between devices with their start and end apart: 7, of which 3 were waited for; matrix products, arithmetic and copies ran while one was open for 0% of the time, Pallas kernels for 9%

profile of v5, /device:TPU:19, one launch (start us, length us, event | category | flops | bytes accessed | tf_op | source)
XLA Modules:
  0.0 49.5 jit_solution(6713339430368528028)
XLA Ops:
  0.6 0.7 %collective-permute-start = (f32[32,16,256]{2,1,0:T(8,128)}, f32[32,16,256]{2,1,0:T(8,128)S(1)}, u32[]{:S(2)}, u32[]{:S(2)}) collective-permute-start(f32[32,16,256]{2,1,0:T(8,128)} %bitcast.4), channel_id=1, source_target_pairs={{0,16},{16,0},{1,17},{17,1},{2,18},{18,2},{3,19},{19,3},{4,20},{20... | collective-permute-start | bytes 1572872 | tf_op jit(solution)/shard_map/ppermute | solution.py:444
  2.0 1.2 %shard_map.59 = (f32[32,16,256]{2,1,0:T(8,128)S(1)}, f32[32,16,256]{2,1,0:T(8,128)S(1)}, f32[2,256]{1,0:T(2,128)S(1)}) custom-call(f32[32,16,256]{2,1,0:T(8,128)} %bitcast.5, f32[32,16,256]{2,1,0:T(8,128)} %refs_1_.1, f32[2,256]{1,0:T(2,128)} %refs_2_.1), custom_call_target="tpu_custom_call" | custom-call | bytes 2097152 | tf_op jit(solution)/shard_map/pallas_call | solution.py:446
  3.3 0.0 collective-permute-done.other
  3.3 0.3 shard_map.60
  3.5 3.3 %collective-permute-start.2 = (f32[2,1096,128]{2,1,0:T(8,128)S(1)}, f32[2,1096,128]{2,1,0:T(8,128)S(1)}, u32[]{:S(2)}, u32[]{:S(2)}) collective-permute-start(f32[2,1096,128]{2,1,0:T(8,128)S(1)} %get-tuple-element.27), channel_id=1, source_target_pairs={{1,16},{16,1},{2,17},{17,2},{3,18},{18,3},{5,20},{20,5},{6,21},{21... | collective-permute-start | bytes 3366920 | tf_op jit(solution)/shard_map/ppermute | solution.py:462
  6.8 2.2 %collective-permute-start.1 = (f32[2,552,128]{2,1,0:T(8,128)S(1)}, f32[2,552,128]{2,1,0:T(8,128)S(1)}, u32[]{:S(2)}, u32[]{:S(2)}) collective-permute-start(f32[2,552,128]{2,1,0:T(8,128)S(1)} %get-tuple-element.26), channel_id=1, source_target_pairs={{4,16},{16,4},{5,17},{17,5},{6,18},{18,6},{7,19},{19,7},{8,20},{20... | collective-permute-start | bytes 1695752 | tf_op jit(solution)/shard_map/ppermute | solution.py:461
  9.0 2.9 %collective-permute-start.3 = (f32[2,168,128]{2,1,0:T(8,128)S(1)}, f32[2,168,128]{2,1,0:T(8,128)S(1)}, u32[]{:S(2)}, u32[]{:S(2)}) collective-permute-start(f32[2,168,128]{2,1,0:T(8,128)S(1)} %get-tuple-element.28), channel_id=1, source_target_pairs={{5,16},{16,5},{6,17},{17,6},{7,18},{18,7},{9,20},{20,9},{10,21},{2... | collective-permute-start | bytes 516104 | tf_op jit(solution)/shard_map/ppermute | solution.py:463
  12.0 3.1 %collective-permute-start.4 = (f32[2,168,128]{2,1,0:T(8,128)S(1)}, f32[2,168,128]{2,1,0:T(8,128)S(1)}, u32[]{:S(2)}, u32[]{:S(2)}) collective-permute-start(f32[2,168,128]{2,1,0:T(8,128)S(1)} %get-tuple-element.29), channel_id=1, source_target_pairs={{4,17},{17,4},{5,18},{18,5},{6,19},{19,6},{8,21},{21,8},{9,22},{22... | collective-permute-start | bytes 516104 | tf_op jit(solution)/shard_map/ppermute | solution.py:464
  15.1 11.3 %collective-permute-done.3.corner_1 = f32[2,168,128]{2,1,0:T(8,128)S(1)} collective-permute-done((f32[2,168,128]{2,1,0:T(8,128)S(1)}, f32[2,168,128]{2,1,0:T(8,128)S(1)}, u32[]{:S(2)}, u32[]{:S(2)}) %collective-permute-start.3) | collective-permute-done | bytes 172064 | tf_op jit(solution)/shard_map/ppermute | solution.py:463
  26.4 0.0 collective-permute-done.4.corner_2
  26.4 4.2 %collective-permute-done.1.halo_x = f32[2,552,128]{2,1,0:T(8,128)S(1)} collective-permute-done((f32[2,552,128]{2,1,0:T(8,128)S(1)}, f32[2,552,128]{2,1,0:T(8,128)S(1)}, u32[]{:S(2)}, u32[]{:S(2)}) %collective-permute-start.1) | collective-permute-done | bytes 565280 | tf_op jit(solution)/shard_map/ppermute | solution.py:461
  30.7 0.0 collective-permute-done.2.halo_y
  30.7 0.0 collective-permute-start.5
  30.7 3.2 %shard_map.61 = (f32[2,2,40,48,128]{4,3,2,1,0:T(8,128)S(1)}, f32[2,2,40,48,128]{4,3,2,1,0:T(8,128)S(1)}, f32[2,40,48,128]{3,2,1,0:T(8,128)S(1)}, f32[2,2,40,48,1...) custom-call(s32[1]{0:T(128)} %bitcast.where_ref, ...), custom_call_target="tpu_custom_call" | custom-call | bytes 8388608 | tf_op jit(solution)/shard_map/pallas_call | solution.py:472
  33.9 0.0 collective-permute-done.5.passed_y
  33.9 12.3 %shard_map.62 = (f32[2,16,16,256]{3,2,1,0:T(8,128)S(1)}, f32[2,16,16,256]{3,2,1,0:T(8,128)S(1)}, f32[2,2,40,48,128]{4,3,2,1,0:T(8,128)S(1)}, f32[2,2,40,48,128]{...) custom-call(s32[1]{0:T(128)} %bitcast.where_ref, ...), custom_call_target="tpu_custom_call", output_to_operand_aliasing={{2}: (8, {}), {3}: (9, {}), {4}: (10, {}), {5}: (11, {}), {... | custom-call | tf_op jit(solution)/shard_map/pallas_call | solution.py:477
  46.2 0.7 %collective-permute-start.6 = (f32[2,16,16,256]{3,2,1,0:T(8,128)S(1)}, f32[2,16,16,256]{3,2,1,0:T(8,128)S(1)}, u32[]{:S(2)}, u32[]{:S(2)}) collective-permute-start(f32[2,16,16,256]{3,2,1,0:T(8,128)S(1)} %get-tuple-element.41), channel_id=1, source_target_pairs={{0,16},{16,0},{1,17},{17,1},{2,18},{18,2},{3,19},{19,3},{4,20},{20... | collective-permute-start | bytes 1572872 | tf_op jit(solution)/shard_map/ppermute | solution.py:484
  46.9 1.5 %collective-permute-done.6.got = f32[2,16,16,256]{3,2,1,0:T(8,128)S(1)} collective-permute-done((f32[2,16,16,256]{3,2,1,0:T(8,128)S(1)}, f32[2,16,16,256]{3,2,1,0:T(8,128)S(1)}, u32[]{:S(2)}, u32[]{:S(2)}) %collective-permute-start.6) | collective-permute-done | bytes 524320 | tf_op jit(solution)/shard_map/ppermute | solution.py:484
  48.5 1.0 %shard_map.63 = (f32[32,16,256]{2,1,0:T(8,128)}, f32[32,16,256]{2,1,0:T(8,128)}) custom-call(s32[1]{0:T(128)} %bitcast.where_ref, f32[2,16,16,256]{3,2,1,0:T(8,128)S(1)} %get-tuple-element.40.mine, f32[2,16,16,256]{3,2,1,0:T(8,128)S(1)} %collective-permute-done.6.got), custom_call_target="tpu_custom_call" | custom-call | tf_op jit(solution)/shard_map/pallas_call | solution.py:485
Async XLA Ops:
  0.6 2.6 %collective-permute-start = (f32[32,16,256]{2,1,0:T(8,128)}, f32[32,16,256]{2,1,0:T(8,128)S(1)}, u32[]{:S(2)}, u32[]{:S(2)}) collective-permute-start(f32[32,16,256]{2,1,0:T(8,128)} %bitcast.4), channel_id=1, source_target_pairs={{0,16},{16,0},{1,17},{17,1},{2,18},{18,2},{3,19},{19,3},{4,20},{20... | collective-permute-start | bytes 1572872 | tf_op jit(solution)/shard_map/ppermute | solution.py:444
  3.5 27.1 %collective-permute-start.2 = (f32[2,1096,128]{2,1,0:T(8,128)S(1)}, f32[2,1096,128]{2,1,0:T(8,128)S(1)}, u32[]{:S(2)}, u32[]{:S(2)}) collective-permute-start(f32[2,1096,128]{2,1,0:T(8,128)S(1)} %get-tuple-element.27), channel_id=1, source_target_pairs={{1,16},{16,1},{2,17},{17,2},{3,18},{18,3},{5,20},{20,5},{6,21},{21... | collective-permute-start | bytes 3366920 | tf_op jit(solution)/shard_map/ppermute | solution.py:462
  6.8 23.8 %collective-permute-start.1 = (f32[2,552,128]{2,1,0:T(8,128)S(1)}, f32[2,552,128]{2,1,0:T(8,128)S(1)}, u32[]{:S(2)}, u32[]{:S(2)}) collective-permute-start(f32[2,552,128]{2,1,0:T(8,128)S(1)} %get-tuple-element.26), channel_id=1, source_target_pairs={{4,16},{16,4},{5,17},{17,5},{6,18},{18,6},{7,19},{19,7},{8,20},{20... | collective-permute-start | bytes 1695752 | tf_op jit(solution)/shard_map/ppermute | solution.py:461
  9.0 17.4 %collective-permute-start.3 = (f32[2,168,128]{2,1,0:T(8,128)S(1)}, f32[2,168,128]{2,1,0:T(8,128)S(1)}, u32[]{:S(2)}, u32[]{:S(2)}) collective-permute-start(f32[2,168,128]{2,1,0:T(8,128)S(1)} %get-tuple-element.28), channel_id=1, source_target_pairs={{5,16},{16,5},{6,17},{17,6},{7,18},{18,7},{9,20},{20,9},{10,21},{2... | collective-permute-start | bytes 516104 | tf_op jit(solution)/shard_map/ppermute | solution.py:463
  12.0 14.4 %collective-permute-start.4 = (f32[2,168,128]{2,1,0:T(8,128)S(1)}, f32[2,168,128]{2,1,0:T(8,128)S(1)}, u32[]{:S(2)}, u32[]{:S(2)}) collective-permute-start(f32[2,168,128]{2,1,0:T(8,128)S(1)} %get-tuple-element.29), channel_id=1, source_target_pairs={{4,17},{17,4},{5,18},{18,5},{6,19},{19,6},{8,21},{21,8},{9,22},{22... | collective-permute-start | bytes 516104 | tf_op jit(solution)/shard_map/ppermute | solution.py:464
  30.7 3.2 %collective-permute-start.5 = (f32[2,1096,128]{2,1,0:T(8,128)S(1)}, f32[2,1096,128]{2,1,0:T(8,128)S(1)}, u32[]{:S(2)}, u32[]{:S(2)}) collective-permute-start(f32[2,1096,128]{2,1,0:T(8,128)S(1)} %collective-permute-done.2.halo_y), channel_id=1, source_target_pairs={{0,16},{16,0},{1,17},{17,1},{2,18},{18,2},{3,19},{19,3},{4,20},{20... | collective-permute-start | bytes 3366920 | tf_op jit(solution)/shard_map/ppermute | solution.py:466
  46.2 2.2 %collective-permute-start.6 = (f32[2,16,16,256]{3,2,1,0:T(8,128)S(1)}, f32[2,16,16,256]{3,2,1,0:T(8,128)S(1)}, u32[]{:S(2)}, u32[]{:S(2)}) collective-permute-start(f32[2,16,16,256]{3,2,1,0:T(8,128)S(1)} %get-tuple-element.41), channel_id=1, source_target_pairs={{0,16},{16,0},{1,17},{17,1},{2,18},{18,2},{3,19},{19,3},{4,20},{20... | collective-permute-start | bytes 1572872 | tf_op jit(solution)/shard_map/ppermute | solution.py:484

commit v6 on v5

--- a/solution.py
+++ b/solution.py
@@ -123,7 +123,7 @@
             if near == 0:
                 group = 4 if own_rows % 4 == 0 else 2
 
-                @pl.loop(0, own_rows // group)
+                @pl.loop(0, own_rows // group, unroll=2)
                 def _(i, column=column, tiles=tiles, group=group):
                     block(HALO + group * i, group, column, tiles)
             else:
@@ -232,11 +232,11 @@
         one.wait()
 
 
-def pack_kernel(where_ref, code, own, other, mixing, beside_x, beside_y, diagonal_1, diagonal_2):
+def pack_kernel(where_ref, code, own, other, mixing, beside_x, diagonal_1, diagonal_2, *beside_y):
     t = where_ref[0]
     rows, columns, levels = own.shape
     word = jnp.full((TILE, LANES), (code[0, 0] + 1).astype(jnp.float32))
-    for ref in (beside_x, beside_y, diagonal_1, diagonal_2):
+    for ref in (beside_x, diagonal_1, diagonal_2, *beside_y):
         ref[0, pl.ds(ref.shape[1] - TILE, TILE), :] = word
 
     def side(low):
@@ -259,7 +259,7 @@
                 for z in range(levels // LANES):
                     for a, depth in enumerate(DEPTHS):
                         line = arrays[a][x, pl.ds(0 if low else columns - depth, depth), pl.ds(z * LANES, LANES)]
-                        beside_y[z, pl.ds(BEFORE[a] * rows + x * depth, depth), :] = line
+                        beside_y[z][0, pl.ds(BEFORE[a] * rows + x * depth, depth), :] = line
 
     pl.when(t == 0)(lambda: side(True))
     pl.when(t != 0)(lambda: side(False))
@@ -287,7 +287,7 @@
             i = 4 * group + r
             for z in range(levels // LANES):
                 for a, depth in enumerate(DEPTHS):
-                    value = arrived[z, pl.ds(BEFORE[a] * block_rows + (from_own + i) * depth, depth), :]
+                    value = arrived[z][0, pl.ds(BEFORE[a] * block_rows + (from_own + i) * depth, depth), :]
                     fill(a, z, at_own + i, HALO + columns if beyond else HALO - depth, value)
 
 
@@ -319,14 +319,14 @@
     ref[n, z, x, pl.ds(y, TILE), :] = value
 
 
-def fill_kernel(where_ref, code, wind, own, other, mixing, halo_x, halo_y, corner_1, corner_2,
-                start, act_a, mix, f, mid, act_b, codes):
+def fill_kernel(where_ref, code, wind, own, other, mixing, halo_x, corner_1, corner_2, *rest):
     t = where_ref[0]
     block_rows, columns, levels = own.shape
     halves = levels // LANES
+    halo_y, (start, act_a, mix, f, mid, act_b, codes) = rest[:halves], rest[halves:]
     inner = block_rows // 2 + HALO
     fill = filler(start, act_a, mix)
-    words = [word_of(halo_x), word_of(halo_y), 0, word_of(corner_1), word_of(corner_2)]
+    words = [word_of(halo_x), word_of(halo_y[0]), 0, word_of(corner_1), word_of(corner_2)]
 
     def side(low):
         at_own, from_own = (HALO, 0) if low else (0, block_rows - inner)
@@ -361,11 +361,12 @@
     pl.when(t != 0)(lambda: side(False))
 
 
-def pair_kernel(where_ref, code, wind, halo_x, halo_y, passed_y, corner_1, corner_2, *rest):
-    mine, theirs, start, act_a, mix, f, mid, act_b, last_1, last_2, g1, g1b, g2, g2b, both, codes = rest[6:]
+def pair_kernel(halves, where_ref, code, wind, halo_x, corner_1, corner_2, *rest):
+    halo_y, passed_y = rest[:halves], rest[halves:2 * halves]
+    mine, theirs, start, act_a, mix, f, mid, act_b, last_1, last_2, g1, g1b, g2, g2b, both, codes = rest[2 * halves + 6:]
     t = where_ref[0]
     half, columns = both.shape[2:4]
-    words = [word_of(r) for r in (halo_x, halo_y, passed_y, corner_1, corner_2)]
+    words = [word_of(r) for r in (halo_x, halo_y[0], passed_y[0], corner_1, corner_2)]
 
     def run(stages, part, write):
         sweeps(stages, part, half, columns, codes, wind, mix, start, mid, last_1, last_2, f, g1, g1b, g2, g2b, act_a, act_b, write)
@@ -450,37 +451,36 @@
         cost_estimate=pl.CostEstimate(flops=0, bytes_accessed=16 * state.size, transcendentals=0),
     )(*local)
     state, mixing, wind = map(near, local)
-    corner = (halves, CORNER_SIZE + TILE, LANES)
-    to_x, to_y, to_1, to_2 = pl.pallas_call(
-        pack_kernel,
-        out_shape=[pltpu.VMEM(s, jnp.float32) for s in (
-            (halves, BEFORE[-1] * columns + TILE, LANES), (halves, BEFORE[-1] * rows + TILE, LANES), corner, corner)],
-        in_specs=[SMEM, SMEM, VMEM, VMEM, VMEM], out_specs=[VMEM] * 4,
-        compiler_params=small,
+    shapes = [(halves, BEFORE[-1] * columns + TILE, LANES)] + [(halves, CORNER_SIZE + TILE, LANES)] * 2
+    shapes += [(1, BEFORE[-1] * rows + TILE, LANES)] * halves
+    to_x, to_1, to_2, *to_y = pl.pallas_call(
+        pack_kernel, out_shape=[pltpu.VMEM(s, jnp.float32) for s in shapes],
+        in_specs=[SMEM, SMEM, VMEM, VMEM, VMEM], out_specs=[VMEM] * len(shapes), compiler_params=small,
     )(where, code, state, other, mixing)
     halo_x = lax.ppermute(to_x, axes, partners(1, 0))
-    halo_y = lax.ppermute(to_y, axes, partners(0, 1))
+    halo_y = [lax.ppermute(y, axes, partners(0, 1)) for y in to_y]
     corner_1 = lax.ppermute(to_1, axes, partners(1, 1))
     corner_2 = lax.ppermute(to_2, axes, partners(1, -1))
     halo_x, halo_y, corner_1, corner_2 = lax.optimization_barrier((halo_x, halo_y, corner_1, corner_2))
-    passed_y = near(lax.ppermute(halo_y, "tm", swap))
-    halo_x, halo_y, corner_1, corner_2 = map(near, (halo_x, halo_y, corner_1, corner_2))
+    passed_y = [near(lax.ppermute(y, "tm", swap)) for y in halo_y]
+    halo_x, corner_1, corner_2, *halo_y = map(near, (halo_x, corner_1, corner_2, *halo_y))
     half = rows // 2
     plane = (halves, half + 2 * HALO, columns + 2 * HALO + TILE, LANES)
     planes = [pltpu.VMEM(s, jnp.float32) for s in ((2, *plane), (2, *plane), plane, (2, *plane), (2, *plane), (2, *plane))]
     params = pltpu.CompilerParams(vmem_limit_bytes=LIMIT)
     filled = pl.pallas_call(
-        fill_kernel, out_shape=planes, in_specs=[SMEM, SMEM] + [VMEM] * 8, out_specs=[VMEM] * 6,
+        fill_kernel, out_shape=planes, in_specs=[SMEM, SMEM] + [VMEM] * (7 + halves), out_specs=[VMEM] * 6,
         scratch_shapes=[pltpu.SMEM((3 * (half + 2 * HALO),), jnp.int32)], compiler_params=small,
         cost_estimate=pl.CostEstimate(flops=0, bytes_accessed=1 << 23, transcendentals=0),
-    )(where, code, wind, state, other, mixing, halo_x, halo_y, corner_1, corner_2)
+    )(where, code, wind, state, other, mixing, halo_x, corner_1, corner_2, *halo_y)
     mine, theirs, *_ = pl.pallas_call(
-        pair_kernel, out_shape=[pltpu.VMEM((2, half, columns, levels), jnp.float32)] * 2 + planes,
-        in_specs=[SMEM, SMEM] + [VMEM] * 12, out_specs=[VMEM] * 8, input_output_aliases={8 + k: 2 + k for k in range(6)},
+        functools.partial(pair_kernel, halves), out_shape=[pltpu.VMEM((2, half, columns, levels), jnp.float32)] * 2 + planes,
+        in_specs=[SMEM, SMEM] + [VMEM] * (10 + 2 * halves), out_specs=[VMEM] * 8,
+        input_output_aliases={6 + 2 * halves + k: 2 + k for k in range(6)},
         scratch_shapes=[pltpu.VMEM((2, *plane), jnp.float32)] * 6 + [
             pltpu.VMEM((2, 2, half, columns, levels), jnp.float32), pltpu.SMEM((3 * (half + 2 * HALO),), jnp.int32)],
         compiler_params=params,
-    )(where, code, wind, halo_x, halo_y, passed_y, corner_1, corner_2, *map(near, filled))
+    )(where, code, wind, halo_x, corner_1, corner_2, *halo_y, *passed_y, *map(near, filled))
     got = lax.ppermute(theirs, "tm", swap)
     middle, final = pl.pallas_call(
         merge_kernel, out_shape=[of(*state.shape)] * 2, in_specs=[SMEM, VMEM, VMEM], out_specs=[ANY] * 2,

time: 49.7 us -> 48.7 us (0.980)
  waiting for transfers between devices: 17.1 us -> 12.8 us
  starting transfers between devices: 13 us -> 16.6 us
    ppermute x1, waiting for transfers between devices: 4.24 us -> 0.01 us  [pair_shards(): halo_x = lax.ppermute(to_x, axes, partners(1, 0))]
    ppermute x2 -> x4, starting transfers between devices: 3.29 us -> 6.13 us  [the longest x2 5.56 us: pair_shards(): halo_y = [lax.ppermute(y, axes, partners(0, 1)) for y in to_y]]
    ppermute x1, starting transfers between devices: 2.93 us -> 4.26 us  [pair_shards(): corner_1 = lax.ppermute(to_1, axes, partners(1, 1))]
    ppermute x1, starting transfers between devices: 3.14 us -> 1.97 us  [pair_shards(): corner_2 = lax.ppermute(to_2, axes, partners(1, -1))]
    ppermute x1, starting transfers between devices: 2.19 us -> 3.22 us  [pair_shards(): halo_x = lax.ppermute(to_x, axes, partners(1, 0))]
  transfers between devices with their start and end apart: 7 -> 9, of which waited for: 3 -> 2; matrix products, arithmetic and copies ran while one was open for 0% -> 0% of each run, Pallas kernels for 9% -> 9%
where the time goes in v6:
time: 48.7 us; the launch traced here: 48.5 us
  Pallas kernels  17.7 us (36%)
  starting transfers between devices  16.6 us (34%)
  waiting for transfers between devices  12.8 us (26%)
  between operations  1.4 us (3%)
    pallas_call x1, Pallas kernels, pair_shards(): pl.pallas_call(functools.partial(pair_kernel, halves), out_shape=[pltpu.V...  12.1 us
    ppermute x1, waiting for transfers between devices, pair_shards(): corner_1 = lax.ppermute(to_1, axes, partners(1, 1))  11.1 us
    ppermute x2, starting transfers between devices, pair_shards(): halo_y = [lax.ppermute(y, axes, partners(0, 1)) for y in to_y]  5.56 us
    ppermute x1, starting transfers between devices, pair_shards(): corner_1 = lax.ppermute(to_1, axes, partners(1, 1))  4.26 us
    ppermute x1, starting transfers between devices, pair_shards(): halo_x = lax.ppermute(to_x, axes, partners(1, 0))  3.22 us
    pallas_call x1, Pallas kernels, pair_shards(): pl.pallas_call(fill_kernel, out_shape=planes, in_specs=[SMEM, SMEM] + [VM...  3.14 us
    ppermute x1, starting transfers between devices, pair_shards(): corner_2 = lax.ppermute(to_2, axes, partners(1, -1))  1.97 us
    ppermute x1, waiting for transfers between devices, pair_shards(): got = lax.ppermute(theirs, 'tm', swap)  1.68 us
  transfers between devices with their start and end apart: 9, of which 2 were waited for; matrix products, arithmetic and copies ran while one was open for 0% of the time, Pallas kernels for 9%

profile of v6, /device:TPU:19, one launch (start us, length us, event | category | flops | bytes accessed | tf_op | source)
XLA Modules:
  0.0 48.5 jit_solution(9696776452861887004)
XLA Ops:
  0.6 0.7 %collective-permute-start = (f32[32,16,256]{2,1,0:T(8,128)}, f32[32,16,256]{2,1,0:T(8,128)S(1)}, u32[]{:S(2)}, u32[]{:S(2)}) collective-permute-start(f32[32,16,256]{2,1,0:T(8,128)} %bitcast.4), channel_id=1, source_target_pairs={{0,16},{16,0},{1,17},{17,1},{2,18},{18,2},{3,19},{19,3},{4,20},{20... | collective-permute-start | bytes 1572872 | tf_op jit(solution)/shard_map/ppermute | solution.py:445
  2.0 1.2 %shard_map.59 = (f32[32,16,256]{2,1,0:T(8,128)S(1)}, f32[32,16,256]{2,1,0:T(8,128)S(1)}, f32[2,256]{1,0:T(2,128)S(1)}) custom-call(f32[32,16,256]{2,1,0:T(8,128)} %bitcast.5, f32[32,16,256]{2,1,0:T(8,128)} %refs_1_.1, f32[2,256]{1,0:T(2,128)} %refs_2_.1), custom_call_target="tpu_custom_call" | custom-call | bytes 2097152 | tf_op jit(solution)/shard_map/pallas_call | solution.py:447
  3.3 0.0 collective-permute-done.other
  3.3 0.3 shard_map.60
  3.6 3.2 %collective-permute-start.1 = (f32[2,552,128]{2,1,0:T(8,128)S(1)}, f32[2,552,128]{2,1,0:T(8,128)S(1)}, u32[]{:S(2)}, u32[]{:S(2)}) collective-permute-start(f32[2,552,128]{2,1,0:T(8,128)S(1)} %get-tuple-element.28), channel_id=1, source_target_pairs={{4,16},{16,4},{5,17},{17,5},{6,18},{18,6},{7,19},{19,7},{8,20},{20... | collective-permute-start | bytes 1695752 | tf_op jit(solution)/shard_map/ppermute | solution.py:460
  6.8 2.4 %collective-permute-start.2 = (f32[1,1096,128]{2,1,0:T(8,128)S(1)}, f32[1,1096,128]{2,1,0:T(8,128)S(1)}, u32[]{:S(2)}, u32[]{:S(2)}) collective-permute-start(f32[1,1096,128]{2,1,0:T(8,128)S(1)} %get-tuple-element.29), channel_id=1, source_target_pairs={{1,16},{16,1},{2,17},{17,2},{3,18},{18,3},{5,20},{20,5},{6,21},{21... | collective-permute-start | bytes 1683464 | tf_op jit(solution)/shard_map/ppermute | solution.py:461
  9.2 3.1 %collective-permute-start.3 = (f32[1,1096,128]{2,1,0:T(8,128)S(1)}, f32[1,1096,128]{2,1,0:T(8,128)S(1)}, u32[]{:S(2)}, u32[]{:S(2)}) collective-permute-start(f32[1,1096,128]{2,1,0:T(8,128)S(1)} %get-tuple-element.30), channel_id=1, source_target_pairs={{1,16},{16,1},{2,17},{17,2},{3,18},{18,3},{5,20},{20,5},{6,21},{21... | collective-permute-start | bytes 1683464 | tf_op jit(solution)/shard_map/ppermute | solution.py:461
  12.4 4.3 %collective-permute-start.4 = (f32[2,168,128]{2,1,0:T(8,128)S(1)}, f32[2,168,128]{2,1,0:T(8,128)S(1)}, u32[]{:S(2)}, u32[]{:S(2)}) collective-permute-start(f32[2,168,128]{2,1,0:T(8,128)S(1)} %get-tuple-element.31), channel_id=1, source_target_pairs={{5,16},{16,5},{6,17},{17,6},{7,18},{18,7},{9,20},{20,9},{10,21},{2... | collective-permute-start | bytes 516104 | tf_op jit(solution)/shard_map/ppermute | solution.py:462
  16.6 2.0 %collective-permute-start.5 = (f32[2,168,128]{2,1,0:T(8,128)S(1)}, f32[2,168,128]{2,1,0:T(8,128)S(1)}, u32[]{:S(2)}, u32[]{:S(2)}) collective-permute-start(f32[2,168,128]{2,1,0:T(8,128)S(1)} %get-tuple-element.32), channel_id=1, source_target_pairs={{4,17},{17,4},{5,18},{18,5},{6,19},{19,6},{8,21},{21,8},{9,22},{22... | collective-permute-start | bytes 516104 | tf_op jit(solution)/shard_map/ppermute | solution.py:463
  18.6 11.1 %collective-permute-done.4.corner_1 = f32[2,168,128]{2,1,0:T(8,128)S(1)} collective-permute-done((f32[2,168,128]{2,1,0:T(8,128)S(1)}, f32[2,168,128]{2,1,0:T(8,128)S(1)}, u32[]{:S(2)}, u32[]{:S(2)}) %collective-permute-start.4) | collective-permute-done | bytes 172064 | tf_op jit(solution)/shard_map/ppermute | solution.py:462
  29.7 0.0 collective-permute-done.5.corner_2
  29.7 0.0 collective-permute-done.2.rest_0_
  29.7 0.0 collective-permute-done.3.rest_1_
  29.7 0.0 collective-permute-done.1.halo_x
  29.7 0.1 collective-permute-start.6
  29.8 0.5 %collective-permute-start.7 = (f32[1,1096,128]{2,1,0:T(8,128)S(1)}, f32[1,1096,128]{2,1,0:T(8,128)S(1)}, u32[]{:S(2)}, u32[]{:S(2)}) collective-permute-start(f32[1,1096,128]{2,1,0:T(8,128)S(1)} %collective-permute-done.3.rest_1_), channel_id=1, source_target_pairs={{0,16},{16,0},{1,17},{17,1},{2,18},{18,2},{3,19},{19,3},{4,20},{20... | collective-permute-start | bytes 1683464 | tf_op jit(solution)/shard_map/ppermute | solution.py:465
  30.3 3.1 %shard_map.61 = (f32[2,2,40,48,128]{4,3,2,1,0:T(8,128)S(1)}, f32[2,2,40,48,128]{4,3,2,1,0:T(8,128)S(1)}, f32[2,40,48,128]{3,2,1,0:T(8,128)S(1)}, f32[2,2,40,48,1...) custom-call(s32[1]{0:T(128)} %bitcast.where_ref, ...), custom_call_target="tpu_custom_call" | custom-call | bytes 8388608 | tf_op jit(solution)/shard_map/pallas_call | solution.py:471
  33.4 0.0 collective-permute-done.6.rest_2_
  33.5 0.0 collective-permute-done.7.rest_3_
  33.5 12.1 %shard_map.62 = (f32[2,16,16,256]{3,2,1,0:T(8,128)S(1)}, f32[2,16,16,256]{3,2,1,0:T(8,128)S(1)}, f32[2,2,40,48,128]{4,3,2,1,0:T(8,128)S(1)}, f32[2,2,40,48,128]{...) custom-call(s32[1]{0:T(128)} %bitcast.where_ref, ...), custom_call_target="tpu_custom_call", output_to_operand_aliasing={{2}: (10, {}), {3}: (11, {}), {4}: (12, {}), {5}: (13, {}),... | custom-call | tf_op jit(solution)/shard_map/pallas_call | solution.py:476
  45.5 0.3 collective-permute-start.8
  45.8 1.7 %collective-permute-done.8.got = f32[2,16,16,256]{3,2,1,0:T(8,128)S(1)} collective-permute-done((f32[2,16,16,256]{3,2,1,0:T(8,128)S(1)}, f32[2,16,16,256]{3,2,1,0:T(8,128)S(1)}, u32[]{:S(2)}, u32[]{:S(2)}) %collective-permute-start.8) | collective-permute-done | bytes 524320 | tf_op jit(solution)/shard_map/ppermute | solution.py:484
  47.5 1.0 %shard_map.63 = (f32[32,16,256]{2,1,0:T(8,128)}, f32[32,16,256]{2,1,0:T(8,128)}) custom-call(s32[1]{0:T(128)} %bitcast.where_ref, f32[2,16,16,256]{3,2,1,0:T(8,128)S(1)} %get-tuple-element.44.mine, f32[2,16,16,256]{3,2,1,0:T(8,128)S(1)} %collective-permute-done.8.got), custom_call_target="tpu_custom_call" | custom-call | tf_op jit(solution)/shard_map/pallas_call | solution.py:485
Async XLA Ops:
  0.6 2.6 %collective-permute-start = (f32[32,16,256]{2,1,0:T(8,128)}, f32[32,16,256]{2,1,0:T(8,128)S(1)}, u32[]{:S(2)}, u32[]{:S(2)}) collective-permute-start(f32[32,16,256]{2,1,0:T(8,128)} %bitcast.4), channel_id=1, source_target_pairs={{0,16},{16,0},{1,17},{17,1},{2,18},{18,2},{3,19},{19,3},{4,20},{20... | collective-permute-start | bytes 1572872 | tf_op jit(solution)/shard_map/ppermute | solution.py:445
  3.6 26.2 %collective-permute-start.1 = (f32[2,552,128]{2,1,0:T(8,128)S(1)}, f32[2,552,128]{2,1,0:T(8,128)S(1)}, u32[]{:S(2)}, u32[]{:S(2)}) collective-permute-start(f32[2,552,128]{2,1,0:T(8,128)S(1)} %get-tuple-element.28), channel_id=1, source_target_pairs={{4,16},{16,4},{5,17},{17,5},{6,18},{18,6},{7,19},{19,7},{8,20},{20... | collective-permute-start | bytes 1695752 | tf_op jit(solution)/shard_map/ppermute | solution.py:460
  6.8 22.9 %collective-permute-start.2 = (f32[1,1096,128]{2,1,0:T(8,128)S(1)}, f32[1,1096,128]{2,1,0:T(8,128)S(1)}, u32[]{:S(2)}, u32[]{:S(2)}) collective-permute-start(f32[1,1096,128]{2,1,0:T(8,128)S(1)} %get-tuple-element.29), channel_id=1, source_target_pairs={{1,16},{16,1},{2,17},{17,2},{3,18},{18,3},{5,20},{20,5},{6,21},{21... | collective-permute-start | bytes 1683464 | tf_op jit(solution)/shard_map/ppermute | solution.py:461
  9.2 20.5 %collective-permute-start.3 = (f32[1,1096,128]{2,1,0:T(8,128)S(1)}, f32[1,1096,128]{2,1,0:T(8,128)S(1)}, u32[]{:S(2)}, u32[]{:S(2)}) collective-permute-start(f32[1,1096,128]{2,1,0:T(8,128)S(1)} %get-tuple-element.30), channel_id=1, source_target_pairs={{1,16},{16,1},{2,17},{17,2},{3,18},{18,3},{5,20},{20,5},{6,21},{21... | collective-permute-start | bytes 1683464 | tf_op jit(solution)/shard_map/ppermute | solution.py:461
  12.4 17.3 %collective-permute-start.4 = (f32[2,168,128]{2,1,0:T(8,128)S(1)}, f32[2,168,128]{2,1,0:T(8,128)S(1)}, u32[]{:S(2)}, u32[]{:S(2)}) collective-permute-start(f32[2,168,128]{2,1,0:T(8,128)S(1)} %get-tuple-element.31), channel_id=1, source_target_pairs={{5,16},{16,5},{6,17},{17,6},{7,18},{18,7},{9,20},{20,9},{10,21},{2... | collective-permute-start | bytes 516104 | tf_op jit(solution)/shard_map/ppermute | solution.py:462
  16.6 13.1 %collective-permute-start.5 = (f32[2,168,128]{2,1,0:T(8,128)S(1)}, f32[2,168,128]{2,1,0:T(8,128)S(1)}, u32[]{:S(2)}, u32[]{:S(2)}) collective-permute-start(f32[2,168,128]{2,1,0:T(8,128)S(1)} %get-tuple-element.32), channel_id=1, source_target_pairs={{4,17},{17,4},{5,18},{18,5},{6,19},{19,6},{8,21},{21,8},{9,22},{22... | collective-permute-start | bytes 516104 | tf_op jit(solution)/shard_map/ppermute | solution.py:463
  29.7 3.7 %collective-permute-start.6 = (f32[1,1096,128]{2,1,0:T(8,128)S(1)}, f32[1,1096,128]{2,1,0:T(8,128)S(1)}, u32[]{:S(2)}, u32[]{:S(2)}) collective-permute-start(f32[1,1096,128]{2,1,0:T(8,128)S(1)} %collective-permute-done.2.rest_0_), channel_id=1, source_target_pairs={{0,16},{16,0},{1,17},{17,1},{2,18},{18,2},{3,19},{19,3},{4,20},{20... | collective-permute-start | bytes 1683464 | tf_op jit(solution)/shard_map/ppermute | solution.py:465
  29.8 3.7 %collective-permute-start.7 = (f32[1,1096,128]{2,1,0:T(8,128)S(1)}, f32[1,1096,128]{2,1,0:T(8,128)S(1)}, u32[]{:S(2)}, u32[]{:S(2)}) collective-permute-start(f32[1,1096,128]{2,1,0:T(8,128)S(1)} %collective-permute-done.3.rest_1_), channel_id=1, source_target_pairs={{0,16},{16,0},{1,17},{17,1},{2,18},{18,2},{3,19},{19,3},{4,20},{20... | collective-permute-start | bytes 1683464 | tf_op jit(solution)/shard_map/ppermute | solution.py:465
  45.5 2.0 %collective-permute-start.8 = (f32[2,16,16,256]{3,2,1,0:T(8,128)S(1)}, f32[2,16,16,256]{3,2,1,0:T(8,128)S(1)}, u32[]{:S(2)}, u32[]{:S(2)}) collective-permute-start(f32[2,16,16,256]{3,2,1,0:T(8,128)S(1)} %get-tuple-element.45), channel_id=1, source_target_pairs={{0,16},{16,0},{1,17},{17,1},{2,18},{18,2},{3,19},{19,3},{4,20},{20... | collective-permute-start | bytes 1572872 | tf_op jit(solution)/shard_map/ppermute | solution.py:484

commit v7 on v6

--- a/solution.py
+++ b/solution.py
@@ -392,21 +392,20 @@
     theirs[...] = both[1]
 
 
-def merge_kernel(where_ref, mine, got, middle, final, semaphores):
-    t = where_ref[0]
-    half = mine.shape[1]
-
-    def merge(low):
-        halves = (mine, got) if low else (got, mine)
-        made = [pltpu.make_async_copy(part.at[k], out.at[pl.ds(h * half, half)], semaphores.at[2 * h + k])
-                for h, part in enumerate(halves) for k, out in enumerate((middle, final))]
+def place_kernel(where_ref, part, *rest):
+    middle, final, semaphores = rest[-3:]
+    own = len(rest) == 3
+    half = part.shape[1]
+
+    def place(begin):
+        made = [pltpu.make_async_copy(part.at[k], out.at[pl.ds(begin, half)], semaphores.at[k]) for k, out in enumerate((middle, final))]
         for one in made:
             one.start()
         for one in made:
             one.wait()
 
-    pl.when(t == 0)(lambda: merge(True))
-    pl.when(t != 0)(lambda: merge(False))
+    pl.when(where_ref[0] == 0)(lambda: place(0 if own else half))
+    pl.when(where_ref[0] != 0)(lambda: place(half if own else 0))
 
 
 VMEM = pl.BlockSpec(memory_space=pltpu.VMEM)
@@ -482,10 +481,16 @@
         compiler_params=params,
     )(where, code, wind, halo_x, corner_1, corner_2, *halo_y, *passed_y, *map(near, filled))
     got = lax.ppermute(theirs, "tm", swap)
+    outs = [of(*state.shape)] * 2
+    halves_done = pl.pallas_call(
+        place_kernel, out_shape=outs, in_specs=[SMEM, VMEM], out_specs=[ANY] * 2,
+        scratch_shapes=[pltpu.SemaphoreType.DMA((2,))], compiler_params=small,
+        cost_estimate=pl.CostEstimate(flops=0, bytes_accessed=1 << 22, transcendentals=0),
+    )(where, near(mine))
     middle, final = pl.pallas_call(
-        merge_kernel, out_shape=[of(*state.shape)] * 2, in_specs=[SMEM, VMEM, VMEM], out_specs=[ANY] * 2,
-        scratch_shapes=[pltpu.SemaphoreType.DMA((4,))], compiler_params=small,
-    )(where, near(mine), near(got))
+        place_kernel, out_shape=outs, in_specs=[SMEM, VMEM, ANY, ANY], out_specs=[ANY] * 2,
+        input_output_aliases={2: 0, 3: 1}, scratch_shapes=[pltpu.SemaphoreType.DMA((2,))], compiler_params=small,
+    )(where, near(got), *halves_done)
     return middle[None], final[None]
 
 

time: 48.7 us -> 48.5 us (level)
  waiting for transfers between devices: 12.8 us -> 12 us
  Pallas kernels: 17.7 us -> 18.3 us
    ppermute x1, waiting for transfers between devices: 1.68 us -> 0.88 us  [pair_shards(): got = lax.ppermute(theirs, 'tm', swap)]
    pallas_call x1 -> x2, Pallas kernels: 0.99 us -> 1.61 us  [the longest x1 0.8 us: pair_shards(): pl.pallas_call(place_kernel, out_shape=outs, in_specs=[SMEM, VMEM, ANY, A...]
  transfers between devices with their start and end apart: 9 -> 9, of which waited for: 2 -> 2; matrix products, arithmetic and copies ran while one was open for 0% -> 0% of each run, Pallas kernels for 9% -> 11%
where the time goes in v7:
time: 48.5 us; the launch traced here: 48.3 us
  Pallas kernels  18.3 us (38%)
  starting transfers between devices  16.6 us (34%)
  waiting for transfers between devices  12 us (25%)
  between operations  1.4 us (3%)
    pallas_call x1, Pallas kernels, pair_shards(): pl.pallas_call(functools.partial(pair_kernel, halves), out_shape=[pltpu.V...  12 us
    ppermute x1, waiting for transfers between devices, pair_shards(): corner_1 = lax.ppermute(to_1, axes, partners(1, 1))  11.1 us
    ppermute x2, starting transfers between devices, pair_shards(): halo_y = [lax.ppermute(y, axes, partners(0, 1)) for y in to_y]  5.56 us
    ppermute x1, starting transfers between devices, pair_shards(): corner_1 = lax.ppermute(to_1, axes, partners(1, 1))  4.26 us
    ppermute x1, starting transfers between devices, pair_shards(): halo_x = lax.ppermute(to_x, axes, partners(1, 0))  3.22 us
    pallas_call x1, Pallas kernels, pair_shards(): pl.pallas_call(fill_kernel, out_shape=planes, in_specs=[SMEM, SMEM] + [VM...  3.15 us
    ppermute x1, starting transfers between devices, pair_shards(): corner_2 = lax.ppermute(to_2, axes, partners(1, -1))  1.97 us
    pallas_call x1, Pallas kernels, pair_shards(): pl.pallas_call(load_kernel, out_shape=[pltpu.VMEM(x.shape, jnp.float32) f...  1.23 us
  transfers between devices with their start and end apart: 9, of which 2 were waited for; matrix products, arithmetic and copies ran while one was open for 0% of the time, Pallas kernels for 11%

profile of v7, /device:TPU:19, one launch (start us, length us, event | category | flops | bytes accessed | tf_op | source)
XLA Modules:
  0.0 48.3 jit_solution(15241562986119262085)
XLA Ops:
  0.6 0.7 %collective-permute-start = (f32[32,16,256]{2,1,0:T(8,128)}, f32[32,16,256]{2,1,0:T(8,128)S(1)}, u32[]{:S(2)}, u32[]{:S(2)}) collective-permute-start(f32[32,16,256]{2,1,0:T(8,128)} %bitcast.4), channel_id=1, source_target_pairs={{0,16},{16,0},{1,17},{17,1},{2,18},{18,2},{3,19},{19,3},{4,20},{20... | collective-permute-start | bytes 1572872 | tf_op jit(solution)/shard_map/ppermute | solution.py:444
  2.0 1.2 %shard_map.59 = (f32[32,16,256]{2,1,0:T(8,128)S(1)}, f32[32,16,256]{2,1,0:T(8,128)S(1)}, f32[2,256]{1,0:T(2,128)S(1)}) custom-call(f32[32,16,256]{2,1,0:T(8,128)} %bitcast.5, f32[32,16,256]{2,1,0:T(8,128)} %refs_1_.1, f32[2,256]{1,0:T(2,128)} %refs_2_.1), custom_call_target="tpu_custom_call" | custom-call | bytes 2097152 | tf_op jit(solution)/shard_map/pallas_call | solution.py:446
  3.3 0.0 collective-permute-done.other
  3.3 0.3 shard_map.60
  3.6 3.2 %collective-permute-start.1 = (f32[2,552,128]{2,1,0:T(8,128)S(1)}, f32[2,552,128]{2,1,0:T(8,128)S(1)}, u32[]{:S(2)}, u32[]{:S(2)}) collective-permute-start(f32[2,552,128]{2,1,0:T(8,128)S(1)} %get-tuple-element.30), channel_id=1, source_target_pairs={{4,16},{16,4},{5,17},{17,5},{6,18},{18,6},{7,19},{19,7},{8,20},{20... | collective-permute-start | bytes 1695752 | tf_op jit(solution)/shard_map/ppermute | solution.py:459
  6.8 2.4 %collective-permute-start.2 = (f32[1,1096,128]{2,1,0:T(8,128)S(1)}, f32[1,1096,128]{2,1,0:T(8,128)S(1)}, u32[]{:S(2)}, u32[]{:S(2)}) collective-permute-start(f32[1,1096,128]{2,1,0:T(8,128)S(1)} %get-tuple-element.31), channel_id=1, source_target_pairs={{1,16},{16,1},{2,17},{17,2},{3,18},{18,3},{5,20},{20,5},{6,21},{21... | collective-permute-start | bytes 1683464 | tf_op jit(solution)/shard_map/ppermute | solution.py:460
  9.2 3.1 %collective-permute-start.3 = (f32[1,1096,128]{2,1,0:T(8,128)S(1)}, f32[1,1096,128]{2,1,0:T(8,128)S(1)}, u32[]{:S(2)}, u32[]{:S(2)}) collective-permute-start(f32[1,1096,128]{2,1,0:T(8,128)S(1)} %get-tuple-element.32), channel_id=1, source_target_pairs={{1,16},{16,1},{2,17},{17,2},{3,18},{18,3},{5,20},{20,5},{6,21},{21... | collective-permute-start | bytes 1683464 | tf_op jit(solution)/shard_map/ppermute | solution.py:460
  12.4 4.3 %collective-permute-start.4 = (f32[2,168,128]{2,1,0:T(8,128)S(1)}, f32[2,168,128]{2,1,0:T(8,128)S(1)}, u32[]{:S(2)}, u32[]{:S(2)}) collective-permute-start(f32[2,168,128]{2,1,0:T(8,128)S(1)} %get-tuple-element.33), channel_id=1, source_target_pairs={{5,16},{16,5},{6,17},{17,6},{7,18},{18,7},{9,20},{20,9},{10,21},{2... | collective-permute-start | bytes 516104 | tf_op jit(solution)/shard_map/ppermute | solution.py:461
  16.6 2.0 %collective-permute-start.5 = (f32[2,168,128]{2,1,0:T(8,128)S(1)}, f32[2,168,128]{2,1,0:T(8,128)S(1)}, u32[]{:S(2)}, u32[]{:S(2)}) collective-permute-start(f32[2,168,128]{2,1,0:T(8,128)S(1)} %get-tuple-element.34), channel_id=1, source_target_pairs={{4,17},{17,4},{5,18},{18,5},{6,19},{19,6},{8,21},{21,8},{9,22},{22... | collective-permute-start | bytes 516104 | tf_op jit(solution)/shard_map/ppermute | solution.py:462
  18.6 11.1 %collective-permute-done.4.corner_1 = f32[2,168,128]{2,1,0:T(8,128)S(1)} collective-permute-done((f32[2,168,128]{2,1,0:T(8,128)S(1)}, f32[2,168,128]{2,1,0:T(8,128)S(1)}, u32[]{:S(2)}, u32[]{:S(2)}) %collective-permute-start.4) | collective-permute-done | bytes 172064 | tf_op jit(solution)/shard_map/ppermute | solution.py:461
  29.7 0.0 collective-permute-done.5.corner_2
  29.7 0.0 collective-permute-done.2.rest_0_
  29.7 0.0 collective-permute-done.3.rest_1_
  29.7 0.0 collective-permute-done.1.halo_x
  29.7 0.1 collective-permute-start.6
  29.8 0.5 %collective-permute-start.7 = (f32[1,1096,128]{2,1,0:T(8,128)S(1)}, f32[1,1096,128]{2,1,0:T(8,128)S(1)}, u32[]{:S(2)}, u32[]{:S(2)}) collective-permute-start(f32[1,1096,128]{2,1,0:T(8,128)S(1)} %collective-permute-done.3.rest_1_), channel_id=1, source_target_pairs={{0,16},{16,0},{1,17},{17,1},{2,18},{18,2},{3,19},{19,3},{4,20},{20... | collective-permute-start | bytes 1683464 | tf_op jit(solution)/shard_map/ppermute | solution.py:464
  30.3 3.1 %shard_map.61 = (f32[2,2,40,48,128]{4,3,2,1,0:T(8,128)S(1)}, f32[2,2,40,48,128]{4,3,2,1,0:T(8,128)S(1)}, f32[2,40,48,128]{3,2,1,0:T(8,128)S(1)}, f32[2,2,40,48,1...) custom-call(s32[1]{0:T(128)} %bitcast.where_ref, ...), custom_call_target="tpu_custom_call" | custom-call | bytes 8388608 | tf_op jit(solution)/shard_map/pallas_call | solution.py:470
  33.5 0.0 collective-permute-done.6.rest_2_
  33.5 0.0 collective-permute-done.7.rest_3_
  33.5 12.0 %shard_map.62 = (f32[2,16,16,256]{3,2,1,0:T(8,128)S(1)}, f32[2,16,16,256]{3,2,1,0:T(8,128)S(1)}, f32[2,2,40,48,128]{4,3,2,1,0:T(8,128)S(1)}, f32[2,2,40,48,128]{...) custom-call(s32[1]{0:T(128)} %bitcast.where_ref, ...), custom_call_target="tpu_custom_call", output_to_operand_aliasing={{2}: (10, {}), {3}: (11, {}), {4}: (12, {}), {5}: (13, {}),... | custom-call | tf_op jit(solution)/shard_map/pallas_call | solution.py:475
  45.5 0.3 collective-permute-start.8
  45.8 0.8 %shard_map.63 = (f32[32,16,256]{2,1,0:T(8,128)}, f32[32,16,256]{2,1,0:T(8,128)}) custom-call(s32[1]{0:T(128)} %bitcast.where_ref, f32[2,16,16,256]{3,2,1,0:T(8,128)S(1)} %get-tuple-element.47.part), custom_call_target="tpu_custom_call" | custom-call | bytes 4194304 | tf_op jit(solution)/shard_map/pallas_call | solution.py:485
  46.6 0.9 %collective-permute-done.8.part = f32[2,16,16,256]{3,2,1,0:T(8,128)S(1)} collective-permute-done((f32[2,16,16,256]{3,2,1,0:T(8,128)S(1)}, f32[2,16,16,256]{3,2,1,0:T(8,128)S(1)}, u32[]{:S(2)}, u32[]{:S(2)}) %collective-permute-start.8) | collective-permute-done | bytes 524320 | tf_op jit(solution)/shard_map/ppermute | solution.py:483
  47.5 0.8 %shard_map.64 = (f32[32,16,256]{2,1,0:T(8,128)}, f32[32,16,256]{2,1,0:T(8,128)}) custom-call(s32[1]{0:T(128)} %bitcast.where_ref, f32[2,16,16,256]{3,2,1,0:T(8,128)S(1)} %collective-permute-done.8.part, f32[32,16,256]{2,1,0:T(8,128)} %get-tuple-element.48.rest_0_, f32[32,16,256]{2,1,0:T(8,128)} %get-tuple-element.49.rest_1_), custom_call_target="tpu_custom_call", output_to_operand_aliasing={{0}: (2, {}), {1}: (3, {})} | custom-call | tf_op jit(solution)/shard_map/pallas_call | solution.py:490
Async XLA Ops:
  0.6 2.6 %collective-permute-start = (f32[32,16,256]{2,1,0:T(8,128)}, f32[32,16,256]{2,1,0:T(8,128)S(1)}, u32[]{:S(2)}, u32[]{:S(2)}) collective-permute-start(f32[32,16,256]{2,1,0:T(8,128)} %bitcast.4), channel_id=1, source_target_pairs={{0,16},{16,0},{1,17},{17,1},{2,18},{18,2},{3,19},{19,3},{4,20},{20... | collective-permute-start | bytes 1572872 | tf_op jit(solution)/shard_map/ppermute | solution.py:444
  3.6 26.2 %collective-permute-start.1 = (f32[2,552,128]{2,1,0:T(8,128)S(1)}, f32[2,552,128]{2,1,0:T(8,128)S(1)}, u32[]{:S(2)}, u32[]{:S(2)}) collective-permute-start(f32[2,552,128]{2,1,0:T(8,128)S(1)} %get-tuple-element.30), channel_id=1, source_target_pairs={{4,16},{16,4},{5,17},{17,5},{6,18},{18,6},{7,19},{19,7},{8,20},{20... | collective-permute-start | bytes 1695752 | tf_op jit(solution)/shard_map/ppermute | solution.py:459
  6.8 22.9 %collective-permute-start.2 = (f32[1,1096,128]{2,1,0:T(8,128)S(1)}, f32[1,1096,128]{2,1,0:T(8,128)S(1)}, u32[]{:S(2)}, u32[]{:S(2)}) collective-permute-start(f32[1,1096,128]{2,1,0:T(8,128)S(1)} %get-tuple-element.31), channel_id=1, source_target_pairs={{1,16},{16,1},{2,17},{17,2},{3,18},{18,3},{5,20},{20,5},{6,21},{21... | collective-permute-start | bytes 1683464 | tf_op jit(solution)/shard_map/ppermute | solution.py:460
  9.2 20.5 %collective-permute-start.3 = (f32[1,1096,128]{2,1,0:T(8,128)S(1)}, f32[1,1096,128]{2,1,0:T(8,128)S(1)}, u32[]{:S(2)}, u32[]{:S(2)}) collective-permute-start(f32[1,1096,128]{2,1,0:T(8,128)S(1)} %get-tuple-element.32), channel_id=1, source_target_pairs={{1,16},{16,1},{2,17},{17,2},{3,18},{18,3},{5,20},{20,5},{6,21},{21... | collective-permute-start | bytes 1683464 | tf_op jit(solution)/shard_map/ppermute | solution.py:460
  12.4 17.3 %collective-permute-start.4 = (f32[2,168,128]{2,1,0:T(8,128)S(1)}, f32[2,168,128]{2,1,0:T(8,128)S(1)}, u32[]{:S(2)}, u32[]{:S(2)}) collective-permute-start(f32[2,168,128]{2,1,0:T(8,128)S(1)} %get-tuple-element.33), channel_id=1, source_target_pairs={{5,16},{16,5},{6,17},{17,6},{7,18},{18,7},{9,20},{20,9},{10,21},{2... | collective-permute-start | bytes 516104 | tf_op jit(solution)/shard_map/ppermute | solution.py:461
  16.6 13.1 %collective-permute-start.5 = (f32[2,168,128]{2,1,0:T(8,128)S(1)}, f32[2,168,128]{2,1,0:T(8,128)S(1)}, u32[]{:S(2)}, u32[]{:S(2)}) collective-permute-start(f32[2,168,128]{2,1,0:T(8,128)S(1)} %get-tuple-element.34), channel_id=1, source_target_pairs={{4,17},{17,4},{5,18},{18,5},{6,19},{19,6},{8,21},{21,8},{9,22},{22... | collective-permute-start | bytes 516104 | tf_op jit(solution)/shard_map/ppermute | solution.py:462
  29.7 3.7 %collective-permute-start.6 = (f32[1,1096,128]{2,1,0:T(8,128)S(1)}, f32[1,1096,128]{2,1,0:T(8,128)S(1)}, u32[]{:S(2)}, u32[]{:S(2)}) collective-permute-start(f32[1,1096,128]{2,1,0:T(8,128)S(1)} %collective-permute-done.2.rest_0_), channel_id=1, source_target_pairs={{0,16},{16,0},{1,17},{17,1},{2,18},{18,2},{3,19},{19,3},{4,20},{20... | collective-permute-start | bytes 1683464 | tf_op jit(solution)/shard_map/ppermute | solution.py:464
  29.8 3.7 %collective-permute-start.7 = (f32[1,1096,128]{2,1,0:T(8,128)S(1)}, f32[1,1096,128]{2,1,0:T(8,128)S(1)}, u32[]{:S(2)}, u32[]{:S(2)}) collective-permute-start(f32[1,1096,128]{2,1,0:T(8,128)S(1)} %collective-permute-done.3.rest_1_), channel_id=1, source_target_pairs={{0,16},{16,0},{1,17},{17,1},{2,18},{18,2},{3,19},{19,3},{4,20},{20... | collective-permute-start | bytes 1683464 | tf_op jit(solution)/shard_map/ppermute | solution.py:464
  45.5 2.0 %collective-permute-start.8 = (f32[2,16,16,256]{3,2,1,0:T(8,128)S(1)}, f32[2,16,16,256]{3,2,1,0:T(8,128)S(1)}, u32[]{:S(2)}, u32[]{:S(2)}) collective-permute-start(f32[2,16,16,256]{3,2,1,0:T(8,128)S(1)} %get-tuple-element.46), channel_id=1, source_target_pairs={{0,16},{16,0},{1,17},{17,1},{2,18},{18,2},{3,19},{19,3},{4,20},{20... | collective-permute-start | bytes 1572872 | tf_op jit(solution)/shard_map/ppermute | solution.py:483
